TPU v7x, 32 devices: a whole 2x2x4 slice. The times are simulated.
32 devices in a mesh: groups: 2 (over x), tp: 4 (over y, core), seq: 4 (over z).
Axes of the slice: x: 2, y: 2, z: 4, core: 2. Of those that a mesh axis runs over, the one named last changes fastest.
Arguments:
- hidden_in: bfloat16 [6144, 4608], P(('groups', 'seq', 'tp')), parts along dimension 0, may hold values from -6 to 6
- pre_gain: float32 [4608], replicated, may hold values from 0.1 to 1.9
- post_gain: float32 [4608], replicated, may hold values from 0.1 to 1.9
- w_query: bfloat16 [4608, 1024], P(None, 'tp')
- w_key: bfloat16 [4608, 512], P(None, 'tp')
- w_value: bfloat16 [4608, 512], P(None, 'tp'), may hold values from -0.09375 to 0.09375
- w_out: bfloat16 [1024, 4608], P('tp'), may hold values from -0.1875 to 0.1875
- block_of: int32 [8], replicated, may hold values from 0 to 7, each once
Outputs:
- hidden_out: bfloat16 [6144, 4608], P(('groups', 'seq', 'tp')), parts along dimension 0
There are 2 independent parts, one for each index of `groups`. A program takes and returns all parts, laid end to end along the dimension named above; an argument that names none is the same for every part. Nothing has to cross between parts.
Inputs may be any that keep to these rules, and one draw needn't show every extreme that they name: block_of is a permutation: storage block b (rows b * 384 onward) holds the prompt's positions from block_of[b] * 384 onward.
All inputs are finite; a program needn't handle non-finite values.
Results may differ from a plain program's by a relative error of at most 0.012.
Values may be sent and summed in bfloat16 or wider, within the bound.
No kernel may reach another device: no remote copies, remote signals or barrier semaphores. Data moves between devices by JAX's collectives and lax.ppermute only.
A program may use at most 64 MiB of HBM per device.

v0:
```python
import jax
import jax.numpy as jnp
from jax import lax
from jax.sharding import PartitionSpec as P

HD = 128
ATT_SCALAR = 144


def normalize(row_values, gain_vector):
    features = row_values.astype(jnp.float32)
    return (
        features
        * lax.rsqrt(jnp.mean(features * features, axis=-1, keepdims=True) + 1e-06)
        * gain_vector
    )


def rotate_pairs(features, positions):
    half_dim = HD // 2
    frequency = jnp.power(
        jnp.float32(10000.0), -jnp.arange(half_dim, dtype=jnp.float32) * (2.0 / HD)
    )
    angles = positions.astype(jnp.float32)[:, None] * frequency[None, :]
    cosine = jnp.cos(angles)[:, None, :]
    sine_part = jnp.sin(angles)[:, None, :]
    first_half = features[..., :half_dim]
    second_half = features[..., half_dim:]
    return jnp.concatenate(
        [
            first_half * cosine - second_half * sine_part,
            second_half * cosine + first_half * sine_part,
        ],
        axis=-1,
    )


def table_positions(block_of, row_index, block_rows):
    block_ids = jnp.arange(block_of.shape[0], dtype=jnp.int32)
    picked = jnp.sum(
        jnp.where((row_index // block_rows)[:, None] == block_ids[None, :], block_of[None, :], 0),
        axis=1,
    )
    return picked * block_rows + row_index % block_rows


def body(hidden_in, pre_gain, post_gain, w_query, w_key, w_value, w_out, block_of):
    tp_count = lax.axis_size("tp")
    local_rows = hidden_in.shape[0]
    seq_rows = local_rows * tp_count
    block_rows = seq_rows // 2
    row_offset = lax.axis_index("seq") * seq_rows
    query_heads = w_query.shape[1] // HD
    normed_local = normalize(hidden_in, pre_gain).astype(jnp.bfloat16)
    normed = lax.all_gather(normed_local, "tp", axis=0, tiled=True)
    row_index = row_offset + jnp.arange(normed.shape[0], dtype=jnp.int32)
    positions = table_positions(block_of, row_index, block_rows)
    project_queries = jnp.dot(normed, w_query, preferred_element_type=jnp.float32).reshape(
        -1, query_heads, HD
    )
    project_queries = (
        (rotate_pairs(project_queries, positions) * ATT_SCALAR ** (-0.5))
        .astype(jnp.bfloat16)
        .reshape(-1, query_heads * HD)
    )
    keys_local = jnp.dot(normed, w_key, preferred_element_type=jnp.float32).reshape(-1, 1, HD)
    keys_local = rotate_pairs(keys_local, positions).astype(jnp.bfloat16).reshape(-1, HD)
    values_local = jnp.dot(normed, w_value, preferred_element_type=jnp.float32).astype(jnp.bfloat16)
    projected = jnp.concatenate([project_queries, keys_local, values_local], axis=1)
    queries = projected[:, : query_heads * HD].reshape(seq_rows, query_heads, HD)
    keys_local = projected[:, query_heads * HD : (query_heads + 1) * HD]
    values_local = projected[:, (query_heads + 1) * HD :]
    query_positions = table_positions(
        block_of, row_offset + jnp.arange(seq_rows, dtype=jnp.int32), block_rows
    )

    def update(softmax_state, keys_block, values_block, key_positions):
        running_max, denominator, accumulated = softmax_state
        scores = jnp.einsum("qhd,kd->hqk", queries, keys_block, preferred_element_type=jnp.float32)
        visible = (key_positions[None, :] <= query_positions[:, None])[None, :, :]
        new_max = jnp.maximum(running_max, jnp.max(jnp.where(visible, scores, -1e30), axis=2))
        exponent = jnp.where(visible, jnp.exp(scores - new_max[:, :, None]), 0.0)
        rescale = jnp.exp(running_max - new_max)
        denominator = denominator * rescale + jnp.sum(exponent, axis=2)
        weighted = jnp.einsum(
            "hqk,kd->qhd",
            exponent.astype(jnp.bfloat16),
            values_block,
            preferred_element_type=jnp.float32,
        )
        accumulated = accumulated * jnp.transpose(rescale)[:, :, None] + weighted
        return (new_max, denominator, accumulated)

    initial = (
        jnp.full((query_heads, seq_rows), -1e30, jnp.float32),
        jnp.zeros((query_heads, seq_rows), jnp.float32),
        jnp.zeros((seq_rows, query_heads, HD), jnp.float32),
    )
    keys_all, values_all = (
        lax.all_gather(keys_local, "seq", axis=0, tiled=True),
        lax.all_gather(values_local, "seq", axis=0, tiled=True),
    )
    softmax_state = initial
    keys_piece = keys_all
    values_piece = values_all
    block_count = keys_piece.shape[0] // block_rows
    keys_piece = keys_piece.reshape(block_count, block_rows, HD)
    values_piece = values_piece.reshape(block_count, block_rows, HD)

    def one_block(carried, operands):
        keys_block, values_block, block_index = operands
        key_positions = table_positions(
            block_of,
            0 + block_index * block_rows + jnp.arange(block_rows, dtype=jnp.int32),
            block_rows,
        )
        carried = update(carried, keys_block, values_block, key_positions)
        return (carried, None)

    softmax_state, unused = lax.scan(
        one_block,
        softmax_state,
        (keys_piece, values_piece, jnp.arange(block_count, dtype=jnp.int32)),
    )
    running_max, denominator, accumulated = softmax_state
    attended = (
        (accumulated / jnp.transpose(denominator)[:, :, None])
        .astype(jnp.bfloat16)
        .reshape(seq_rows, query_heads * HD)
    )
    summed = lax.psum_scatter(
        jnp.dot(attended, w_out, preferred_element_type=jnp.float32).astype(jnp.bfloat16),
        "tp",
        scatter_dimension=0,
        tiled=True,
    ).astype(jnp.float32)
    post_normed = normalize(summed, post_gain)
    return (hidden_in.astype(jnp.float32) + post_normed).astype(jnp.bfloat16)


def solution(mesh):
    return jax.shard_map(
        body,
        mesh=mesh,
        in_specs=(
            P(("groups", "seq", "tp"), None),
            P(),
            P(),
            P(None, "tp"),
            P(None, "tp"),
            P(None, "tp"),
            P("tp", None),
            P(),
        ),
        out_specs=P(("groups", "seq", "tp"), None),
        check_vma=False,
    )
```

profile of v0, /device:TPU:0, one launch (start us, length us, event | category | flops | bytes accessed | tf_op | source)
XLA Modules:
  0.0 272.3 jit_solution(5571795569796005449)
XLA Ops:
  6.5 2.1 fusion.29
  8.7 2.4 fusion.31
  12.0 2.5 multiply_cosine_fusion
  14.5 50.4 %all-gather.2.cloned.1.call-done = bf16[768,4608]{1,0:T(8,128)(2,1)} async-done(((bf16[192,4608]{1,0:T(8,128)(2,1)}), bf16[768,4608]{1,0:T(8,128)(2,1)}) %all-gather.2.cloned.1.call-update) | async-done | bytes 7077904 | tf_op jit(solution)/shard_map/all_gather | solution.py:55
  64.9 5.7 %fusion.54 = f32[768,256]{0,1:T(8,128)S(1)} fusion(bf16[768,4608]{1,0:T(8,128)(2,1)} %all-gather.2.cloned.1.call-done, bf16[4608,256]{1,0:T(8,128)(2,1)} %param.13), kind=kOutput, calls=%fused_computation.91 | convolution fusion | flops 1811939328 | bytes 10223616 | tf_op jit(solution)/shard_map/dot_general | solution.py:58
  71.4 2.2 copy.22
  74.8 5.7 %convolution_bitcast_fusion.1 = f32[768,1,128]{0,2,1:T(8,128)S(1)} fusion(bf16[768,4608]{1,0:T(8,128)(2,1)} %all-gather.2.cloned.1.call-done, bf16[4608,128]{1,0:T(8,128)(2,1)} %param.14), kind=kOutput, calls=%fused_computation.52 | convolution fusion | flops 905969664 | bytes 8650752 | tf_op jit(solution)/shard_map/dot_general | solution.py:66
  81.4 19.9 %all_gather.10 = bf16[3072,128]{0,1:T(8,128)(2,1)} all-gather(bf16[768,128]{0,1:T(8,128)(2,1)S(1)} %pad_maximum_fusion), channel_id=1, replica_groups=mesh['groups'=2,'tp'=4,'seq'=4] {'seq'}, dimensions={0}, use_global_device_ids=true | all-gather | bytes 983040 | tf_op jit(solution)/shard_map/all_gather | solution.py:100
  101.3 2.3 copy.20
  103.6 5.4 %convolution_convert_fusion.1 = bf16[768,128]{1,0:T(8,128)(2,1)S(1)} fusion(bf16[768,4608]{1,0:T(8,128)(2,1)} %all-gather.2.cloned.1.call-done, bf16[4608,128]{1,0:T(8,128)(2,1)} %param.15), kind=kOutput, calls=%fused_computation.53 | convolution fusion | flops 906067968 | bytes 8454144 | tf_op jit(solution)/shard_map/dot_general | solution.py:68
  109.0 18.8 %all_gather.11 = bf16[3072,128]{1,0:T(8,128)(2,1)} all-gather(bf16[768,128]{1,0:T(8,128)(2,1)S(1)} %convolution_convert_fusion.1), channel_id=1, replica_groups=mesh['groups'=2,'tp'=4,'seq'=4] {'seq'}, dimensions={0}, use_global_device_ids=true | all-gather | bytes 983040 | tf_op jit(solution)/shard_map/all_gather | solution.py:101
  129.1 63.2 %while.17 = (s32[]{:T(128)}, f32[2,768]{1,0:T(2,128)S(1)}, f32[2,768]{1,0:T(2,128)S(1)}, f32[768,2,128]{0,2,1:T(8,128)S(1)}, s32[8]{0:T(128)S(1)}, /*index=5*/s3...) while((s32[]{:T(128)}, f32[2,768]{1,0:T(2,128)S(1)}, ...), condition=%wide.region_6.7_spmd.clone, body=%wide.region_2.6_spmd.clone.sunk | while | flops 307618176 | bytes 19969252 | solution.py:120
  130.7 3.0 %fusion.77 = (f32[2,768]{1,0:T(2,128)S(1)}, f32[384,768,2]{1,0,2:T(8,128)}) fusion(pred[768,384]{0,1:T(8,128)(4,1)S(1)} %broadcast_compare_fusion.2, bf16[768,2,128]{2,0,1:T(8,128)(2,1)} %get-tuple-element.326, bf16[8,384,128]{2,1,0:T(8,128)(2,1)} %get-tuple-element.325, s32[]{:T(128)} %get-tuple-element.305), kind=kOutput, calls=%fused_computation.2.clone.1 | convolution fusion | flops 152173056 | bytes 3152384 | tf_op jit(solution)/shard_map/while/body/eval_jaxpr/qhd,kd->hqk/dot_general | solution.py:79
  133.7 2.7 fusion.81
  138.6 3.0 %fusion.77 = (f32[2,768]{1,0:T(2,128)S(1)}, f32[384,768,2]{1,0,2:T(8,128)}) fusion(pred[768,384]{0,1:T(8,128)(4,1)S(1)} %broadcast_compare_fusion.2, bf16[768,2,128]{2,0,1:T(8,128)(2,1)} %get-tuple-element.326, bf16[8,384,128]{2,1,0:T(8,128)(2,1)} %get-tuple-element.325, s32[]{:T(128)} %get-tuple-element.305), kind=kOutput, calls=%fused_computation.2.clone.1 | convolution fusion | flops 152173056 | bytes 3152384 | tf_op jit(solution)/shard_map/while/body/eval_jaxpr/qhd,kd->hqk/dot_general | solution.py:79
  141.6 2.7 fusion.81
  146.5 3.0 %fusion.77 = (f32[2,768]{1,0:T(2,128)S(1)}, f32[384,768,2]{1,0,2:T(8,128)}) fusion(pred[768,384]{0,1:T(8,128)(4,1)S(1)} %broadcast_compare_fusion.2, bf16[768,2,128]{2,0,1:T(8,128)(2,1)} %get-tuple-element.326, bf16[8,384,128]{2,1,0:T(8,128)(2,1)} %get-tuple-element.325, s32[]{:T(128)} %get-tuple-element.305), kind=kOutput, calls=%fused_computation.2.clone.1 | convolution fusion | flops 152173056 | bytes 3152384 | tf_op jit(solution)/shard_map/while/body/eval_jaxpr/qhd,kd->hqk/dot_general | solution.py:79
  149.5 2.7 fusion.81
  154.4 3.0 %fusion.77 = (f32[2,768]{1,0:T(2,128)S(1)}, f32[384,768,2]{1,0,2:T(8,128)}) fusion(pred[768,384]{0,1:T(8,128)(4,1)S(1)} %broadcast_compare_fusion.2, bf16[768,2,128]{2,0,1:T(8,128)(2,1)} %get-tuple-element.326, bf16[8,384,128]{2,1,0:T(8,128)(2,1)} %get-tuple-element.325, s32[]{:T(128)} %get-tuple-element.305), kind=kOutput, calls=%fused_computation.2.clone.1 | convolution fusion | flops 152173056 | bytes 3152384 | tf_op jit(solution)/shard_map/while/body/eval_jaxpr/qhd,kd->hqk/dot_general | solution.py:79
  157.4 2.7 fusion.81
  162.3 3.0 %fusion.77 = (f32[2,768]{1,0:T(2,128)S(1)}, f32[384,768,2]{1,0,2:T(8,128)}) fusion(pred[768,384]{0,1:T(8,128)(4,1)S(1)} %broadcast_compare_fusion.2, bf16[768,2,128]{2,0,1:T(8,128)(2,1)} %get-tuple-element.326, bf16[8,384,128]{2,1,0:T(8,128)(2,1)} %get-tuple-element.325, s32[]{:T(128)} %get-tuple-element.305), kind=kOutput, calls=%fused_computation.2.clone.1 | convolution fusion | flops 152173056 | bytes 3152384 | tf_op jit(solution)/shard_map/while/body/eval_jaxpr/qhd,kd->hqk/dot_general | solution.py:79
  165.3 2.7 fusion.81
  170.2 3.0 %fusion.77 = (f32[2,768]{1,0:T(2,128)S(1)}, f32[384,768,2]{1,0,2:T(8,128)}) fusion(pred[768,384]{0,1:T(8,128)(4,1)S(1)} %broadcast_compare_fusion.2, bf16[768,2,128]{2,0,1:T(8,128)(2,1)} %get-tuple-element.326, bf16[8,384,128]{2,1,0:T(8,128)(2,1)} %get-tuple-element.325, s32[]{:T(128)} %get-tuple-element.305), kind=kOutput, calls=%fused_computation.2.clone.1 | convolution fusion | flops 152173056 | bytes 3152384 | tf_op jit(solution)/shard_map/while/body/eval_jaxpr/qhd,kd->hqk/dot_general | solution.py:79
  173.2 2.7 fusion.81
  178.1 3.0 %fusion.77 = (f32[2,768]{1,0:T(2,128)S(1)}, f32[384,768,2]{1,0,2:T(8,128)}) fusion(pred[768,384]{0,1:T(8,128)(4,1)S(1)} %broadcast_compare_fusion.2, bf16[768,2,128]{2,0,1:T(8,128)(2,1)} %get-tuple-element.326, bf16[8,384,128]{2,1,0:T(8,128)(2,1)} %get-tuple-element.325, s32[]{:T(128)} %get-tuple-element.305), kind=kOutput, calls=%fused_computation.2.clone.1 | convolution fusion | flops 152173056 | bytes 3152384 | tf_op jit(solution)/shard_map/while/body/eval_jaxpr/qhd,kd->hqk/dot_general | solution.py:79
  181.1 2.7 fusion.81
  186.0 3.0 %fusion.77 = (f32[2,768]{1,0:T(2,128)S(1)}, f32[384,768,2]{1,0,2:T(8,128)}) fusion(pred[768,384]{0,1:T(8,128)(4,1)S(1)} %broadcast_compare_fusion.2, bf16[768,2,128]{2,0,1:T(8,128)(2,1)} %get-tuple-element.326, bf16[8,384,128]{2,1,0:T(8,128)(2,1)} %get-tuple-element.325, s32[]{:T(128)} %get-tuple-element.305), kind=kOutput, calls=%fused_computation.2.clone.1 | convolution fusion | flops 152173056 | bytes 3152384 | tf_op jit(solution)/shard_map/while/body/eval_jaxpr/qhd,kd->hqk/dot_general | solution.py:79
  189.0 2.7 fusion.81
  192.3 5.0 %convolution_convert_fusion = bf16[768,4608]{1,0:T(8,128)(2,1)} fusion(bf16[768,256]{0,1:T(8,128)(2,1)S(1)} %bitcast.72, bf16[256,4608]{1,0:T(8,128)(2,1)S(1)} %copy-done), kind=kOutput, calls=%fused_computation.40 | convolution fusion | flops 1815478272 | bytes 9830400 | tf_op jit(solution)/shard_map/dot_general | solution.py:132
  197.3 62.6 %reduce-scatter.2.cloned.1.call-done = bf16[192,4608]{1,0:T(8,128)(2,1)} async-done(((bf16[768,4608]{1,0:T(8,128)(2,1)}), bf16[192,4608]{1,0:T(8,128)(2,1)}) %reduce-scatter.2.cloned.1.call-update) | async-done | bytes 1769488 | tf_op jit(solution)/shard_map/reduce_scatter | solution.py:131
  259.9 2.0 fusion.27
  262.0 3.4 %fusion.32 = bf16[192,4608]{1,0:T(8,128)(2,1)} fusion(bf16[192,4608]{1,0:T(8,128)(2,1)} %reduce-scatter.2.cloned.1.call-done, bf16[192,4608]{1,0:T(8,128)(2,1)S(1)} %copy-done.3, f32[4608]{0:T(1024)S(1)} %copy-done.11, f32[192]{0:T(256)S(1)} %add_rsqrt_fusion), kind=kLoop, calls=%fused_computation.51 | loop fusion | flops 5308416 | bytes 5327616 | tf_op jit(solution)/shard_map/convert_element_type | solution.py:138
  (139 shorter events, 17.1 us)
Async XLA Ops:
  6.5 185.8 %copy-start = (bf16[256,4608]{1,0:T(8,128)(2,1)S(1)}, bf16[256,4608]{1,0:T(8,128)(2,1)}, u32[]{:S(2)}) copy-start(bf16[256,4608]{1,0:T(8,128)(2,1)} %param.16) | copy-start | bytes 7077892
  6.5 58.3 %all-gather.2.cloned.1.call-start = ((), (), s32[]{:S(2)}) async-start(), calls=%async_computation.1 | async-start | bytes 8847360 | tf_op jit(solution)/shard_map/all_gather | solution.py:55
  6.5 2.2 copy-start.2
  8.7 2.6 copy-start.12
  11.2 248.8 %reduce-scatter.2.cloned.1.call-start = ((), (), s32[]{:S(2)}) async-start(), calls=%async_computation.2 | async-start | bytes 8847360 | tf_op jit(solution)/shard_map/reduce_scatter | solution.py:131
  11.3 59.3 %copy-start.14 = (f32[64]{0:T(128)}, f32[64]{0:T(128)S(1)}, u32[]{:S(2)}) copy-start(f32[64]{0:T(128)S(1)} %multiply_power_fusion) | copy-start | bytes 772
  12.0 58.6 %copy-start.9 = (f32[768]{0:T(1024)}, f32[768]{0:T(1024)S(1)}, u32[]{:S(2)}) copy-start(f32[768]{0:T(1024)S(1)} %get-tuple-element.211) | copy-start | bytes 9220
  74.8 5.7 %copy-start.10 = (f32[768]{0:T(1024)S(1)}, f32[768]{0:T(1024)}, u32[]{:S(2)}) copy-start(f32[768]{0:T(1024)} %copy-done.9) | copy-start | bytes 9220
  74.8 5.7 %copy-start.15 = (f32[64]{0:T(128)S(1)}, f32[64]{0:T(128)}, u32[]{:S(2)}) copy-start(f32[64]{0:T(128)} %copy-done.14) | copy-start | bytes 772
  103.6 24.2 %copy-start.4 = (f32[768,2,64]{2,0,1:T(8,128)S(1)}, f32[768,2,64]{2,0,1:T(8,128)}, u32[]{:S(2)}) copy-start(f32[768,2,64]{2,0,1:T(8,128)} %copy.22) | copy-start | bytes 1179652
  103.6 24.2 %copy-start.5 = (f32[768,2,64]{2,0,1:T(8,128)S(1)}, f32[768,2,64]{2,0,1:T(8,128)}, u32[]{:S(2)}) copy-start(f32[768,2,64]{2,0,1:T(8,128)} %copy.23) | copy-start | bytes 1179652
  103.6 24.2 %copy-start.6 = (f32[768,64]{1,0:T(8,128)S(1)}, f32[768,64]{1,0:T(8,128)}, u32[]{:S(2)}) copy-start(f32[768,64]{1,0:T(8,128)} %get-tuple-element.221) | copy-start | bytes 589828
  103.6 24.2 %copy-start.7 = (f32[768,64]{1,0:T(8,128)S(1)}, f32[768,64]{1,0:T(8,128)}, u32[]{:S(2)}) copy-start(f32[768,64]{1,0:T(8,128)} %get-tuple-element.222) | copy-start | bytes 589828
  127.8 1.2 copy-start.8
  127.8 1.2 copy-start.13
  133.7 2.7 %copy-start.1 = (f32[384,768,2]{1,0,2:T(8,128)S(1)}, f32[384,768,2]{1,0,2:T(8,128)}, u32[]{:S(2)}) copy-start(f32[384,768,2]{1,0,2:T(8,128)} %get-tuple-element.290) | copy-start | bytes 7077892 | tf_op jit(solution)/shard_map/while
  141.6 2.7 %copy-start.1 = (f32[384,768,2]{1,0,2:T(8,128)S(1)}, f32[384,768,2]{1,0,2:T(8,128)}, u32[]{:S(2)}) copy-start(f32[384,768,2]{1,0,2:T(8,128)} %get-tuple-element.290) | copy-start | bytes 7077892 | tf_op jit(solution)/shard_map/while
  149.5 2.7 %copy-start.1 = (f32[384,768,2]{1,0,2:T(8,128)S(1)}, f32[384,768,2]{1,0,2:T(8,128)}, u32[]{:S(2)}) copy-start(f32[384,768,2]{1,0,2:T(8,128)} %get-tuple-element.290) | copy-start | bytes 7077892 | tf_op jit(solution)/shard_map/while
  157.4 2.7 %copy-start.1 = (f32[384,768,2]{1,0,2:T(8,128)S(1)}, f32[384,768,2]{1,0,2:T(8,128)}, u32[]{:S(2)}) copy-start(f32[384,768,2]{1,0,2:T(8,128)} %get-tuple-element.290) | copy-start | bytes 7077892 | tf_op jit(solution)/shard_map/while
  165.3 2.7 %copy-start.1 = (f32[384,768,2]{1,0,2:T(8,128)S(1)}, f32[384,768,2]{1,0,2:T(8,128)}, u32[]{:S(2)}) copy-start(f32[384,768,2]{1,0,2:T(8,128)} %get-tuple-element.290) | copy-start | bytes 7077892 | tf_op jit(solution)/shard_map/while
  173.2 2.7 %copy-start.1 = (f32[384,768,2]{1,0,2:T(8,128)S(1)}, f32[384,768,2]{1,0,2:T(8,128)}, u32[]{:S(2)}) copy-start(f32[384,768,2]{1,0,2:T(8,128)} %get-tuple-element.290) | copy-start | bytes 7077892 | tf_op jit(solution)/shard_map/while
  181.1 2.7 %copy-start.1 = (f32[384,768,2]{1,0,2:T(8,128)S(1)}, f32[384,768,2]{1,0,2:T(8,128)}, u32[]{:S(2)}) copy-start(f32[384,768,2]{1,0,2:T(8,128)} %get-tuple-element.290) | copy-start | bytes 7077892 | tf_op jit(solution)/shard_map/while
  189.0 2.7 %copy-start.1 = (f32[384,768,2]{1,0,2:T(8,128)S(1)}, f32[384,768,2]{1,0,2:T(8,128)}, u32[]{:S(2)}) copy-start(f32[384,768,2]{1,0,2:T(8,128)} %get-tuple-element.290) | copy-start | bytes 7077892 | tf_op jit(solution)/shard_map/while
  197.3 64.7 %copy-start.11 = (f32[4608]{0:T(1024)S(1)}, f32[4608]{0:T(1024)}, u32[]{:S(2)}) copy-start(f32[4608]{0:T(1024)} %param.12) | copy-start | bytes 55300
  259.9 2.1 copy-start.3
Sparse Core Ops, SparseCore 0:
  11.3 53.5 all-gather.1
  197.4 62.4 reduce-scatter.1
where the time goes:
time: 273 us; the launch traced here: 272 us
  waiting for transfers between devices  113 us (41%)
  matrix products  67.3 us (25%)
  blocking collectives  38.7 us (14%)
  other arithmetic  22.2 us (8%)
  between operations  13.6 us (5%)
  local copies, waits for them, and re-layouts  11.8 us (4%)
  loops' own time  5.53 us (2%)
    reduce_scatter x1, waiting for transfers between devices, body(): lax.psum_scatter(jnp.dot(attended, w_out, preferred_element_type=jnp.floa...  62.6 us
    all_gather x1, waiting for transfers between devices, body(): normed = lax.all_gather(normed_local, 'tp', axis=0, tiled=True)  50.4 us
    dot_general x8, matrix products, update(): jnp.einsum('qhd,kd->hqk', queries, keys_block, preferred_element_type=jnp...  24 us
    dot_general x8, matrix products, update(): jnp.einsum('hqk,kd->qhd', exponent.astype(jnp.bfloat16), values_block, pr...  21.6 us
    all_gather x1, blocking collectives, body(): lax.all_gather(keys_local, 'seq', axis=0, tiled=True)  19.9 us
    all_gather x1, blocking collectives, body(): lax.all_gather(values_local, 'seq', axis=0, tiled=True)  18.8 us
    unnamed x33, local copies, waits for them, and re-layouts  5.83 us
    dot_general x1, matrix products, body(): jnp.dot(normed, w_key, preferred_element_type=jnp.float32)  5.71 us
  transfers between devices with their start and end apart: 2, of which 2 were waited for; matrix products, arithmetic and copies ran while one was open for 1% of the time, Pallas kernels for 0%

commit v1 on v0

v1 whole, which is shorter than its diff:
```python
import functools
import math

import jax
import jax.numpy as jnp
from jax import lax
from jax.experimental import pallas as pl
from jax.experimental.pallas import tpu as pltpu
from jax.sharding import PartitionSpec as P

HD = 128
ATT_SCALAR = 144
EPS = 1e-6
VMEM = 56 * 1024 * 1024
B_CHUNKS = 2


def params(**more):
    return pltpu.CompilerParams(vmem_limit_bytes=VMEM, **more)


def qkv_kernel(parts, heads, *refs):
    x_refs = refs[:parts]
    gain, wq, wk, wv, cosine, sine, q_out, kv_out, acc, squares = refs[parts:]
    step, steps = pl.program_id(0), pl.num_programs(0)
    rows = x_refs[0].shape[0]
    width = x_refs[0].shape[1]

    @pl.when(step == 0)
    def _():
        acc[...] = jnp.zeros_like(acc)
        squares[...] = jnp.zeros_like(squares)

    weights = jnp.concatenate([wq[...], wk[...], wv[...]], axis=1)
    for part, x_ref in enumerate(x_refs):
        span = pl.ds(part * rows, rows)
        x = x_ref[...].astype(jnp.float32)
        square = x * x
        folded = square[:, :128]
        for lane in range(128, width, 128):
            folded = folded + square[:, lane : lane + 128]
        squares[span, :] += folded
        scaled = (x * gain[...]).astype(jnp.bfloat16)
        acc[span, :] += jnp.dot(scaled, weights, preferred_element_type=jnp.float32)

    @pl.when(step == steps - 1)
    def _():
        total = jnp.sum(squares[...], axis=1, keepdims=True)
        scale = lax.rsqrt(total / (width * steps) + EPS)
        cos, sin = cosine[...], sine[...]

        def rotated(at):
            y = acc[:, at * HD : (at + 1) * HD] * scale
            return y * cos + pltpu.roll(y, HD // 2, 1) * sin

        factor = ATT_SCALAR ** (-0.5) * math.log2(math.e)
        for head in range(heads):
            q_out[:, head * HD : (head + 1) * HD] = (rotated(head) * factor).astype(jnp.bfloat16)
        kv_out[:, :HD] = rotated(heads).astype(jnp.bfloat16)
        kv_out[:, HD:] = (acc[:, (heads + 1) * HD :] * scale).astype(jnp.bfloat16)


def qkv(xs, gain, wq, wk, wv, cosine, sine):
    parts, (rows, width) = len(xs), xs[0].shape
    total = parts * rows
    heads = wq.shape[1] // HD
    columns = wq.shape[1] + 2 * HD
    depth = width // 4
    by_depth = lambda n: pl.BlockSpec((depth, n), lambda k: (k, 0))
    whole = lambda n: pl.BlockSpec((total, n), lambda k: (0, 0))
    return pl.pallas_call(
        functools.partial(qkv_kernel, parts, heads),
        grid=(width // depth,),
        in_specs=[pl.BlockSpec((rows, depth), lambda k: (0, k))] * parts
        + [pl.BlockSpec((1, depth), lambda k: (0, k))]
        + [by_depth(wq.shape[1]), by_depth(HD), by_depth(HD), whole(HD), whole(HD)],
        out_specs=[whole(wq.shape[1]), whole(2 * HD)],
        out_shape=[
            jax.ShapeDtypeStruct((total, wq.shape[1]), jnp.bfloat16),
            jax.ShapeDtypeStruct((total, 2 * HD), jnp.bfloat16),
        ],
        scratch_shapes=[
            pltpu.VMEM((total, columns), jnp.float32),
            pltpu.VMEM((total, 128), jnp.float32),
        ],
        compiler_params=params(),
        cost_estimate=pl.CostEstimate(
            flops=2 * total * width * columns,
            bytes_accessed=2 * width * (total + columns),
            transcendentals=0,
        ),
        name="norm_qkv",
    )(*xs, gain.reshape(1, -1), wq, wk, wv, cosine, sine)


def attention_kernel(kv_parts, heads, tile, starts, *refs):
    (q_ref,) = refs[:1]
    kv_refs = refs[1 : 1 + kv_parts]
    out, kv, peak, acc, arrived = refs[1 + kv_parts :]
    q_blocks, rows, _ = q_ref.shape
    slots = kv.shape[0]
    each = slots // kv_parts
    copies = [
        pltpu.make_async_copy(part, kv.at[pl.ds(at * each, each)], arrived.at[at])
        for at, part in enumerate(kv_refs)
    ]
    for copy in copies:
        copy.start()
    for copy in copies:
        copy.wait()
    ones = jnp.ones((rows, HD), jnp.bfloat16)

    def attend(block, slot, diagonal):
        keys = kv[slot, :, :HD]
        values = jnp.concatenate([kv[slot, :, HD:], ones], axis=1)
        for first in range(0, rows, tile):
            for head in range(heads):
                span = pl.ds(first, tile)
                q = q_ref[block, span, head * HD : (head + 1) * HD]
                scores = lax.dot_general(
                    q, keys, (((1,), (1,)), ((), ())), preferred_element_type=jnp.float32
                )
                if diagonal:
                    row = first + lax.broadcasted_iota(jnp.int32, scores.shape, 0)
                    column = lax.broadcasted_iota(jnp.int32, scores.shape, 1)
                    scores = jnp.where(column <= row, scores, -1e30)
                top = jnp.broadcast_to(jnp.max(scores, axis=1, keepdims=True), (tile, HD))
                if not diagonal:
                    before = peak[block, head, span, :]
                    top = jnp.maximum(before, top)
                wide = jnp.concatenate([top] * (rows // HD), axis=1)
                weights = jnp.exp2(scores - wide).astype(jnp.bfloat16)
                summed = jnp.dot(weights, values, preferred_element_type=jnp.float32)
                if not diagonal:
                    fade = jnp.exp2(before - top)
                    fade = jnp.concatenate([fade, fade], axis=1)
                    summed = summed + acc[block, head, span, :] * fade
                acc[block, head, span, :] = summed
                peak[block, head, span, :] = top

    def per_block(block, carry):
        q_start = starts[block]

        def same(slot, carry):
            @pl.when(starts[q_blocks + slot] == q_start)
            def _():
                attend(block, slot, True)

            return carry

        def earlier(slot, carry):
            @pl.when(starts[q_blocks + slot] < q_start)
            def _():
                attend(block, slot, False)

            return carry

        lax.fori_loop(0, slots, same, 0)
        lax.fori_loop(0, slots, earlier, 0)
        for head in range(heads):
            result = acc[block, head]
            out[block, :, head * HD : (head + 1) * HD] = (
                result[:, :HD] / result[:, HD:]
            ).astype(jnp.bfloat16)
        return carry

    lax.fori_loop(0, q_blocks, per_block, 0)


def attention(q, kv_parts, q_starts, kv_starts):
    blocks, rows, columns = q.shape
    heads = columns // HD
    slots = sum(part.shape[0] for part in kv_parts)
    return pl.pallas_call(
        functools.partial(attention_kernel, len(kv_parts), heads, 128),
        in_specs=[pl.BlockSpec(memory_space=pltpu.SMEM), pl.BlockSpec(memory_space=pltpu.VMEM)]
        + [pl.BlockSpec(memory_space=pl.ANY)] * len(kv_parts),
        out_specs=pl.BlockSpec(memory_space=pltpu.VMEM),
        out_shape=jax.ShapeDtypeStruct(q.shape, jnp.bfloat16),
        scratch_shapes=[
            pltpu.VMEM((slots, rows, 2 * HD), jnp.bfloat16),
            pltpu.VMEM((blocks, heads, rows, HD), jnp.float32),
            pltpu.VMEM((blocks, heads, rows, 2 * HD), jnp.float32),
            pltpu.SemaphoreType.DMA((len(kv_parts),)),
        ],
        compiler_params=params(),
        cost_estimate=pl.CostEstimate(
            flops=4 * q.size * slots * rows,
            bytes_accessed=4 * q.size + 4 * slots * rows * HD,
            transcendentals=blocks * heads * slots * rows * rows,
        ),
        name="attention",
    )(jnp.concatenate([q_starts, kv_starts]), q, *kv_parts)


def output_kernel(places, chunks, at, *refs):
    attended = refs[:4]
    pieces = refs[4 : 4 + len(places)]
    hidden, gain, out, weights, projected, arrived = refs[4 + len(places) :]
    width = hidden.shape[1]
    step = width // chunks

    def copies(chunk):
        lanes = pl.ds(chunk * step, step)
        return [
            pltpu.make_async_copy(
                piece.at[:, lanes],
                weights.at[pl.ds(pl.multiple_of(at[index], 16), places[index]), lanes],
                arrived.at[chunk, index],
            )
            for index, piece in enumerate(pieces)
        ]

    for chunk in range(chunks):
        for copy in copies(chunk):
            copy.start()
    left = jnp.concatenate([part[...] for part in attended], axis=1)
    square = jnp.zeros((hidden.shape[0], 128), jnp.float32)
    for chunk in range(chunks):
        for copy in copies(chunk):
            copy.wait()
        lanes = pl.ds(chunk * step, step)
        part = jnp.dot(left, weights[:, lanes], preferred_element_type=jnp.float32)
        projected[:, lanes] = part
        for lane in range(0, step, 128):
            piece = part[:, lane : lane + 128]
            square = square + piece * piece
    mean = jnp.sum(square, axis=1, keepdims=True) / width
    scale = lax.rsqrt(mean + EPS)
    for chunk in range(chunks):
        lanes = pl.ds(chunk * step, step)
        normed = projected[:, lanes] * scale * gain[:, lanes]
        out[:, lanes] = (hidden[:, lanes].astype(jnp.float32) + normed).astype(jnp.bfloat16)


def output(attended, pieces, places, hidden, gain):
    rows, width = hidden.shape
    depth = sum(piece.shape[0] for piece in pieces)
    chunks = 6
    vmem = pl.BlockSpec(memory_space=pltpu.VMEM)
    return pl.pallas_call(
        functools.partial(output_kernel, [piece.shape[0] for piece in pieces], chunks),
        in_specs=[pl.BlockSpec(memory_space=pltpu.SMEM)]
        + [vmem] * 4
        + [pl.BlockSpec(memory_space=pl.ANY)] * len(pieces)
        + [vmem, vmem],
        out_specs=vmem,
        out_shape=jax.ShapeDtypeStruct(hidden.shape, jnp.bfloat16),
        scratch_shapes=[
            pltpu.VMEM((depth, width), jnp.bfloat16),
            pltpu.VMEM((rows, width), jnp.float32),
            pltpu.SemaphoreType.DMA((chunks, len(pieces))),
        ],
        compiler_params=params(),
        cost_estimate=pl.CostEstimate(
            flops=2 * rows * width * depth,
            bytes_accessed=2 * width * (depth + 2 * rows),
            transcendentals=0,
        ),
        name="output_norm",
    )(places, *attended, *pieces, hidden, gain.reshape(1, -1))


def rotary_tables(positions):
    half = HD // 2
    frequency = jnp.power(
        jnp.float32(10000.0), -jnp.arange(half, dtype=jnp.float32) * (2.0 / HD)
    )
    angles = positions.astype(jnp.float32)[:, None] * frequency[None, :]
    cos, sin = jnp.cos(angles), jnp.sin(angles)
    return jnp.concatenate([cos, cos], axis=1), jnp.concatenate([-sin, sin], axis=1)


def lookup(block_of, index):
    ids = jnp.arange(block_of.shape[0], dtype=jnp.int32)
    return jnp.sum(jnp.where(index[..., None] == ids, block_of, 0), axis=-1)


def flipped(array, axis, bit):
    size = lax.axis_size(axis)
    return lax.ppermute(array, axis, [(i, i ^ bit) for i in range(size)])


def shifted(array, axis, by):
    size = lax.axis_size(axis)
    return lax.ppermute(array, axis, [(i, (i + by) % size) for i in range(size)])


def after(array, *others):
    return lax.optimization_barrier((array, *others))[0]


def two_chips(hidden, pre_gain, post_gain, wq, wk, wv, w_out, block_of):
    rows = hidden.shape[0]
    block_rows = 2 * rows
    seq_count, group_count = lax.axis_size("seq"), lax.axis_size("groups")
    seq, tp, group = lax.axis_index("seq"), lax.axis_index("tp"), lax.axis_index("groups")
    chip = tp // 2
    core = tp % 2

    def in_order(mine, other):
        return jnp.where(core == 0, mine, other), jnp.where(core == 0, other, mine)

    lines = (seq - jnp.arange(seq_count, dtype=jnp.int32)) % seq_count
    near_starts = lookup(block_of, 2 * lines + chip) * block_rows
    far_starts = lookup(block_of, 2 * lines + 1 - chip) * block_rows
    offsets = jnp.arange(block_rows, dtype=jnp.int32)
    positions = jnp.concatenate([near_starts[0] + offsets, far_starts[0] + offsets])
    cosine, sine = rotary_tables(positions)

    size = rows // B_CHUNKS
    far = []
    for at in range(B_CHUNKS):
        far.append(flipped(hidden[at * size : (at + 1) * size], "tp", 2))
    partner = flipped(hidden, "tp", 1)

    def project(mine, other, which):
        xs = in_order(mine, other)
        return qkv(xs, pre_gain, wq, wk, wv, cosine[which], sine[which])

    q_near, kv_near = project(hidden, partner, slice(0, block_rows))
    near_parts = [kv_near] + [shifted(kv_near, "seq", by) for by in range(1, seq_count)]

    half = w_out.shape[0] // group_count
    sent = lax.dynamic_slice_in_dim(w_out, group * half, half, axis=0)
    sent = after(sent, *far)
    w_far = [flipped(sent, "tp", 2)]
    w_far += [shifted(w_far[0], "groups", by) for by in range(1, group_count)]
    w_partner = flipped(w_out, "tp", 1)
    w_cross = [flipped(piece, "tp", 1) for piece in w_far]

    far_mine = jnp.concatenate(far, axis=0)
    far_other = jnp.concatenate([flipped(piece, "tp", 1) for piece in far], axis=0)
    q_far, kv_far = project(far_mine, far_other, slice(block_rows, 2 * block_rows))
    far_parts = [kv_far] + [shifted(kv_far, "seq", by) for by in range(1, seq_count)]

    attended = attention(
        jnp.stack([q_near, q_far]),
        [part[None] for part in near_parts + far_parts],
        jnp.stack([near_starts[0], far_starts[0]]),
        jnp.concatenate([near_starts, far_starts]),
    )
    near = attended[0].reshape(2, rows, -1)
    away = attended[1].reshape(2, rows, -1)
    pick = lambda pair, which: jnp.where(which == 0, pair[0], pair[1])
    gathered = [
        pick(near, core),
        flipped(pick(near, 1 - core), "tp", 1),
        flipped(pick(away, core), "tp", 2),
        flipped(pick(away, 1 - core), "tp", 3),
    ]
    depth = w_out.shape[0]
    order = [(group - by) % group_count * half for by in range(group_count)]
    places = [0, depth] + [2 * depth + at for at in order] + [3 * depth + at for at in order]
    places = jnp.stack([jnp.asarray(at, jnp.int32) for at in places])
    return output(gathered, [w_out, w_partner] + w_far + w_cross, places, hidden, post_gain)


def any_count(hidden, pre_gain, post_gain, wq, wk, wv, w_out, block_of):
    normed_rows = lax.all_gather(hidden, "tp", axis=0, tiled=True)
    seq_rows = normed_rows.shape[0]
    block_rows = seq_rows // 2
    own = 2 * lax.axis_index("seq") + jnp.arange(2, dtype=jnp.int32)
    q_starts = lookup(block_of, own) * block_rows
    offsets = jnp.arange(block_rows, dtype=jnp.int32)
    cosine, sine = rotary_tables((q_starts[:, None] + offsets).reshape(-1))
    q, kv = qkv([normed_rows], pre_gain, wq, wk, wv, cosine, sine)
    kv = lax.all_gather(kv, "seq", axis=0, tiled=True).reshape(-1, block_rows, kv.shape[1])
    attended = attention(
        q.reshape(2, block_rows, -1), [kv], q_starts, block_of * block_rows
    ).reshape(seq_rows, -1)
    partial = jnp.dot(attended, w_out, preferred_element_type=jnp.float32)
    summed = lax.psum_scatter(
        partial.astype(jnp.bfloat16), "tp", scatter_dimension=0, tiled=True
    ).astype(jnp.float32)
    mean = jnp.mean(summed * summed, axis=-1, keepdims=True)
    normed = summed * lax.rsqrt(mean + EPS) * post_gain
    return (hidden.astype(jnp.float32) + normed).astype(jnp.bfloat16)


def solution(mesh):
    return jax.shard_map(
        two_chips if mesh.shape["tp"] == 4 else any_count,
        mesh=mesh,
        in_specs=(
            P(("groups", "seq", "tp"), None),
            P(),
            P(),
            P(None, "tp"),
            P(None, "tp"),
            P(None, "tp"),
            P("tp", None),
            P(),
        ),
        out_specs=P(("groups", "seq", "tp"), None),
        check_vma=False,
    )
```

time: 273 us -> 169 us (0.62)
  matrix products: 67.3 us -> 0 us
  blocking collectives: 38.7 us -> 0 us
  Pallas kernels: 0 us -> 34.2 us
  waiting for transfers between devices: 113 us -> 84.8 us
  starting transfers between devices: 0.04 us -> 26.4 us
  between operations: 13.6 us -> 0.23 us
  other arithmetic: 22.2 us -> 11.8 us
  loops' own time: 5.53 us -> 0 us
    ppermute x0 -> x19, waiting for transfers between devices: none -> 84.8 us  [the longest x12 46.6 us: flipped(): return lax.ppermute(array, axis, [(i, i ^ bit) for i in range(size)])]
    dot_general x20 -> x0, matrix products: 67.3 us -> none  [the longest x8 24 us: update(): jnp.einsum('qhd,kd->hqk', queries, keys_block, preferred_element_type=jnp...]
    reduce_scatter x1 -> x0, waiting for transfers between devices: 62.6 us -> none  [body(): lax.psum_scatter(jnp.dot(attended, w_out, preferred_element_type=jnp.floa...]
    all_gather x1 -> x0, waiting for transfers between devices: 50.4 us -> none  [body(): normed = lax.all_gather(normed_local, 'tp', axis=0, tiled=True)]
    all_gather x2 -> x0, blocking collectives: 38.7 us -> none  [the longest x1 19.9 us: body(): lax.all_gather(keys_local, 'seq', axis=0, tiled=True)]
    pallas_call x0 -> x4, Pallas kernels: none -> 34.2 us  [the longest x2 14 us: qkv(): pl.pallas_call(functools.partial(qkv_kernel, parts, heads), grid=(width /...]
    ppermute x0 -> x19, starting transfers between devices: none -> 26.4 us  [the longest x7 18.3 us: shifted(): lax.ppermute(array, axis, [(i, (i + by) % size) for i in range(size)])]
    reduce_sum x19 -> x1, other arithmetic: 8.76 us -> 0.21 us  [lookup(): return jnp.sum(jnp.where(index[..., None] == ids, block_of, 0), axis=-1)]
  transfers between devices with their start and end apart: 2 -> 19, of which waited for: 2 -> 10; matrix products, arithmetic and copies ran while one was open for 1% -> 12% of each run, Pallas kernels for 0% -> 15%
where the time goes in v1:
time: 169 us; the launch traced here: 168 us
  waiting for transfers between devices  84.8 us (50%)
  Pallas kernels  34.2 us (20%)
  starting transfers between devices  26.4 us (16%)
  other arithmetic  11.8 us (7%)
  local copies, waits for them, and re-layouts  10.6 us (6%)
    ppermute x12, waiting for transfers between devices, flipped(): return lax.ppermute(array, axis, [(i, i ^ bit) for i in range(size)])  46.6 us
    ppermute x7, waiting for transfers between devices, shifted(): lax.ppermute(array, axis, [(i, (i + by) % size) for i in range(size)])  38.3 us
    ppermute x7, starting transfers between devices, shifted(): lax.ppermute(array, axis, [(i, (i + by) % size) for i in range(size)])  18.3 us
    pallas_call x2, Pallas kernels, qkv(): pl.pallas_call(functools.partial(qkv_kernel, parts, heads), grid=(width /...  14 us
    pallas_call x1, Pallas kernels, attention(): pl.pallas_call(functools.partial(attention_kernel, len(kv_parts), heads,...  11.2 us
    pallas_call x1, Pallas kernels, output(): pl.pallas_call(functools.partial(output_kernel, [piece.shape[0] for piece...  8.99 us
    ppermute x12, starting transfers between devices, flipped(): return lax.ppermute(array, axis, [(i, i ^ bit) for i in range(size)])  8.06 us
    select_n x2, other arithmetic, in_order(): jnp.where(core == 0, other, mine)  4.08 us
  transfers between devices with their start and end apart: 19, of which 10 were waited for; matrix products, arithmetic and copies ran while one was open for 12% of the time, Pallas kernels for 15%

profile of v1, /device:TPU:0, one launch (start us, length us, event | category | flops | bytes accessed | tf_op | source)
XLA Modules:
  0.0 168.0 jit_solution(13240511121556590530)
XLA Ops:
  0.5 2.8 %fusion.5 = (bf16[96,4608]{1,0:T(8,128)(2,1)}, bf16[96,4608]{1,0:T(8,128)(2,1)}) fusion(bf16[192,4608]{1,0:T(8,128)(2,1)} %refs_10_.1), kind=kLoop, calls=%fused_computation.43 | loop fusion | bytes 3538944 | tf_op jit(solution)/shard_map/slice | solution.py:314
  3.2 2.5 %collective-permute-start.1 = (bf16[96,4608]{1,0:T(8,128)(2,1)}, bf16[96,4608]{1,0:T(8,128)(2,1)}, u32[]{:S(2)}, u32[]{:S(2)}) collective-permute-start(bf16[96,4608]{1,0:T(8,128)(2,1)} %get-tuple-element.22), channel_id=1, source_target_pairs={{0,8},{4,12},{8,0},{12,4},{1,9},{5,13},{9,1},{13,5},{2,10},{6,14},... | collective-permute-start | bytes 2654216 | tf_op jit(solution)/shard_map/ppermute | solution.py:281
  6.4 1.4 fusion.2
  10.3 1.3 constant_dynamic-slice_fusion
  11.7 14.9 %collective-permute-done.1 = bf16[96,4608]{1,0:T(8,128)(2,1)} collective-permute-done((bf16[96,4608]{1,0:T(8,128)(2,1)}, bf16[96,4608]{1,0:T(8,128)(2,1)}, u32[]{:S(2)}, u32[]{:S(2)}) %collective-permute-start.1) | collective-permute-done | bytes 884768 | tf_op jit(solution)/shard_map/ppermute | solution.py:281
  26.6 18.8 %collective-permute-done.2 = bf16[96,4608]{1,0:T(8,128)(2,1)} collective-permute-done((bf16[96,4608]{1,0:T(8,128)(2,1)}, bf16[96,4608]{1,0:T(8,128)(2,1)}, u32[]{:S(2)}, u32[]{:S(2)}) %collective-permute-start.2) | collective-permute-done | bytes 884768 | tf_op jit(solution)/shard_map/ppermute | solution.py:281
  45.4 1.7 %collective-permute-start.15 = (bf16[128,4608]{1,0:T(8,128)(2,1)S(1)}, bf16[128,4608]{1,0:T(8,128)(2,1)}, u32[]{:S(2)}, u32[]{:S(2)}) collective-permute-start(bf16[128,4608]{1,0:T(8,128)(2,1)S(1)} %constant_dynamic-slice_fusion), channel_id=1, source_target_pairs={{0,8},{4,12},{8,0},{12,4},{1,9},{5,13},{9,1},{13,5},{2,10},{6,14},... | collective-permute-start | bytes 3538952 | tf_op jit(solution)/shard_map/ppermute | solution.py:281
  47.6 1.2 constant_dynamic-update-slice_fusion.1
  48.8 1.2 constant_dynamic-update-slice_fusion
  51.1 2.0 %broadcast_select_fusion = (bf16[192,4608]{1,0:T(8,128)(2,1)}, bf16[192,4608]{1,0:T(8,128)(2,1)}) fusion(bf16[192,4608]{1,0:T(8,128)(2,1)S(1)} %constant_dynamic-update-slice_fusion.2, bf16[192,4608]{1,0:T(8,128)(2,1)S(1)} %constant_dynamic-update-slice_fusion, pred[]{:T(512)S(6)} %eq.22), kind=kLoop, calls=%fused_computation | loop fusion | flops 1769472 | bytes 7077889 | tf_op jit(solution)/shard_map/jit(_where)/select_n | solution.py:302
  53.1 7.0 %norm_qkv.3 = (bf16[384,256]{1,0:T(8,128)(2,1)}, bf16[384,256]{1,0:T(8,128)(2,1)}) custom-call(bf16[192,4608]{1,0:T(8,128)(2,1)} %get-tuple-element.20.refs_0_, bf16[192,4608]{1,0:T(8,128)(2,1)} %get-tuple-element.19.refs_1_, f32[1,4608]{1,0:T(1,128)} %reshape.63.refs_2_, bf16[4608,256]{1,0:T(8,128)(2,1)} %refs_3_.3, bf16[4608,128]{1,0:T(8,128)(2,1)} %refs_4_.4, ...), custom_call_target="tpu_custom_call" | custom-call | flops 1811939328 | bytes 8257536 | tf_op jit(solution)/shard_map/norm_qkv/pallas_call | solution.py:71
  60.1 1.6 collective-permute-start.8
  61.7 2.6 %collective-permute-start.9 = (bf16[384,256]{1,0:T(8,128)(2,1)}, bf16[384,256]{1,0:T(8,128)(2,1)S(1)}, u32[]{:S(2)}, u32[]{:S(2)}) collective-permute-start(bf16[384,256]{1,0:T(8,128)(2,1)} %get-tuple-element.13), channel_id=1, source_target_pairs={{0,2},{1,3},{2,0},{3,1},{4,6},{5,7},{6,4},{7,5},{8,10},{9,11},{10,... | collective-permute-start | bytes 589832 | tf_op jit(solution)/shard_map/ppermute | solution.py:286
  64.3 8.9 %collective-permute-done.15.refs_6_ = bf16[128,4608]{1,0:T(8,128)(2,1)} collective-permute-done((bf16[128,4608]{1,0:T(8,128)(2,1)S(1)}, bf16[128,4608]{1,0:T(8,128)(2,1)}, u32[]{:S(2)}, u32[]{:S(2)}) %collective-permute-start.15) | collective-permute-done | bytes 1179680 | tf_op jit(solution)/shard_map/ppermute | solution.py:281
  73.2 1.5 collective-permute-start.16
  74.8 2.0 %broadcast_select_fusion.2 = (bf16[192,4608]{1,0:T(8,128)(2,1)}, bf16[192,4608]{1,0:T(8,128)(2,1)}) fusion(bf16[192,4608]{1,0:T(8,128)(2,1)S(1)} %collective-permute-done, bf16[192,4608]{1,0:T(8,128)(2,1)S(1)} %copy-done, pred[]{:T(512)S(6)} %eq.22), kind=kLoop, calls=%fused_computation.2 | loop fusion | flops 1769472 | bytes 7077889 | tf_op jit(solution)/shard_map/jit(_where)/select_n | solution.py:302
  76.8 23.7 %collective-permute-done.16.refs_7_ = bf16[128,4608]{1,0:T(8,128)(2,1)} collective-permute-done((bf16[128,4608]{1,0:T(8,128)(2,1)}, bf16[128,4608]{1,0:T(8,128)(2,1)}, u32[]{:S(2)}, u32[]{:S(2)}) %collective-permute-start.16) | collective-permute-done | bytes 1179680 | tf_op jit(solution)/shard_map/ppermute | solution.py:286
  100.5 6.9 %norm_qkv.2 = (bf16[384,256]{1,0:T(8,128)(2,1)}, bf16[384,256]{1,0:T(8,128)(2,1)}) custom-call(bf16[192,4608]{1,0:T(8,128)(2,1)} %get-tuple-element.18.refs_0_, bf16[192,4608]{1,0:T(8,128)(2,1)} %get-tuple-element.17.refs_1_, f32[1,4608]{1,0:T(1,128)} %reshape.63.refs_2_, bf16[4608,256]{1,0:T(8,128)(2,1)} %refs_3_.3, bf16[4608,128]{1,0:T(8,128)(2,1)} %refs_4_.4, ...), custom_call_target="tpu_custom_call" | custom-call | flops 1811939328 | bytes 8257536 | tf_op jit(solution)/shard_map/norm_qkv/pallas_call | solution.py:71
  107.5 3.4 %collective-permute-start.10 = (bf16[384,256]{1,0:T(8,128)(2,1)S(1)}, bf16[384,256]{1,0:T(8,128)(2,1)S(1)}, u32[]{:S(2)}, u32[]{:S(2)}) collective-permute-start(bf16[384,256]{1,0:T(8,128)(2,1)S(1)} %copy-done.10), channel_id=1, source_target_pairs={{0,3},{1,0},{2,1},{3,2},{4,7},{5,4},{6,5},{7,6},{8,11},{9,8},{10,9... | collective-permute-start | bytes 589832 | tf_op jit(solution)/shard_map/ppermute | solution.py:286
  110.9 5.2 %collective-permute-done.10 = bf16[384,256]{1,0:T(8,128)(2,1)S(1)} collective-permute-done((bf16[384,256]{1,0:T(8,128)(2,1)S(1)}, bf16[384,256]{1,0:T(8,128)(2,1)S(1)}, u32[]{:S(2)}, u32[]{:S(2)}) %collective-permute-start.10) | collective-permute-done | bytes 196640 | tf_op jit(solution)/shard_map/ppermute | solution.py:286
  116.2 4.3 %collective-permute-start.7 = (bf16[384,256]{1,0:T(8,128)(2,1)}, bf16[384,256]{1,0:T(8,128)(2,1)S(1)}, u32[]{:S(2)}, u32[]{:S(2)}) collective-permute-start(bf16[384,256]{1,0:T(8,128)(2,1)} %get-tuple-element.12), channel_id=1, source_target_pairs={{0,3},{1,0},{2,1},{3,2},{4,7},{5,4},{6,5},{7,6},{8,11},{9,8},{10,9... | collective-permute-start | bytes 589832 | tf_op jit(solution)/shard_map/ppermute | solution.py:286
  120.5 4.1 %collective-permute-done.6 = bf16[384,256]{1,0:T(8,128)(2,1)} collective-permute-done((bf16[384,256]{1,0:T(8,128)(2,1)}, bf16[384,256]{1,0:T(8,128)(2,1)}, u32[]{:S(2)}, u32[]{:S(2)}) %collective-permute-start.6) | collective-permute-done | bytes 196640 | tf_op jit(solution)/shard_map/ppermute | solution.py:286
  124.6 4.8 %collective-permute-start.5 = (bf16[384,256]{1,0:T(8,128)(2,1)}, bf16[384,256]{1,0:T(8,128)(2,1)S(1)}, u32[]{:S(2)}, u32[]{:S(2)}) collective-permute-start(bf16[384,256]{1,0:T(8,128)(2,1)} %get-tuple-element.12), channel_id=1, source_target_pairs={{0,1},{1,2},{2,3},{3,0},{4,5},{5,6},{6,7},{7,4},{8,9},{9,10},{10,1... | collective-permute-start | bytes 589832 | tf_op jit(solution)/shard_map/ppermute | solution.py:286
  130.1 1.7 %pad_maximum_fusion.refs_0_ = bf16[2,384,256]{2,1,0:T(8,128)(2,1)} fusion(bf16[1,384,256]{2,1,0:T(8,128)(2,1)S(1)} %bitcast.26, bf16[1,384,256]{2,1,0:T(8,128)(2,1)} %bitcast.27), kind=kLoop, calls=%fused_computation.10 | loop fusion | flops 196608 | bytes 786432 | tf_op jit(solution)/shard_map/stack | solution.py:338
  131.8 5.2 %collective-permute-done.5 = bf16[384,256]{1,0:T(8,128)(2,1)S(1)} collective-permute-done((bf16[384,256]{1,0:T(8,128)(2,1)}, bf16[384,256]{1,0:T(8,128)(2,1)S(1)}, u32[]{:S(2)}, u32[]{:S(2)}) %collective-permute-start.5) | collective-permute-done | bytes 196640 | tf_op jit(solution)/shard_map/ppermute | solution.py:286
  137.7 11.2 %attention.1 = bf16[2,384,256]{2,1,0:T(8,128)(2,1)} custom-call(s32[10]{0:T(128)} %pad_add_fusion.starts, bf16[2,384,256]{2,1,0:T(8,128)(2,1)} %pad_maximum_fusion.refs_0_, bf16[1,384,256]{2,1,0:T(8,128)(2,1)} %bitcast.35, bf16[1,384,256]{2,1,0:T(8,128)(2,1)} %bitcast.38, bf16[1,384,256]{2,1,0:T(8,128)(2,1)} %bitcast.10.refs_3_, ...), custom_call_target="tpu_custom_call" | custom-call | flops 2415919104 | bytes 2359296 | tf_op jit(solution)/shard_map/attention/pallas_call | solution.py:174
  148.9 1.7 %select_bitcast_fusion = (bf16[192,256]{1,0:T(8,128)(2,1)S(1)}, bf16[192,256]{1,0:T(8,128)(2,1)S(1)}, bf16[192,256]{1,0:T(8,128)(2,1)}, bf16[192,256]{1,0:T(8,128)(2,1)S(1)}) fusion(pred[]{:T(512)S(6)} %eq.51, bf16[2,384,256]{2,1,0:T(8,128)(2,1)} %attention.1, pred[]{:T(512)S(6)} %eq.22), kind=kLoop, calls=%fused_computation.16 | loop fusion | flops 196608 | bytes 786434 | tf_op jit(solution)/shard_map/jit(_where)/select_n | solution.py:345
  150.7 1.5 collective-permute-start.12
  152.2 1.1 collective-permute-start.13
  154.5 1.7 %collective-permute-done.12.refs_2_ = bf16[192,256]{1,0:T(8,128)(2,1)S(1)} collective-permute-done((bf16[192,256]{1,0:T(8,128)(2,1)S(1)}, bf16[192,256]{1,0:T(8,128)(2,1)S(1)}, u32[]{:S(2)}, u32[]{:S(2)}) %collective-permute-start.12) | collective-permute-done | bytes 98336 | tf_op jit(solution)/shard_map/ppermute | solution.py:281
  156.3 1.3 collective-permute-done.13.refs_3_
  159.0 9.0 %output_norm.1 = bf16[192,4608]{1,0:T(8,128)(2,1)} custom-call(s32[6]{0:T(128)} %stack.28.at, bf16[192,256]{1,0:T(8,128)(2,1)} %get-tuple-element.27.refs_0_, bf16[192,256]{1,0:T(8,128)(2,1)} %copy-done.4, bf16[192,256]{1,0:T(8,128)(2,1)} %copy-done.5, bf16[192,256]{1,0:T(8,128)(2,1)} %copy-done.6, bf16[256,4608]{1,0:T(8,128)(2,1)} %refs_4_.5, ...), custom_call_target="tpu_custom_call" | custom-call | flops 1811939328 | bytes 12976128 | tf_op jit(solution)/shard_map/output_norm/pallas_call | solution.py:241
  (67 shorter events, 9.0 us)
Async XLA Ops:
  0.0 6.0 %copy-start.9 = (s32[8]{0:T(128)S(1)}, s32[8]{0:T(128)}, u32[]{:S(2)}) copy-start(s32[8]{0:T(128)} %param.15) | copy-start | bytes 100
  0.0 7.9 %copy-start.7 = (f32[4608]{0:T(1024)S(1)}, f32[4608]{0:T(1024)}, u32[]{:S(2)}) copy-start(f32[4608]{0:T(1024)} %param.9) | copy-start | bytes 55300
  0.0 74.7 %collective-permute-start = (bf16[192,4608]{1,0:T(8,128)(2,1)}, bf16[192,4608]{1,0:T(8,128)(2,1)S(1)}, u32[]{:S(2)}, u32[]{:S(2)}) collective-permute-start(bf16[192,4608]{1,0:T(8,128)(2,1)} %refs_10_.1), channel_id=1, source_target_pairs={{0,4},{4,0},{8,12},{12,8},{1,5},{5,1},{9,13},{13,9},{2,6},{6,2},{1... | collective-permute-start | bytes 5308424 | tf_op jit(solution)/shard_map/ppermute | solution.py:281
  3.2 23.4 %collective-permute-start.1 = (bf16[96,4608]{1,0:T(8,128)(2,1)}, bf16[96,4608]{1,0:T(8,128)(2,1)}, u32[]{:S(2)}, u32[]{:S(2)}) collective-permute-start(bf16[96,4608]{1,0:T(8,128)(2,1)} %get-tuple-element.22), channel_id=1, source_target_pairs={{0,8},{4,12},{8,0},{12,4},{1,9},{5,13},{9,1},{13,5},{2,10},{6,14},... | collective-permute-start | bytes 2654216 | tf_op jit(solution)/shard_map/ppermute | solution.py:281
  5.8 39.6 %collective-permute-start.2 = (bf16[96,4608]{1,0:T(8,128)(2,1)}, bf16[96,4608]{1,0:T(8,128)(2,1)}, u32[]{:S(2)}, u32[]{:S(2)}) collective-permute-start(bf16[96,4608]{1,0:T(8,128)(2,1)} %get-tuple-element.21), channel_id=1, source_target_pairs={{0,8},{4,12},{8,0},{12,4},{1,9},{5,13},{9,1},{13,5},{2,10},{6,14},... | collective-permute-start | bytes 2654216 | tf_op jit(solution)/shard_map/ppermute | solution.py:281
  5.8 151.8 %collective-permute-start.14 = (bf16[256,4608]{1,0:T(8,128)(2,1)}, bf16[256,4608]{1,0:T(8,128)(2,1)}, u32[]{:S(2)}, u32[]{:S(2)}) collective-permute-start(bf16[256,4608]{1,0:T(8,128)(2,1)} %refs_4_.5), channel_id=1, source_target_pairs={{0,4},{4,0},{8,12},{12,8},{1,5},{5,1},{9,13},{13,9},{2,6},{6,2},{1... | collective-permute-start | bytes 7077896 | tf_op jit(solution)/shard_map/ppermute | solution.py:281
  45.4 27.9 %collective-permute-start.15 = (bf16[128,4608]{1,0:T(8,128)(2,1)S(1)}, bf16[128,4608]{1,0:T(8,128)(2,1)}, u32[]{:S(2)}, u32[]{:S(2)}) collective-permute-start(bf16[128,4608]{1,0:T(8,128)(2,1)S(1)} %constant_dynamic-slice_fusion), channel_id=1, source_target_pairs={{0,8},{4,12},{8,0},{12,4},{1,9},{5,13},{9,1},{13,5},{2,10},{6,14},... | collective-permute-start | bytes 3538952 | tf_op jit(solution)/shard_map/ppermute | solution.py:281
  47.1 3.0 %collective-permute-start.3 = (bf16[96,4608]{1,0:T(8,128)(2,1)}, bf16[96,4608]{1,0:T(8,128)(2,1)S(1)}, u32[]{:S(2)}, u32[]{:S(2)}) collective-permute-start(bf16[96,4608]{1,0:T(8,128)(2,1)} %collective-permute-done.1), channel_id=1, source_target_pairs={{0,4},{4,0},{8,12},{12,8},{1,5},{5,1},{9,13},{13,9},{2,6},{6,2},{1... | collective-permute-start | bytes 2654216 | tf_op jit(solution)/shard_map/ppermute | solution.py:281
  47.1 3.9 %collective-permute-start.4 = (bf16[96,4608]{1,0:T(8,128)(2,1)}, bf16[96,4608]{1,0:T(8,128)(2,1)S(1)}, u32[]{:S(2)}, u32[]{:S(2)}) collective-permute-start(bf16[96,4608]{1,0:T(8,128)(2,1)} %collective-permute-done.2), channel_id=1, source_target_pairs={{0,4},{4,0},{8,12},{12,8},{1,5},{5,1},{9,13},{13,9},{2,6},{6,2},{1... | collective-permute-start | bytes 2654216 | tf_op jit(solution)/shard_map/ppermute | solution.py:281
  53.1 21.7 %copy-start = (bf16[192,4608]{1,0:T(8,128)(2,1)S(1)}, bf16[192,4608]{1,0:T(8,128)(2,1)}, u32[]{:S(2)}) copy-start(bf16[192,4608]{1,0:T(8,128)(2,1)} %refs_10_.1) | copy-start | bytes 5308420
  60.1 47.3 %collective-permute-start.8 = (bf16[384,256]{1,0:T(8,128)(2,1)}, bf16[384,256]{1,0:T(8,128)(2,1)S(1)}, u32[]{:S(2)}, u32[]{:S(2)}) collective-permute-start(bf16[384,256]{1,0:T(8,128)(2,1)} %get-tuple-element.13), channel_id=1, source_target_pairs={{0,1},{1,2},{2,3},{3,0},{4,5},{5,6},{6,7},{7,4},{8,9},{9,10},{10,1... | collective-permute-start | bytes 589832 | tf_op jit(solution)/shard_map/ppermute | solution.py:286
  61.7 49.2 %collective-permute-start.9 = (bf16[384,256]{1,0:T(8,128)(2,1)}, bf16[384,256]{1,0:T(8,128)(2,1)S(1)}, u32[]{:S(2)}, u32[]{:S(2)}) collective-permute-start(bf16[384,256]{1,0:T(8,128)(2,1)} %get-tuple-element.13), channel_id=1, source_target_pairs={{0,2},{1,3},{2,0},{3,1},{4,6},{5,7},{6,4},{7,5},{8,10},{9,11},{10,... | collective-permute-start | bytes 589832 | tf_op jit(solution)/shard_map/ppermute | solution.py:286
  73.2 27.2 %collective-permute-start.16 = (bf16[128,4608]{1,0:T(8,128)(2,1)}, bf16[128,4608]{1,0:T(8,128)(2,1)}, u32[]{:S(2)}, u32[]{:S(2)}) collective-permute-start(bf16[128,4608]{1,0:T(8,128)(2,1)} %collective-permute-done.15.refs_6_), channel_id=1, source_target_pairs={{0,16},{16,0},{1,17},{17,1},{2,18},{18,2},{3,19},{19,3},{4,20},{20... | collective-permute-start | bytes 3538952 | tf_op jit(solution)/shard_map/ppermute | solution.py:286
  76.8 80.8 %collective-permute-start.17 = (bf16[128,4608]{1,0:T(8,128)(2,1)}, bf16[128,4608]{1,0:T(8,128)(2,1)S(1)}, u32[]{:S(2)}, u32[]{:S(2)}) collective-permute-start(bf16[128,4608]{1,0:T(8,128)(2,1)} %collective-permute-done.15.refs_6_), channel_id=1, source_target_pairs={{0,4},{4,0},{8,12},{12,8},{1,5},{5,1},{9,13},{13,9},{2,6},{6,2},{1... | collective-permute-start | bytes 3538952 | tf_op jit(solution)/shard_map/ppermute | solution.py:281
  100.5 57.1 %collective-permute-start.18 = (bf16[128,4608]{1,0:T(8,128)(2,1)}, bf16[128,4608]{1,0:T(8,128)(2,1)S(1)}, u32[]{:S(2)}, u32[]{:S(2)}) collective-permute-start(bf16[128,4608]{1,0:T(8,128)(2,1)} %collective-permute-done.16.refs_7_), channel_id=1, source_target_pairs={{0,4},{4,0},{8,12},{12,8},{1,5},{5,1},{9,13},{13,9},{2,6},{6,2},{1... | collective-permute-start | bytes 3538952 | tf_op jit(solution)/shard_map/ppermute | solution.py:281
  100.5 7.0 %copy-start.10 = (bf16[384,256]{1,0:T(8,128)(2,1)S(1)}, bf16[384,256]{1,0:T(8,128)(2,1)}, u32[]{:S(2)}) copy-start(bf16[384,256]{1,0:T(8,128)(2,1)} %get-tuple-element.13) | copy-start | bytes 589828
  100.5 29.6 %copy-start.3 = (bf16[384,256]{1,0:T(8,128)(2,1)S(1)}, bf16[384,256]{1,0:T(8,128)(2,1)}, u32[]{:S(2)}) copy-start(bf16[384,256]{1,0:T(8,128)(2,1)} %get-tuple-element.11) | copy-start | bytes 589828
  107.4 29.6 %copy-start.11 = (bf16[384,256]{1,0:T(8,128)(2,1)}, bf16[384,256]{1,0:T(8,128)(2,1)S(1)}, u32[]{:S(2)}) copy-start(bf16[384,256]{1,0:T(8,128)(2,1)S(1)} %collective-permute-done.8) | copy-start | bytes 589828
  107.5 8.7 %collective-permute-start.10 = (bf16[384,256]{1,0:T(8,128)(2,1)S(1)}, bf16[384,256]{1,0:T(8,128)(2,1)S(1)}, u32[]{:S(2)}, u32[]{:S(2)}) collective-permute-start(bf16[384,256]{1,0:T(8,128)(2,1)S(1)} %copy-done.10), channel_id=1, source_target_pairs={{0,3},{1,0},{2,1},{3,2},{4,7},{5,4},{6,5},{7,6},{8,11},{9,8},{10,9... | collective-permute-start | bytes 589832 | tf_op jit(solution)/shard_map/ppermute | solution.py:286
  110.9 26.2 %copy-start.12 = (bf16[384,256]{1,0:T(8,128)(2,1)}, bf16[384,256]{1,0:T(8,128)(2,1)S(1)}, u32[]{:S(2)}) copy-start(bf16[384,256]{1,0:T(8,128)(2,1)S(1)} %collective-permute-done.9) | copy-start | bytes 589828
  110.9 13.7 %collective-permute-start.6 = (bf16[384,256]{1,0:T(8,128)(2,1)}, bf16[384,256]{1,0:T(8,128)(2,1)}, u32[]{:S(2)}, u32[]{:S(2)}) collective-permute-start(bf16[384,256]{1,0:T(8,128)(2,1)} %get-tuple-element.12), channel_id=1, source_target_pairs={{0,2},{1,3},{2,0},{3,1},{4,6},{5,7},{6,4},{7,5},{8,10},{9,11},{10,... | collective-permute-start | bytes 589832 | tf_op jit(solution)/shard_map/ppermute | solution.py:286
  116.2 20.9 %copy-start.13 = (bf16[384,256]{1,0:T(8,128)(2,1)}, bf16[384,256]{1,0:T(8,128)(2,1)S(1)}, u32[]{:S(2)}) copy-start(bf16[384,256]{1,0:T(8,128)(2,1)S(1)} %collective-permute-done.10) | copy-start | bytes 589828
  116.2 15.6 %collective-permute-start.7 = (bf16[384,256]{1,0:T(8,128)(2,1)}, bf16[384,256]{1,0:T(8,128)(2,1)S(1)}, u32[]{:S(2)}, u32[]{:S(2)}) collective-permute-start(bf16[384,256]{1,0:T(8,128)(2,1)} %get-tuple-element.12), channel_id=1, source_target_pairs={{0,3},{1,0},{2,1},{3,2},{4,7},{5,4},{6,5},{7,6},{8,11},{9,8},{10,9... | collective-permute-start | bytes 589832 | tf_op jit(solution)/shard_map/ppermute | solution.py:286
  124.6 12.5 %collective-permute-start.5 = (bf16[384,256]{1,0:T(8,128)(2,1)}, bf16[384,256]{1,0:T(8,128)(2,1)S(1)}, u32[]{:S(2)}, u32[]{:S(2)}) collective-permute-start(bf16[384,256]{1,0:T(8,128)(2,1)} %get-tuple-element.12), channel_id=1, source_target_pairs={{0,1},{1,2},{2,3},{3,0},{4,5},{5,6},{6,7},{7,4},{8,9},{9,10},{10,1... | collective-permute-start | bytes 589832 | tf_op jit(solution)/shard_map/ppermute | solution.py:286
  131.8 5.3 %copy-start.14 = (bf16[384,256]{1,0:T(8,128)(2,1)}, bf16[384,256]{1,0:T(8,128)(2,1)S(1)}, u32[]{:S(2)}) copy-start(bf16[384,256]{1,0:T(8,128)(2,1)S(1)} %collective-permute-done.7) | copy-start | bytes 589828
  137.7 15.5 %copy-start.8 = (f32[4608]{0:T(1024)S(1)}, f32[4608]{0:T(1024)}, u32[]{:S(2)}) copy-start(f32[4608]{0:T(1024)} %param.10) | copy-start | bytes 55300
  150.7 1.5 collective-permute-start.11
  150.7 5.6 %collective-permute-start.12 = (bf16[192,256]{1,0:T(8,128)(2,1)S(1)}, bf16[192,256]{1,0:T(8,128)(2,1)S(1)}, u32[]{:S(2)}, u32[]{:S(2)}) collective-permute-start(bf16[192,256]{1,0:T(8,128)(2,1)S(1)} %get-tuple-element.26), channel_id=1, source_target_pairs={{0,8},{4,12},{8,0},{12,4},{1,9},{5,13},{9,1},{13,5},{2,10},{6,14},... | collective-permute-start | bytes 294920 | tf_op jit(solution)/shard_map/ppermute | solution.py:281
  152.2 5.4 %copy-start.4 = (bf16[192,256]{1,0:T(8,128)(2,1)}, bf16[192,256]{1,0:T(8,128)(2,1)S(1)}, u32[]{:S(2)}) copy-start(bf16[192,256]{1,0:T(8,128)(2,1)S(1)} %collective-permute-done.11.refs_1_) | copy-start | bytes 294916
  152.2 5.4 %collective-permute-start.13 = (bf16[192,256]{1,0:T(8,128)(2,1)S(1)}, bf16[192,256]{1,0:T(8,128)(2,1)S(1)}, u32[]{:S(2)}, u32[]{:S(2)}) collective-permute-start(bf16[192,256]{1,0:T(8,128)(2,1)S(1)} %get-tuple-element.25), channel_id=1, source_target_pairs={{0,12},{4,8},{8,4},{12,0},{1,13},{5,9},{9,5},{13,1},{2,14},{6,10},... | collective-permute-start | bytes 294920 | tf_op jit(solution)/shard_map/ppermute | solution.py:281
  156.3 1.4 copy-start.5
  157.6 1.4 copy-start.2
  (3 other events, 2.4 us)

commit v2 on v0

v2 whole, which is shorter than its diff:
```python
import functools
import math

import jax
import jax.numpy as jnp
from jax import lax
from jax.experimental import pallas as pl
from jax.experimental.pallas import tpu as pltpu
from jax.sharding import PartitionSpec as P

HD = 128
ATT_SCALAR = 144
EPS = 1e-6
MIB = 1024 * 1024
HIDDEN = -1e30

ANY = pl.BlockSpec(memory_space=pl.ANY)
VMEM = pl.BlockSpec(memory_space=pltpu.VMEM)
SMEM = pl.BlockSpec(memory_space=pltpu.SMEM)


def params(mib):
    return pltpu.CompilerParams(vmem_limit_bytes=mib * MIB)


def norm_kernel(hidden, gain, out):
    x = hidden[...].astype(jnp.float32)
    square = x * x
    folded = square[:, :128]
    for lane in range(128, x.shape[1], 128):
        folded = folded + square[:, lane : lane + 128]
    mean = jnp.sum(folded, axis=1, keepdims=True) / x.shape[1]
    out[...] = (x * lax.rsqrt(mean + EPS) * gain[...]).astype(jnp.bfloat16)


def norm(hidden, gain, first, rows):
    width = hidden.shape[1]
    step = math.gcd(math.gcd(first, rows), 64) if first else math.gcd(rows, 64)
    return pl.pallas_call(
        norm_kernel,
        grid=(rows // step,),
        in_specs=[
            pl.BlockSpec((step, width), lambda i: (first // step + i, 0)),
            pl.BlockSpec((1, width), lambda i: (0, 0)),
        ],
        out_specs=pl.BlockSpec((step, width), lambda i: (i, 0)),
        out_shape=jax.ShapeDtypeStruct((rows, width), jnp.bfloat16),
        compiler_params=params(12),
        cost_estimate=pl.CostEstimate(
            flops=6 * rows * width, bytes_accessed=4 * rows * width, transcendentals=0
        ),
        name="norm_rows",
    )(hidden, gain.reshape(1, -1))


def qkv_kernel(parts, heads, *refs):
    parts_refs = refs[:parts]
    weights, cosine, sine, q_out, kv_out, rows, arrived = refs[parts:]
    copies, first = [], 0
    for at, part in enumerate(parts_refs):
        span = pl.ds(first, part.shape[0])
        copies.append(pltpu.make_async_copy(part, rows.at[span], arrived.at[at]))
        first += part.shape[0]
    for copy in copies:
        copy.start()
    for copy in copies:
        copy.wait()
    product = jnp.dot(rows[...], weights[...], preferred_element_type=jnp.float32)
    cos, sin = cosine[...], sine[...]

    def rotated(at):
        y = product[:, at * HD : (at + 1) * HD]
        return y * cos + pltpu.roll(y, HD // 2, 1) * sin

    factor = ATT_SCALAR ** (-0.5) * math.log2(math.e)
    for head in range(heads):
        q_out[head] = (rotated(head) * factor).astype(jnp.bfloat16)
    kv_out[:, :HD] = rotated(heads).astype(jnp.bfloat16)
    kv_out[:, HD:] = product[:, (heads + 1) * HD :].astype(jnp.bfloat16)


def qkv(parts, weights, cosine, sine):
    total = sum(part.shape[0] for part in parts)
    width, columns = weights.shape
    heads = columns // HD - 2
    return pl.pallas_call(
        functools.partial(qkv_kernel, len(parts), heads),
        in_specs=[ANY] * len(parts) + [VMEM] * 3,
        out_specs=[VMEM, VMEM],
        out_shape=[
            jax.ShapeDtypeStruct((heads, total, HD), jnp.bfloat16),
            jax.ShapeDtypeStruct((total, 2 * HD), jnp.bfloat16),
        ],
        scratch_shapes=[
            pltpu.VMEM((total, width), jnp.bfloat16),
            pltpu.SemaphoreType.DMA((len(parts),)),
        ],
        compiler_params=params(24),
        cost_estimate=pl.CostEstimate(
            flops=2 * total * width * columns,
            bytes_accessed=2 * width * (total + columns),
            transcendentals=0,
        ),
        name="qkv",
    )(*parts, weights, cosine, sine)


class Step:
    def __init__(self, q, group, slots, same=None, merged=False):
        self.q, self.group, self.slots = q, group, slots
        self.same, self.merged = same, merged


def attention_kernel(plan, fresh, final, sizes, *refs):
    q_count, group_parts = sizes
    refs = list(refs)
    take = lambda n: [refs.pop(0) for _ in range(n)]
    q_starts, k_starts = take(2)
    q_refs = take(q_count)
    q_places = take(q_count)
    k_places = take(len(group_parts))
    kv_parts = [take(n) for n in group_parts]
    old = {q: take(2) for q in range(q_count) if q not in fresh}
    outs = take(len(final)) if final else None
    new = [take(2) for _ in range(q_count)]
    kvs = take(len(group_parts))
    (arrived,) = refs
    copies, at = [], 0
    for parts, kv in zip(kv_parts, kvs):
        for slot, part in enumerate(parts):
            each = kv.shape[0] // len(parts)
            copies.append(
                pltpu.make_async_copy(part, kv.at[pl.ds(slot * each, each)], arrived.at[at])
            )
            at += 1
    for copy in copies:
        copy.start()
    for q, (peak, acc) in old.items():
        new[q][0][...] = peak[...]
        new[q][1][...] = acc[...]
    for copy in copies:
        copy.wait()
    offsets, total = [], 0
    for parts, kv in zip(kv_parts, kvs):
        offsets.append(total)
        total += kv.shape[0]

    def attend(q, keys_values, begin, visible=None, bias=None):
        q_ref, (peak, acc) = q_refs[q], new[q]
        heads, rows, _ = q_ref.shape
        keys, values = keys_values[:, :HD], keys_values[:, HD:]
        values = jnp.concatenate([values, jnp.ones_like(values)], axis=1)
        count = keys.shape[0]
        tile = min(rows, 128)
        for first in range(0, rows, tile):
            q_tile = q_ref[:, first : first + tile, :].reshape(heads * tile, HD)
            scores = lax.dot_general(
                q_tile, keys, (((1,), (1,)), ((), ())), preferred_element_type=jnp.float32
            )
            if visible is not None:
                seen = visible(first, tile)
                seen = jnp.concatenate([seen] * heads, axis=0)
                scores = jnp.where(seen, scores, HIDDEN)
            if bias is not None:
                scores = scores + bias
            top = jnp.max(scores, axis=1, keepdims=True)
            top = jnp.broadcast_to(top, (heads * tile, HD))
            span = pl.ds(first * heads, heads * tile)
            if not begin:
                before = peak[span, :]
                top = jnp.maximum(before, top)
            wide = jnp.concatenate([top] * (count // HD), axis=1)
            weights = jnp.exp2(scores - wide).astype(jnp.bfloat16)
            summed = jnp.dot(weights, values, preferred_element_type=jnp.float32)
            if not begin:
                fade = jnp.exp2(before - top)
                summed = summed + acc[span, :] * jnp.concatenate([fade, fade], axis=1)
            acc[span, :] = summed
            peak[span, :] = top

    begun = set(range(q_count)) - set(fresh)
    for step in plan:
        q, group, kv = step.q, step.group, kvs[step.group]
        base = offsets[group]
        if step.same is not None:
            q_place, k_place = q_places[q], k_places[group]
            visible = lambda first, tile: k_place[...] <= q_place[first : first + tile, :]
            attend(q, kv[step.same], q not in begun, visible=visible)
            begun.add(q)
        start = q_starts[q]
        slots = step.slots
        if not slots:
            continue
        if step.merged:
            count = kv.shape[1]
            shown = [k_starts[base + slot] < start for slot in slots]
            anything = functools.reduce(jnp.logical_or, shown)

            @pl.when(anything)
            def _():
                bias = [
                    jnp.where(see, 0.0, HIDDEN) * jnp.ones((1, count), jnp.float32)
                    for see in shown
                ]
                keys_values = kv[slots[0] : slots[-1] + 1].reshape(len(slots) * count, 2 * HD)
                attend(q, keys_values, False, bias=jnp.concatenate(bias, axis=1))

        else:

            def one(slot, carry):
                @pl.when(k_starts[base + slot] < start)
                def _():
                    attend(q, kv[slot], False)

                return carry

            lax.fori_loop(slots[0], slots[-1] + 1, one, 0)

    if final:
        for out, spans in zip(outs, final):
            put = 0
            for q, first, rows in spans:
                acc = new[q][1]
                heads, q_rows, _ = q_refs[q].shape
                tile = min(q_rows, 128)
                for head in range(heads):
                    for at in range(first, first + rows, min(tile, rows)):
                        size = min(tile, rows)
                        from_row = at // tile * tile * heads + head * tile + at % tile
                        part = acc[from_row : from_row + size, :]
                        out[
                            put + at - first : put + at - first + size,
                            head * HD : (head + 1) * HD,
                        ] = (part[:, :HD] / part[:, HD:]).astype(jnp.bfloat16)
                put += rows


def attention(plan, qs, q_starts, q_places, groups, k_starts, k_places, state, final=None):
    fresh = [at for at, held in enumerate(state) if held is None]
    held = [array for pair in state if pair is not None for array in pair]
    shapes = []
    for q in qs:
        heads, rows, _ = q.shape
        shapes += [(heads * rows, HD), (heads * rows, 2 * HD)]
    states = [jax.ShapeDtypeStruct(shape, jnp.float32) for shape in shapes]
    if final:
        width = qs[0].shape[0] * HD
        out_shape = [
            jax.ShapeDtypeStruct((sum(rows for _, _, rows in spans), width), jnp.bfloat16)
            for spans in final
        ]
        scratch = [pltpu.VMEM(shape, jnp.float32) for shape in shapes]
    else:
        out_shape, scratch = states, []
    buffers = [
        pltpu.VMEM((sum(p.shape[0] for p in parts),) + parts[0].shape[1:], jnp.bfloat16)
        for parts in groups
    ]
    parts = [part for parts in groups for part in parts]
    work = 0
    for step in plan:
        slots = len(step.slots) + (step.same is not None)
        work += qs[step.q].size // HD * groups[step.group][0].shape[1] * slots
    sizes = (len(qs), [len(parts) for parts in groups])
    results = pl.pallas_call(
        functools.partial(attention_kernel, plan, fresh, final, sizes),
        in_specs=[SMEM] * 2
        + [VMEM] * (2 * len(qs) + len(groups))
        + [ANY] * len(parts)
        + [VMEM] * len(held),
        out_specs=[VMEM] * len(out_shape),
        out_shape=out_shape,
        scratch_shapes=scratch + buffers + [pltpu.SemaphoreType.DMA((len(parts),))],
        compiler_params=params(20),
        cost_estimate=pl.CostEstimate(
            flops=4 * work * HD, bytes_accessed=2 * work // HD, transcendentals=work
        ),
        name="attention",
    )(q_starts, k_starts, *qs, *q_places, *k_places, *parts, *held)
    if final:
        return results
    return [tuple(results[2 * at : 2 * at + 2]) for at in range(len(qs))]


def output_kernel(pieces, chunks, at, *refs):
    attended = refs[:4]
    weights = refs[4 : 4 + len(pieces)]
    hidden, gain, out, projected = refs[4 + len(pieces) :]
    width = hidden.shape[1]
    step = width // chunks
    lefts = []
    for index, (part, piece) in enumerate(zip(pieces, weights)):
        depth = piece.shape[0]
        if depth == attended[part].shape[1]:
            lefts.append(attended[part][...])
        else:
            lefts.append(attended[part][:, pl.ds(pl.multiple_of(at[index], HD), depth)])
    square = jnp.zeros((hidden.shape[0], 128), jnp.float32)
    for chunk in range(chunks):
        lanes = slice(chunk * step, chunk * step + step)
        total = jnp.dot(lefts[0], weights[0][:, lanes], preferred_element_type=jnp.float32)
        for left, piece in zip(lefts[1:], weights[1:]):
            total = total + jnp.dot(left, piece[:, lanes], preferred_element_type=jnp.float32)
        projected[:, lanes] = total
        for lane in range(0, step, 128):
            piece = total[:, lane : lane + 128]
            square = square + piece * piece
    mean = jnp.sum(square, axis=1, keepdims=True) / width
    scale = lax.rsqrt(mean + EPS)
    for chunk in range(chunks):
        lanes = slice(chunk * step, chunk * step + step)
        normed = projected[:, lanes] * scale * gain[:, lanes]
        out[:, lanes] = (hidden[:, lanes].astype(jnp.float32) + normed).astype(jnp.bfloat16)


def output(attended, pieces, weights, places, hidden, gain):
    rows, width = hidden.shape
    depth = sum(piece.shape[0] for piece in weights)
    return pl.pallas_call(
        functools.partial(output_kernel, pieces, 6),
        in_specs=[SMEM] + [VMEM] * (4 + len(weights) + 2),
        out_specs=VMEM,
        out_shape=jax.ShapeDtypeStruct(hidden.shape, jnp.bfloat16),
        scratch_shapes=[pltpu.VMEM((rows, width), jnp.float32)],
        compiler_params=params(26),
        cost_estimate=pl.CostEstimate(
            flops=2 * rows * width * depth,
            bytes_accessed=2 * width * (depth + 2 * rows),
            transcendentals=0,
        ),
        name="output_norm",
    )(places, *attended, *weights, hidden, gain.reshape(1, -1))


def rotary_tables(positions):
    half = HD // 2
    frequency = jnp.power(
        jnp.float32(10000.0), -jnp.arange(half, dtype=jnp.float32) * (2.0 / HD)
    )
    angles = positions.astype(jnp.float32)[:, None] * frequency[None, :]
    cos, sin = jnp.cos(angles), jnp.sin(angles)
    return jnp.concatenate([cos, cos], axis=1), jnp.concatenate([-sin, sin], axis=1)


def lookup(block_of, index):
    ids = jnp.arange(block_of.shape[0], dtype=jnp.int32)
    return jnp.sum(jnp.where(index[..., None] == ids, block_of, 0), axis=-1)


def flipped(array, axis, bit):
    size = lax.axis_size(axis)
    return lax.ppermute(array, axis, [(i, i ^ bit) for i in range(size)])


def shifted(array, axis, by):
    size = lax.axis_size(axis)
    return lax.ppermute(array, axis, [(i, (i + by) % size) for i in range(size)])


def after(array, *others):
    return lax.optimization_barrier((array, *others))[0]


def two_chips(hidden, pre_gain, post_gain, wq, wk, wv, w_out, block_of):
    rows = hidden.shape[0]
    block_rows = 2 * rows
    cuts = [rows * 2 // 3, rows - rows * 2 // 3]
    lines, group_count = lax.axis_size("seq"), lax.axis_size("groups")
    seq, tp, group = lax.axis_index("seq"), lax.axis_index("tp"), lax.axis_index("groups")
    chip, core = tp // 2, tp % 2

    line = (seq - jnp.arange(lines, dtype=jnp.int32)) % lines
    near_starts = lookup(block_of, 2 * line + chip) * block_rows
    far_starts = lookup(block_of, 2 * line + 1 - chip) * block_rows
    place = []
    for first, size in zip((0, cuts[0]), cuts):
        run = first + jnp.arange(size, dtype=jnp.int32)
        place += [core * rows + run, (1 - core) * rows + run]
    place = jnp.concatenate(place)
    cosine, sine = rotary_tables(
        jnp.concatenate([near_starts[0] + place, far_starts[0] + place])
    )
    first, last = 2 * cuts[0], block_rows

    own = [norm(hidden, pre_gain, 0, cuts[0]), norm(hidden, pre_gain, cuts[0], cuts[1])]
    away = [flipped(chunk, "tp", 2) for chunk in own]
    partner = [flipped(chunk, "tp", 1) for chunk in own]
    weights = jnp.concatenate([wq, wk, wv], axis=1)

    q_near, kv_near = qkv(
        [own[0], partner[0], own[1], partner[1]],
        weights,
        cosine[:block_rows],
        sine[:block_rows],
    )
    near = [kv_near] + [shifted(kv_near, "seq", by) for by in range(1, lines)]
    near = [part[None] for part in near]
    column, row = place[:, None], place[None, :]
    head, tail = slice(0, first), slice(first, last)
    others = list(range(1, lines))
    (near_state,) = attention(
        [Step(0, 0, others, same=0)],
        [q_near],
        near_starts[:1],
        [column],
        [near],
        near_starts,
        [row],
        [None],
    )

    def project(chunk, span):
        other = flipped(chunk, "tp", 1)
        at = slice(block_rows + span.start, block_rows + span.stop)
        return qkv([chunk, other], weights, cosine[at], sine[at])

    away[0] = after(away[0], *near_state)
    q_head, kv_head = project(away[0], head)
    far_head = [kv_head] + [shifted(kv_head, "seq", by) for by in range(1, lines)]
    far_head = [part[None] for part in far_head]

    half = w_out.shape[0] // group_count
    sent = lax.dynamic_slice_in_dim(w_out, group * half, half, axis=0)
    sent = after(sent, kv_head)
    w_far = [flipped(sent, "tp", 2)]
    w_far += [shifted(w_far[0], "groups", by) for by in range(1, group_count)]
    w_partner = flipped(after(w_out, kv_near), "tp", 1)
    w_cross = [flipped(piece, "tp", 1) for piece in w_far]

    away[1] = after(away[1], kv_head)
    q_tail, kv_tail = project(away[1], tail)
    far_tail = [kv_tail] + [shifted(kv_tail, "seq", by) for by in range(1, lines)]
    far_tail = [part[None] for part in far_tail]

    q_starts = jnp.stack([near_starts[0], far_starts[0], far_starts[0]])
    qs = [q_near, q_head, q_tail]
    q_places = [column, column[head], column[tail]]
    everyone = list(range(lines))
    state = attention(
        [
            Step(1, 1, others, same=0),
            Step(2, 2, [], same=0),
            Step(0, 1, everyone),
            Step(1, 0, everyone),
            Step(2, 0, everyone),
            Step(2, 1, others, same=0),
        ],
        qs,
        q_starts,
        q_places,
        [near, far_head, far_tail[:1]],
        jnp.concatenate([near_starts, far_starts, far_starts[:1]]),
        [row, row[:, head], row[:, tail]],
        [near_state, None, None],
    )
    to = lambda half: [(0, half * cuts[0], cuts[0]), (0, first + half * cuts[1], cuts[1])]
    over = lambda half: [(1, half * cuts[0], cuts[0]), (2, half * cuts[1], cuts[1])]
    mine, partners, same, cross = attention(
        [
            Step(1, 0, others, same=0, merged=True),
            Step(2, 0, others, merged=True),
            Step(0, 0, everyone, merged=True),
        ],
        qs,
        q_starts,
        q_places,
        [far_tail],
        far_starts,
        [row[:, tail]],
        state,
        final=[to(0), to(1), over(0), over(1)],
    )
    gathered = [
        mine,
        flipped(partners, "tp", 1),
        flipped(same, "tp", 2),
        flipped(cross, "tp", 3),
    ]
    order = [(group - by) % group_count * half for by in range(group_count)]
    places = jnp.stack([jnp.asarray(at, jnp.int32) for at in [0, 0] + order + order])
    pieces = [0, 1] + [2] * group_count + [3] * group_count
    return output(
        gathered, pieces, [w_out, w_partner] + w_far + w_cross, places, hidden, post_gain
    )


def any_count(hidden, pre_gain, post_gain, wq, wk, wv, w_out, block_of):
    normed = norm(hidden, pre_gain, 0, hidden.shape[0])
    normed = lax.all_gather(normed, "tp", axis=0, tiled=True)
    seq_rows = normed.shape[0]
    block_rows = seq_rows // 2
    lines = lax.axis_size("seq")
    place = jnp.arange(block_rows, dtype=jnp.int32)
    line = (lax.axis_index("seq") - jnp.arange(lines, dtype=jnp.int32)) % lines
    block = (2 * line[:, None] + jnp.arange(2, dtype=jnp.int32)).reshape(-1)
    starts = lookup(block_of, block) * block_rows
    cosine, sine = rotary_tables((starts[:2, None] + place).reshape(-1))
    weights = jnp.concatenate([wq, wk, wv], axis=1)
    qs, keys_values = [], []
    for at in range(2):
        span = slice(at * block_rows, (at + 1) * block_rows)
        q, kv = qkv([normed[span]], weights, cosine[span], sine[span])
        qs.append(q)
        keys_values.append(kv)
    kv = lax.all_gather(jnp.stack(keys_values), "seq")[line].reshape(-1, block_rows, 2 * HD)
    rest = list(range(2, 2 * lines))
    attended = attention(
        [
            Step(0, 0, [1], same=0),
            Step(1, 0, [0], same=1),
            Step(0, 0, rest),
            Step(1, 0, rest),
        ],
        qs,
        starts[:2],
        [place[:, None]] * 2,
        [[kv]],
        starts,
        [place[None, :]],
        [None, None],
        final=[[(0, 0, block_rows), (1, 0, block_rows)]],
    )[0]
    partial = jnp.dot(attended, w_out, preferred_element_type=jnp.float32)
    summed = lax.psum_scatter(
        partial.astype(jnp.bfloat16), "tp", scatter_dimension=0, tiled=True
    ).astype(jnp.float32)
    mean = jnp.mean(summed * summed, axis=-1, keepdims=True)
    projected = summed * lax.rsqrt(mean + EPS) * post_gain
    return (hidden.astype(jnp.float32) + projected).astype(jnp.bfloat16)


def solution(mesh):
    return jax.shard_map(
        two_chips if mesh.shape["tp"] == 4 else any_count,
        mesh=mesh,
        in_specs=(
            P(("groups", "seq", "tp"), None),
            P(),
            P(),
            P(None, "tp"),
            P(None, "tp"),
            P(None, "tp"),
            P("tp", None),
            P(),
        ),
        out_specs=P(("groups", "seq", "tp"), None),
        check_vma=False,
    )
```

time: 273 us -> 169 us (0.62)
  matrix products: 67.3 us -> 0 us
  blocking collectives: 38.7 us -> 0 us
  Pallas kernels: 0 us -> 37.5 us
  waiting for transfers between devices: 113 us -> 77.8 us
  starting transfers between devices: 0.04 us -> 29.9 us
  other arithmetic: 22.2 us -> 6.74 us
  between operations: 13.6 us -> 0.55 us
  loops' own time: 5.53 us -> 0 us
  local copies, waits for them, and re-layouts: 11.8 us -> 16 us
    ppermute x0 -> x23, waiting for transfers between devices: none -> 77.8 us  [the longest x10 45.5 us: shifted(): lax.ppermute(array, axis, [(i, (i + by) % size) for i in range(size)])]
    dot_general x20 -> x0, matrix products: 67.3 us -> none  [the longest x8 24 us: update(): jnp.einsum('qhd,kd->hqk', queries, keys_block, preferred_element_type=jnp...]
    reduce_scatter x1 -> x0, waiting for transfers between devices: 62.6 us -> none  [body(): lax.psum_scatter(jnp.dot(attended, w_out, preferred_element_type=jnp.floa...]
    all_gather x1 -> x0, waiting for transfers between devices: 50.4 us -> none  [body(): normed = lax.all_gather(normed_local, 'tp', axis=0, tiled=True)]
    all_gather x2 -> x0, blocking collectives: 38.7 us -> none  [the longest x1 19.9 us: body(): lax.all_gather(keys_local, 'seq', axis=0, tiled=True)]
    pallas_call x0 -> x9, Pallas kernels: none -> 37.5 us  [the longest x3 19.8 us: attention(): pl.pallas_call(functools.partial(attention_kernel, plan, fresh, final, si...]
    ppermute x0 -> x23, starting transfers between devices: none -> 29.9 us  [the longest x10 21.2 us: shifted(): lax.ppermute(array, axis, [(i, (i + by) % size) for i in range(size)])]
    reduce_sum x19 -> x1, other arithmetic: 8.76 us -> 0.87 us  [lookup(): return jnp.sum(jnp.where(index[..., None] == ids, block_of, 0), axis=-1)]
  transfers between devices with their start and end apart: 2 -> 23, of which waited for: 2 -> 9; matrix products, arithmetic and copies ran while one was open for 1% -> 7% of each run, Pallas kernels for 0% -> 15%
where the time goes in v2:
time: 169 us
  waiting for transfers between devices  77.8 us (46%)
  Pallas kernels  37.5 us (22%)
  starting transfers between devices  29.9 us (18%)
  local copies, waits for them, and re-layouts  16 us (9%)
  other arithmetic  6.74 us (4%)
    ppermute x10, waiting for transfers between devices, shifted(): lax.ppermute(array, axis, [(i, (i + by) % size) for i in range(size)])  45.5 us
    ppermute x13, waiting for transfers between devices, flipped(): return lax.ppermute(array, axis, [(i, i ^ bit) for i in range(size)])  32.2 us
    ppermute x10, starting transfers between devices, shifted(): lax.ppermute(array, axis, [(i, (i + by) % size) for i in range(size)])  21.2 us
    pallas_call x3, Pallas kernels, attention(): pl.pallas_call(functools.partial(attention_kernel, plan, fresh, final, si...  19.8 us
    unnamed x70, local copies, waits for them, and re-layouts  13.2 us
    ppermute x13, starting transfers between devices, flipped(): return lax.ppermute(array, axis, [(i, i ^ bit) for i in range(size)])  8.72 us
    pallas_call x1, Pallas kernels, output(): pl.pallas_call(functools.partial(output_kernel, pieces, 6), in_specs=[SME...  8.39 us
    pallas_call x3, Pallas kernels, qkv(): pl.pallas_call(functools.partial(qkv_kernel, len(parts), heads), in_specs...  8.32 us
  transfers between devices with their start and end apart: 23, of which 9 were waited for; matrix products, arithmetic and copies ran while one was open for 7% of the time, Pallas kernels for 15%

profile of v2, /device:TPU:0, one launch (start us, length us, event | category | flops | bytes accessed | tf_op | source)
XLA Modules:
  0.0 168.6 jit_solution(6760287279283392518)
XLA Ops:
  0.8 1.5 copy-done.3
  3.4 2.6 %collective-permute-start.2 = (bf16[128,4608]{1,0:T(8,128)(2,1)S(1)}, bf16[128,4608]{1,0:T(8,128)(2,1)S(1)}, u32[]{:S(2)}, u32[]{:S(2)}) collective-permute-start(bf16[128,4608]{1,0:T(8,128)(2,1)S(1)} %norm_rows.2.refs_0_), channel_id=1, source_target_pairs={{0,8},{4,12},{8,0},{12,4},{1,9},{5,13},{9,1},{13,5},{2,10},{6,14},... | collective-permute-start | bytes 3538952 | tf_op jit(solution)/shard_map/ppermute | solution.py:352
  8.0 1.9 %constant_dynamic-update-slice_fusion.2 = bf16[4608,512]{1,0:T(8,128)(2,1)S(1)} fusion(bf16[4608,256]{1,0:T(8,128)(2,1)} %param.11), kind=kLoop, calls=%fused_computation.19 | loop fusion | bytes 4718592
  10.8 1.5 multiply_sine_fusion
  13.5 4.6 %qkv.3 = (bf16[2,384,128]{2,1,0:T(8,128)(2,1)S(1)}, bf16[384,256]{1,0:T(8,128)(2,1)S(1)}) custom-call(bf16[128,4608]{1,0:T(8,128)(2,1)S(1)} %norm_rows.2.refs_0_, bf16[128,4608]{1,0:T(8,128)(2,1)} %collective-permute-done.refs_1_, bf16[64,4608]{1,0:T(8,128)(2,1)S(1)} %norm_rows.3.refs_2_, bf16[64,4608]{1,0:T(8,128)(2,1)S(1)} %collective-permute-done.1.refs_3_, ...), custom_call_target="tpu_custom_call" | custom-call | flops 1811939328 | bytes 8257536 | tf_op jit(solution)/shard_map/qkv/pallas_call | solution.py:86
  18.1 1.6 collective-permute-start.3
  19.7 2.6 %collective-permute-start.4 = (bf16[384,256]{1,0:T(8,128)(2,1)S(1)}, bf16[384,256]{1,0:T(8,128)(2,1)S(1)}, u32[]{:S(2)}, u32[]{:S(2)}) collective-permute-start(bf16[384,256]{1,0:T(8,128)(2,1)S(1)} %get-tuple-element.28), channel_id=1, source_target_pairs={{0,2},{1,3},{2,0},{3,1},{4,6},{5,7},{6,4},{7,5},{8,10},{9,11},{10,... | collective-permute-start | bytes 589832 | tf_op jit(solution)/shard_map/ppermute | solution.py:357
  22.3 1.3 collective-permute-start.5
  23.8 4.0 %collective-permute-done.3 = bf16[384,256]{1,0:T(8,128)(2,1)S(1)} collective-permute-done((bf16[384,256]{1,0:T(8,128)(2,1)S(1)}, bf16[384,256]{1,0:T(8,128)(2,1)S(1)}, u32[]{:S(2)}, u32[]{:S(2)}) %collective-permute-start.3) | collective-permute-done | bytes 196640 | tf_op jit(solution)/shard_map/ppermute | solution.py:357
  27.8 7.9 %collective-permute-done.4 = bf16[384,256]{1,0:T(8,128)(2,1)S(1)} collective-permute-done((bf16[384,256]{1,0:T(8,128)(2,1)S(1)}, bf16[384,256]{1,0:T(8,128)(2,1)S(1)}, u32[]{:S(2)}, u32[]{:S(2)}) %collective-permute-start.4) | collective-permute-done | bytes 196640 | tf_op jit(solution)/shard_map/ppermute | solution.py:357
  35.7 5.5 %attention.3 = (f32[768,128]{1,0:T(8,128)S(1)}, f32[768,256]{1,0:T(8,128)S(1)}) custom-call(s32[1]{0:T(128)S(1)} %bitcast.30, s32[4]{0:T(128)S(1)} %broadcast_multiply_fusion.1.refs_1_, bf16[2,384,128]{2,1,0:T(8,128)(2,1)S(1)} %get-tuple-element.27.refs_2_, s32[384,1]{1,0:T(8,128)S(1)} %broadcast_in_dim.74.refs_3_.refs_5_, ...), custom_call_target="tpu_custom_call" | custom-call | flops 603979776 | bytes 18432 | tf_op jit(solution)/shard_map/attention/pallas_call | solution.py:265
  45.2 1.4 constant_dynamic-slice_fusion
  46.5 2.3 %copy-done.1 = bf16[4608,512]{1,0:T(8,128)(2,1)S(1)} copy-done((bf16[4608,512]{1,0:T(8,128)(2,1)S(1)}, bf16[4608,512]{1,0:T(8,128)(2,1)}, u32[]{:S(2)}) %copy-start.1) | copy-done | bytes 4718616
  48.9 2.6 %qkv.4 = (bf16[2,256,128]{2,1,0:T(8,128)(2,1)S(1)}, bf16[256,256]{1,0:T(8,128)(2,1)}) custom-call(bf16[128,4608]{1,0:T(8,128)(2,1)S(1)} %collective-permute-done.2.refs_0_, bf16[128,4608]{1,0:T(8,128)(2,1)S(1)} %collective-permute-done.6.refs_1_, bf16[4608,512]{1,0:T(8,128)(2,1)S(1)} %copy-done.1, f32[256,128]{1,0:T(8,128)S(1)} %fusion.3.refs_3_, ...), custom_call_target="tpu_custom_call" | custom-call | flops 1207959552 | bytes 7077888 | tf_op jit(solution)/shard_map/qkv/pallas_call | solution.py:86
  52.1 27.8 %collective-permute-done.19.refs_6_ = bf16[128,4608]{1,0:T(8,128)(2,1)S(1)} collective-permute-done((bf16[128,4608]{1,0:T(8,128)(2,1)S(1)}, bf16[128,4608]{1,0:T(8,128)(2,1)S(1)}, u32[]{:S(2)}, u32[]{:S(2)}) %collective-permute-start.19) | collective-permute-done | bytes 1179680 | tf_op jit(solution)/shard_map/ppermute | solution.py:352
  79.9 1.5 collective-permute-start.20
  81.7 25.9 %collective-permute-done.20.refs_7_ = bf16[128,4608]{1,0:T(8,128)(2,1)} collective-permute-done((bf16[128,4608]{1,0:T(8,128)(2,1)S(1)}, bf16[128,4608]{1,0:T(8,128)(2,1)}, u32[]{:S(2)}, u32[]{:S(2)}) %collective-permute-start.20) | collective-permute-done | bytes 1179680 | tf_op jit(solution)/shard_map/ppermute | solution.py:357
  108.2 3.8 %collective-permute-start.12 = (bf16[256,256]{1,0:T(8,128)(2,1)}, bf16[256,256]{1,0:T(8,128)(2,1)S(1)}, u32[]{:S(2)}, u32[]{:S(2)}) collective-permute-start(bf16[256,256]{1,0:T(8,128)(2,1)} %get-tuple-element.33), channel_id=1, source_target_pairs={{0,1},{1,2},{2,3},{3,0},{4,5},{5,6},{6,7},{7,4},{8,9},{9,10},{10,1... | collective-permute-start | bytes 393224 | tf_op jit(solution)/shard_map/ppermute | solution.py:357
  113.3 3.5 %collective-permute-done.12 = bf16[256,256]{1,0:T(8,128)(2,1)S(1)} collective-permute-done((bf16[256,256]{1,0:T(8,128)(2,1)}, bf16[256,256]{1,0:T(8,128)(2,1)S(1)}, u32[]{:S(2)}, u32[]{:S(2)}) %collective-permute-start.12) | collective-permute-done | bytes 131104 | tf_op jit(solution)/shard_map/ppermute | solution.py:357
  118.1 2.6 %collective-permute-start.14 = (bf16[256,256]{1,0:T(8,128)(2,1)}, bf16[256,256]{1,0:T(8,128)(2,1)S(1)}, u32[]{:S(2)}, u32[]{:S(2)}) collective-permute-start(bf16[256,256]{1,0:T(8,128)(2,1)} %get-tuple-element.33), channel_id=1, source_target_pairs={{0,3},{1,0},{2,1},{3,2},{4,7},{5,4},{6,5},{7,6},{8,11},{9,8},{10,9... | collective-permute-start | bytes 393224 | tf_op jit(solution)/shard_map/ppermute | solution.py:357
  120.8 2.3 %copy-done.2 = bf16[4608,512]{1,0:T(8,128)(2,1)S(1)} copy-done((bf16[4608,512]{1,0:T(8,128)(2,1)S(1)}, bf16[4608,512]{1,0:T(8,128)(2,1)}, u32[]{:S(2)}) %copy-start.2) | copy-done | bytes 4718616
  124.3 2.1 %collective-permute-done.13 = bf16[256,256]{1,0:T(8,128)(2,1)S(1)} collective-permute-done((bf16[256,256]{1,0:T(8,128)(2,1)}, bf16[256,256]{1,0:T(8,128)(2,1)S(1)}, u32[]{:S(2)}, u32[]{:S(2)}) %collective-permute-start.13) | collective-permute-done | bytes 131104 | tf_op jit(solution)/shard_map/ppermute | solution.py:357
  126.4 1.4 collective-permute-start.9
  127.9 3.3 %collective-permute-start.10 = (bf16[128,256]{1,0:T(8,128)(2,1)S(1)}, bf16[128,256]{1,0:T(8,128)(2,1)S(1)}, u32[]{:S(2)}, u32[]{:S(2)}) collective-permute-start(bf16[128,256]{1,0:T(8,128)(2,1)S(1)} %get-tuple-element.36), channel_id=1, source_target_pairs={{0,2},{1,3},{2,0},{3,1},{4,6},{5,7},{6,4},{7,5},{8,10},{9,11},{10,... | collective-permute-start | bytes 196616 | tf_op jit(solution)/shard_map/ppermute | solution.py:357
  131.2 2.0 %collective-permute-done.9 = bf16[128,256]{1,0:T(8,128)(2,1)S(1)} collective-permute-done((bf16[128,256]{1,0:T(8,128)(2,1)S(1)}, bf16[128,256]{1,0:T(8,128)(2,1)S(1)}, u32[]{:S(2)}, u32[]{:S(2)}) %collective-permute-start.9) | collective-permute-done | bytes 65568 | tf_op jit(solution)/shard_map/ppermute | solution.py:357
  133.2 2.6 %collective-permute-start.11 = (bf16[128,256]{1,0:T(8,128)(2,1)S(1)}, bf16[128,256]{1,0:T(8,128)(2,1)S(1)}, u32[]{:S(2)}, u32[]{:S(2)}) collective-permute-start(bf16[128,256]{1,0:T(8,128)(2,1)S(1)} %get-tuple-element.36), channel_id=1, source_target_pairs={{0,3},{1,0},{2,1},{3,2},{4,7},{5,4},{6,5},{7,6},{8,11},{9,8},{10,9... | collective-permute-start | bytes 196616 | tf_op jit(solution)/shard_map/ppermute | solution.py:357
  135.9 10.0 %attention.4 = (f32[768,128]{1,0:T(8,128)S(1)}, f32[768,256]{1,0:T(8,128)S(1)}, f32[512,128]{1,0:T(8,128)S(1)}, f32[512,256]{1,0:T(8,128)S(1)}, f32[256,128]{1,0:T(8,128)S(1)}, /*index=5*/f32[256,256]{1,0:T(8,128)S(1)}) custom-call(s32[3]{0:T(128)S(1)} %pad_add_fusion.2.refs_0_, s32[9]{0:T(128)S(1)} %pad_add_fusion.3.refs_1_, ...), custom_call_target="tpu_custom_call" | custom-call | flops 1426063360 | bytes 43520 | tf_op jit(solution)/shard_map/attention/pallas_call | solution.py:265
  145.9 4.3 %attention.5 = (bf16[192,256]{1,0:T(8,128)(2,1)S(1)}, bf16[192,256]{1,0:T(8,128)(2,1)S(1)}, bf16[192,256]{1,0:T(8,128)(2,1)}, bf16[192,256]{1,0:T(8,128)(2,1)}) custom-call(s32[3]{0:T(128)S(1)} %pad_add_fusion.2.refs_0_, s32[4]{0:T(128)S(1)} %broadcast_multiply_fusion.refs_1_, bf16[2,384,128]{2,1,0:T(8,128)(2,1)S(1)} %copy-done.6, ...), custom_call_target="tpu_custom_call" | custom-call | flops 385875968 | bytes 11776 | tf_op jit(solution)/shard_map/attention/pallas_call | solution.py:265
  150.9 2.8 %collective-permute-start.16 = (bf16[192,256]{1,0:T(8,128)(2,1)}, bf16[192,256]{1,0:T(8,128)(2,1)S(1)}, u32[]{:S(2)}, u32[]{:S(2)}) collective-permute-start(bf16[192,256]{1,0:T(8,128)(2,1)} %get-tuple-element.45), channel_id=1, source_target_pairs={{0,8},{4,12},{8,0},{12,4},{1,9},{5,13},{9,1},{13,5},{2,10},{6,14},... | collective-permute-start | bytes 294920 | tf_op jit(solution)/shard_map/ppermute | solution.py:352
  154.9 2.7 %collective-permute-done.16.refs_2_ = bf16[192,256]{1,0:T(8,128)(2,1)S(1)} collective-permute-done((bf16[192,256]{1,0:T(8,128)(2,1)}, bf16[192,256]{1,0:T(8,128)(2,1)S(1)}, u32[]{:S(2)}, u32[]{:S(2)}) %collective-permute-start.16) | collective-permute-done | bytes 98336 | tf_op jit(solution)/shard_map/ppermute | solution.py:352
  157.5 1.7 %collective-permute-done.17.refs_3_ = bf16[192,256]{1,0:T(8,128)(2,1)S(1)} collective-permute-done((bf16[192,256]{1,0:T(8,128)(2,1)}, bf16[192,256]{1,0:T(8,128)(2,1)S(1)}, u32[]{:S(2)}, u32[]{:S(2)}) %collective-permute-start.17) | collective-permute-done | bytes 98336 | tf_op jit(solution)/shard_map/ppermute | solution.py:352
  160.2 8.4 %output_norm.1 = bf16[192,4608]{1,0:T(8,128)(2,1)} custom-call(s32[6]{0:T(128)S(1)} %stack.16.at, bf16[192,256]{1,0:T(8,128)(2,1)S(1)} %copy-done.8, bf16[192,256]{1,0:T(8,128)(2,1)S(1)} %collective-permute-done.15.refs_1_, bf16[192,256]{1,0:T(8,128)(2,1)S(1)} %collective-permute-done.16.refs_2_, bf16[192,256]{1,0:T(8,128)(2,1)S(1)} %collective-permute-done.17.refs_3_, ...), custom_call_target="tpu_custom_call" | custom-call | flops 1811939328 | bytes 12976128 | tf_op jit(solution)/shard_map/output_norm/pallas_call | solution.py:319
  (125 shorter events, 17.9 us)
Async XLA Ops:
  2.9 10.6 %collective-permute-start = (bf16[128,4608]{1,0:T(8,128)(2,1)S(1)}, bf16[128,4608]{1,0:T(8,128)(2,1)}, u32[]{:S(2)}, u32[]{:S(2)}) collective-permute-start(bf16[128,4608]{1,0:T(8,128)(2,1)S(1)} %norm_rows.2.refs_0_), channel_id=1, source_target_pairs={{0,4},{4,0},{8,12},{12,8},{1,5},{5,1},{9,13},{13,9},{2,6},{6,2},{1... | collective-permute-start | bytes 3538952 | tf_op jit(solution)/shard_map/ppermute | solution.py:352
  3.4 39.5 %collective-permute-start.2 = (bf16[128,4608]{1,0:T(8,128)(2,1)S(1)}, bf16[128,4608]{1,0:T(8,128)(2,1)S(1)}, u32[]{:S(2)}, u32[]{:S(2)}) collective-permute-start(bf16[128,4608]{1,0:T(8,128)(2,1)S(1)} %norm_rows.2.refs_0_), channel_id=1, source_target_pairs={{0,8},{4,12},{8,0},{12,4},{1,9},{5,13},{9,1},{13,5},{2,10},{6,14},... | collective-permute-start | bytes 3538952 | tf_op jit(solution)/shard_map/ppermute | solution.py:352
  6.3 7.1 %collective-permute-start.1 = (bf16[64,4608]{1,0:T(8,128)(2,1)S(1)}, bf16[64,4608]{1,0:T(8,128)(2,1)S(1)}, u32[]{:S(2)}, u32[]{:S(2)}) collective-permute-start(bf16[64,4608]{1,0:T(8,128)(2,1)S(1)} %norm_rows.3.refs_2_), channel_id=1, source_target_pairs={{0,4},{4,0},{8,12},{12,8},{1,5},{5,1},{9,13},{13,9},{2,6},{6,2},{1... | collective-permute-start | bytes 1769480 | tf_op jit(solution)/shard_map/ppermute | solution.py:352
  18.1 24.8 %copy-start.5 = (bf16[2,384,128]{2,1,0:T(8,128)(2,1)}, bf16[2,384,128]{2,1,0:T(8,128)(2,1)S(1)}, u32[]{:S(2)}) copy-start(bf16[2,384,128]{2,1,0:T(8,128)(2,1)S(1)} %get-tuple-element.27.refs_2_) | copy-start | bytes 589828
  18.1 24.8 %copy-start.9 = (bf16[384,256]{1,0:T(8,128)(2,1)}, bf16[384,256]{1,0:T(8,128)(2,1)S(1)}, u32[]{:S(2)}) copy-start(bf16[384,256]{1,0:T(8,128)(2,1)S(1)} %get-tuple-element.28) | copy-start | bytes 589828
  18.1 9.7 %collective-permute-start.3 = (bf16[384,256]{1,0:T(8,128)(2,1)S(1)}, bf16[384,256]{1,0:T(8,128)(2,1)S(1)}, u32[]{:S(2)}, u32[]{:S(2)}) collective-permute-start(bf16[384,256]{1,0:T(8,128)(2,1)S(1)} %get-tuple-element.28), channel_id=1, source_target_pairs={{0,1},{1,2},{2,3},{3,0},{4,5},{5,6},{6,7},{7,4},{8,9},{9,10},{10,1... | collective-permute-start | bytes 589832 | tf_op jit(solution)/shard_map/ppermute | solution.py:357
  19.7 16.0 %collective-permute-start.4 = (bf16[384,256]{1,0:T(8,128)(2,1)S(1)}, bf16[384,256]{1,0:T(8,128)(2,1)S(1)}, u32[]{:S(2)}, u32[]{:S(2)}) collective-permute-start(bf16[384,256]{1,0:T(8,128)(2,1)S(1)} %get-tuple-element.28), channel_id=1, source_target_pairs={{0,2},{1,3},{2,0},{3,1},{4,6},{5,7},{6,4},{7,5},{8,10},{9,11},{10,... | collective-permute-start | bytes 589832 | tf_op jit(solution)/shard_map/ppermute | solution.py:357
  22.3 13.4 %collective-permute-start.5 = (bf16[384,256]{1,0:T(8,128)(2,1)S(1)}, bf16[384,256]{1,0:T(8,128)(2,1)S(1)}, u32[]{:S(2)}, u32[]{:S(2)}) collective-permute-start(bf16[384,256]{1,0:T(8,128)(2,1)S(1)} %get-tuple-element.28), channel_id=1, source_target_pairs={{0,3},{1,0},{2,1},{3,2},{4,7},{5,4},{6,5},{7,6},{8,11},{9,8},{10,9... | collective-permute-start | bytes 589832 | tf_op jit(solution)/shard_map/ppermute | solution.py:357
  27.8 17.4 %copy-start.11 = (bf16[384,256]{1,0:T(8,128)(2,1)}, bf16[384,256]{1,0:T(8,128)(2,1)S(1)}, u32[]{:S(2)}) copy-start(bf16[384,256]{1,0:T(8,128)(2,1)S(1)} %collective-permute-done.3) | copy-start | bytes 589828
  42.9 3.6 %collective-permute-start.6 = (bf16[128,4608]{1,0:T(8,128)(2,1)S(1)}, bf16[128,4608]{1,0:T(8,128)(2,1)S(1)}, u32[]{:S(2)}, u32[]{:S(2)}) collective-permute-start(bf16[128,4608]{1,0:T(8,128)(2,1)S(1)} %collective-permute-done.2.refs_0_), channel_id=1, source_target_pairs={{0,4},{4,0},{8,12},{12,8},{1,5},{5,1},{9,13},{13,9},{2,6},{6,2},{1... | collective-permute-start | bytes 3538952 | tf_op jit(solution)/shard_map/ppermute | solution.py:352
  48.9 59.3 %copy-start.24 = (f32[768,64]{1,0:T(8,128)S(1)}, f32[768,64]{1,0:T(8,128)}, u32[]{:S(2)}) copy-start(f32[768,64]{1,0:T(8,128)} %copy-done.23) | copy-start | bytes 589828
  48.9 63.2 %copy-start.31 = (s32[64]{0:T(128)S(1)}, s32[64]{0:T(128)}, u32[]{:S(2)}) copy-start(s32[64]{0:T(128)} %get-tuple-element.59) | copy-start | bytes 772
  48.9 63.2 %copy-start.33 = (s32[64]{0:T(128)S(1)}, s32[64]{0:T(128)}, u32[]{:S(2)}) copy-start(s32[64]{0:T(128)} %get-tuple-element.60) | copy-start | bytes 772
  51.5 28.4 %collective-permute-start.19 = (bf16[128,4608]{1,0:T(8,128)(2,1)S(1)}, bf16[128,4608]{1,0:T(8,128)(2,1)S(1)}, u32[]{:S(2)}, u32[]{:S(2)}) collective-permute-start(bf16[128,4608]{1,0:T(8,128)(2,1)S(1)} %constant_dynamic-slice_fusion), channel_id=1, source_target_pairs={{0,8},{4,12},{8,0},{12,4},{1,9},{5,13},{9,1},{13,5},{2,10},{6,14},... | collective-permute-start | bytes 3538952 | tf_op jit(solution)/shard_map/ppermute | solution.py:352
  51.6 107.7 %collective-permute-start.18 = (bf16[256,4608]{1,0:T(8,128)(2,1)}, bf16[256,4608]{1,0:T(8,128)(2,1)}, u32[]{:S(2)}, u32[]{:S(2)}) collective-permute-start(bf16[256,4608]{1,0:T(8,128)(2,1)} %refs_4_.1), channel_id=1, source_target_pairs={{0,4},{4,0},{8,12},{12,8},{1,5},{5,1},{9,13},{13,9},{2,6},{6,2},{1... | collective-permute-start | bytes 7077896 | tf_op jit(solution)/shard_map/ppermute | solution.py:352
  79.9 27.7 %collective-permute-start.20 = (bf16[128,4608]{1,0:T(8,128)(2,1)S(1)}, bf16[128,4608]{1,0:T(8,128)(2,1)}, u32[]{:S(2)}, u32[]{:S(2)}) collective-permute-start(bf16[128,4608]{1,0:T(8,128)(2,1)S(1)} %collective-permute-done.19.refs_6_), channel_id=1, source_target_pairs={{0,16},{16,0},{1,17},{17,1},{2,18},{18,2},{3,19},{19,3},{4,20},{20... | collective-permute-start | bytes 3538952 | tf_op jit(solution)/shard_map/ppermute | solution.py:357
  81.4 26.2 %collective-permute-start.7 = (bf16[64,4608]{1,0:T(8,128)(2,1)S(1)}, bf16[64,4608]{1,0:T(8,128)(2,1)S(1)}, u32[]{:S(2)}, u32[]{:S(2)}) collective-permute-start(bf16[64,4608]{1,0:T(8,128)(2,1)S(1)} %norm_rows.3.refs_2_), channel_id=1, source_target_pairs={{0,8},{4,12},{8,0},{12,4},{1,9},{5,13},{9,1},{13,5},{2,10},{6,14},... | collective-permute-start | bytes 1769480 | tf_op jit(solution)/shard_map/ppermute | solution.py:352
  81.7 77.6 %collective-permute-start.21 = (bf16[128,4608]{1,0:T(8,128)(2,1)S(1)}, bf16[128,4608]{1,0:T(8,128)(2,1)}, u32[]{:S(2)}, u32[]{:S(2)}) collective-permute-start(bf16[128,4608]{1,0:T(8,128)(2,1)S(1)} %collective-permute-done.19.refs_6_), channel_id=1, source_target_pairs={{0,4},{4,0},{8,12},{12,8},{1,5},{5,1},{9,13},{13,9},{2,6},{6,2},{1... | collective-permute-start | bytes 3538952 | tf_op jit(solution)/shard_map/ppermute | solution.py:352
  107.6 51.7 %collective-permute-start.22 = (bf16[128,4608]{1,0:T(8,128)(2,1)}, bf16[128,4608]{1,0:T(8,128)(2,1)}, u32[]{:S(2)}, u32[]{:S(2)}) collective-permute-start(bf16[128,4608]{1,0:T(8,128)(2,1)} %collective-permute-done.20.refs_7_), channel_id=1, source_target_pairs={{0,4},{4,0},{8,12},{12,8},{1,5},{5,1},{9,13},{13,9},{2,6},{6,2},{1... | collective-permute-start | bytes 3538952 | tf_op jit(solution)/shard_map/ppermute | solution.py:352
  107.6 10.5 %collective-permute-start.8 = (bf16[64,4608]{1,0:T(8,128)(2,1)S(1)}, bf16[64,4608]{1,0:T(8,128)(2,1)S(1)}, u32[]{:S(2)}, u32[]{:S(2)}) collective-permute-start(bf16[64,4608]{1,0:T(8,128)(2,1)S(1)} %collective-permute-done.7.refs_0_), channel_id=1, source_target_pairs={{0,4},{4,0},{8,12},{12,8},{1,5},{5,1},{9,13},{13,9},{2,6},{6,2},{1... | collective-permute-start | bytes 1769480 | tf_op jit(solution)/shard_map/ppermute | solution.py:352
  108.2 8.6 %collective-permute-start.12 = (bf16[256,256]{1,0:T(8,128)(2,1)}, bf16[256,256]{1,0:T(8,128)(2,1)S(1)}, u32[]{:S(2)}, u32[]{:S(2)}) collective-permute-start(bf16[256,256]{1,0:T(8,128)(2,1)} %get-tuple-element.33), channel_id=1, source_target_pairs={{0,1},{1,2},{2,3},{3,0},{4,5},{5,6},{6,7},{7,4},{8,9},{9,10},{10,1... | collective-permute-start | bytes 393224 | tf_op jit(solution)/shard_map/ppermute | solution.py:357
  117.5 8.9 %collective-permute-start.13 = (bf16[256,256]{1,0:T(8,128)(2,1)}, bf16[256,256]{1,0:T(8,128)(2,1)S(1)}, u32[]{:S(2)}, u32[]{:S(2)}) collective-permute-start(bf16[256,256]{1,0:T(8,128)(2,1)} %get-tuple-element.33), channel_id=1, source_target_pairs={{0,2},{1,3},{2,0},{3,1},{4,6},{5,7},{6,4},{7,5},{8,10},{9,11},{10,... | collective-permute-start | bytes 393224 | tf_op jit(solution)/shard_map/ppermute | solution.py:357
  118.1 9.8 %collective-permute-start.14 = (bf16[256,256]{1,0:T(8,128)(2,1)}, bf16[256,256]{1,0:T(8,128)(2,1)S(1)}, u32[]{:S(2)}, u32[]{:S(2)}) collective-permute-start(bf16[256,256]{1,0:T(8,128)(2,1)} %get-tuple-element.33), channel_id=1, source_target_pairs={{0,3},{1,0},{2,1},{3,2},{4,7},{5,4},{6,5},{7,6},{8,11},{9,8},{10,9... | collective-permute-start | bytes 393224 | tf_op jit(solution)/shard_map/ppermute | solution.py:357
  123.1 12.7 %copy-start.16 = (bf16[384,256]{1,0:T(8,128)(2,1)S(1)}, bf16[384,256]{1,0:T(8,128)(2,1)}, u32[]{:S(2)}) copy-start(bf16[384,256]{1,0:T(8,128)(2,1)} %copy-done.15) | copy-start | bytes 589828
  123.1 12.7 %copy-start.18 = (bf16[256,256]{1,0:T(8,128)(2,1)S(1)}, bf16[256,256]{1,0:T(8,128)(2,1)}, u32[]{:S(2)}) copy-start(bf16[256,256]{1,0:T(8,128)(2,1)} %copy-done.17) | copy-start | bytes 393220
  126.4 6.9 %collective-permute-start.9 = (bf16[128,256]{1,0:T(8,128)(2,1)S(1)}, bf16[128,256]{1,0:T(8,128)(2,1)S(1)}, u32[]{:S(2)}, u32[]{:S(2)}) collective-permute-start(bf16[128,256]{1,0:T(8,128)(2,1)S(1)} %get-tuple-element.36), channel_id=1, source_target_pairs={{0,1},{1,2},{2,3},{3,0},{4,5},{5,6},{6,7},{7,4},{8,9},{9,10},{10,1... | collective-permute-start | bytes 196616 | tf_op jit(solution)/shard_map/ppermute | solution.py:357
  127.9 18.0 %collective-permute-start.10 = (bf16[128,256]{1,0:T(8,128)(2,1)S(1)}, bf16[128,256]{1,0:T(8,128)(2,1)S(1)}, u32[]{:S(2)}, u32[]{:S(2)}) collective-permute-start(bf16[128,256]{1,0:T(8,128)(2,1)S(1)} %get-tuple-element.36), channel_id=1, source_target_pairs={{0,2},{1,3},{2,0},{3,1},{4,6},{5,7},{6,4},{7,5},{8,10},{9,11},{10,... | collective-permute-start | bytes 196616 | tf_op jit(solution)/shard_map/ppermute | solution.py:357
  133.2 12.7 %collective-permute-start.11 = (bf16[128,256]{1,0:T(8,128)(2,1)S(1)}, bf16[128,256]{1,0:T(8,128)(2,1)S(1)}, u32[]{:S(2)}, u32[]{:S(2)}) collective-permute-start(bf16[128,256]{1,0:T(8,128)(2,1)S(1)} %get-tuple-element.36), channel_id=1, source_target_pairs={{0,3},{1,0},{2,1},{3,2},{4,7},{5,4},{6,5},{7,6},{8,11},{9,8},{10,9... | collective-permute-start | bytes 196616 | tf_op jit(solution)/shard_map/ppermute | solution.py:357
  145.9 13.4 %copy-start.4 = (bf16[192,4608]{1,0:T(8,128)(2,1)S(1)}, bf16[192,4608]{1,0:T(8,128)(2,1)}, u32[]{:S(2)}) copy-start(bf16[192,4608]{1,0:T(8,128)(2,1)} %refs_10_.1) | copy-start | bytes 5308420
  150.9 2.8 %collective-permute-start.15 = (bf16[192,256]{1,0:T(8,128)(2,1)S(1)}, bf16[192,256]{1,0:T(8,128)(2,1)S(1)}, u32[]{:S(2)}, u32[]{:S(2)}) collective-permute-start(bf16[192,256]{1,0:T(8,128)(2,1)S(1)} %get-tuple-element.44), channel_id=1, source_target_pairs={{0,4},{4,0},{8,12},{12,8},{1,5},{5,1},{9,13},{13,9},{2,6},{6,2},{1... | collective-permute-start | bytes 294920 | tf_op jit(solution)/shard_map/ppermute | solution.py:352
  150.9 6.7 %collective-permute-start.16 = (bf16[192,256]{1,0:T(8,128)(2,1)}, bf16[192,256]{1,0:T(8,128)(2,1)S(1)}, u32[]{:S(2)}, u32[]{:S(2)}) collective-permute-start(bf16[192,256]{1,0:T(8,128)(2,1)} %get-tuple-element.45), channel_id=1, source_target_pairs={{0,8},{4,12},{8,0},{12,4},{1,9},{5,13},{9,1},{13,5},{2,10},{6,14},... | collective-permute-start | bytes 294920 | tf_op jit(solution)/shard_map/ppermute | solution.py:352
  153.7 5.6 %collective-permute-start.17 = (bf16[192,256]{1,0:T(8,128)(2,1)}, bf16[192,256]{1,0:T(8,128)(2,1)S(1)}, u32[]{:S(2)}, u32[]{:S(2)}) collective-permute-start(bf16[192,256]{1,0:T(8,128)(2,1)} %get-tuple-element.46), channel_id=1, source_target_pairs={{0,12},{4,8},{8,4},{12,0},{1,13},{5,9},{9,5},{13,1},{2,14},{6,10},... | collective-permute-start | bytes 294920 | tf_op jit(solution)/shard_map/ppermute | solution.py:352
  (25 other events, 128.0 us)

commit v3 on v2

--- a/solution.py
+++ b/solution.py
@@ -13,6 +13,8 @@
 EPS = 1e-6
 MIB = 1024 * 1024
 HIDDEN = -1e30
+NEVER = 1 << 30
+COST = pl.CostEstimate(flops=1, bytes_accessed=1, transcendentals=0)
 
 ANY = pl.BlockSpec(memory_space=pl.ANY)
 VMEM = pl.BlockSpec(memory_space=pltpu.VMEM)
@@ -46,16 +48,14 @@
         out_specs=pl.BlockSpec((step, width), lambda i: (i, 0)),
         out_shape=jax.ShapeDtypeStruct((rows, width), jnp.bfloat16),
         compiler_params=params(12),
-        cost_estimate=pl.CostEstimate(
-            flops=6 * rows * width, bytes_accessed=4 * rows * width, transcendentals=0
-        ),
+        cost_estimate=COST,
         name="norm_rows",
     )(hidden, gain.reshape(1, -1))
 
 
 def qkv_kernel(parts, heads, *refs):
     parts_refs = refs[:parts]
-    weights, cosine, sine, q_out, kv_out, rows, arrived = refs[parts:]
+    w_query, w_kv, cosine, sine, q_out, kv_out, rows, arrived = refs[parts:]
     copies, first = [], 0
     for at, part in enumerate(parts_refs):
         span = pl.ds(first, part.shape[0])
@@ -65,27 +65,28 @@
         copy.start()
     for copy in copies:
         copy.wait()
-    product = jnp.dot(rows[...], weights[...], preferred_element_type=jnp.float32)
     cos, sin = cosine[...], sine[...]
+    product = jnp.dot(rows[...], w_kv[...], preferred_element_type=jnp.float32)
 
     def rotated(at):
         y = product[:, at * HD : (at + 1) * HD]
         return y * cos + pltpu.roll(y, HD // 2, 1) * sin
 
     factor = ATT_SCALAR ** (-0.5) * math.log2(math.e)
+    kv_out[:, :HD] = rotated(0).astype(jnp.bfloat16)
+    kv_out[:, HD:] = product[:, HD:].astype(jnp.bfloat16)
+    product = jnp.dot(rows[...], w_query[...], preferred_element_type=jnp.float32)
     for head in range(heads):
         q_out[head] = (rotated(head) * factor).astype(jnp.bfloat16)
-    kv_out[:, :HD] = rotated(heads).astype(jnp.bfloat16)
-    kv_out[:, HD:] = product[:, (heads + 1) * HD :].astype(jnp.bfloat16)
-
-
-def qkv(parts, weights, cosine, sine):
+
+
+def qkv(parts, w_query, w_kv, cosine, sine):
     total = sum(part.shape[0] for part in parts)
-    width, columns = weights.shape
-    heads = columns // HD - 2
+    width, columns = w_query.shape
+    heads = columns // HD
     return pl.pallas_call(
         functools.partial(qkv_kernel, len(parts), heads),
-        in_specs=[ANY] * len(parts) + [VMEM] * 3,
+        in_specs=[ANY] * len(parts) + [VMEM] * 4,
         out_specs=[VMEM, VMEM],
         out_shape=[
             jax.ShapeDtypeStruct((heads, total, HD), jnp.bfloat16),
@@ -96,13 +97,9 @@
             pltpu.SemaphoreType.DMA((len(parts),)),
         ],
         compiler_params=params(24),
-        cost_estimate=pl.CostEstimate(
-            flops=2 * total * width * columns,
-            bytes_accessed=2 * width * (total + columns),
-            transcendentals=0,
-        ),
+        cost_estimate=COST,
         name="qkv",
-    )(*parts, weights, cosine, sine)
+    )(*parts, w_query, w_kv, cosine, sine)
 
 
 class Step:
@@ -257,10 +254,6 @@
         for parts in groups
     ]
     parts = [part for parts in groups for part in parts]
-    work = 0
-    for step in plan:
-        slots = len(step.slots) + (step.same is not None)
-        work += qs[step.q].size // HD * groups[step.group][0].shape[1] * slots
     sizes = (len(qs), [len(parts) for parts in groups])
     results = pl.pallas_call(
         functools.partial(attention_kernel, plan, fresh, final, sizes),
@@ -272,9 +265,7 @@
         out_shape=out_shape,
         scratch_shapes=scratch + buffers + [pltpu.SemaphoreType.DMA((len(parts),))],
         compiler_params=params(20),
-        cost_estimate=pl.CostEstimate(
-            flops=4 * work * HD, bytes_accessed=2 * work // HD, transcendentals=work
-        ),
+        cost_estimate=COST,
         name="attention",
     )(q_starts, k_starts, *qs, *q_places, *k_places, *parts, *held)
     if final:
@@ -282,54 +273,123 @@
     return [tuple(results[2 * at : 2 * at + 2]) for at in range(len(qs))]
 
 
-def output_kernel(pieces, chunks, at, *refs):
-    attended = refs[:4]
-    weights = refs[4 : 4 + len(pieces)]
-    hidden, gain, out, projected = refs[4 + len(pieces) :]
+def near_kernel(chunks, *refs):
+    lefts, pieces = refs[:2], refs[2:4]
+    out, weights, arrived = refs[4:]
+    step = out.shape[1] // chunks
+    depth = pieces[0].shape[0]
+
+    def copies(chunk):
+        lanes = pl.ds(chunk * step, step)
+        return [
+            pltpu.make_async_copy(
+                piece.at[:, lanes],
+                weights.at[pl.ds(at * depth, depth), lanes],
+                arrived.at[chunk, at],
+            )
+            for at, piece in enumerate(pieces)
+        ]
+
+    for chunk in range(chunks):
+        for copy in copies(chunk):
+            copy.start()
+    left = jnp.concatenate([part[...] for part in lefts], axis=1)
+    for chunk in range(chunks):
+        for copy in copies(chunk):
+            copy.wait()
+        lanes = slice(chunk * step, chunk * step + step)
+        out[:, lanes] = jnp.dot(left, weights[:, lanes], preferred_element_type=jnp.float32)
+
+
+def output_near(lefts, pieces):
+    rows, width = lefts[0].shape[0], pieces[0].shape[1]
+    depth = sum(piece.shape[0] for piece in pieces)
+    chunks = 6
+    return pl.pallas_call(
+        functools.partial(near_kernel, chunks),
+        in_specs=[VMEM] * 2 + [ANY] * 2,
+        out_specs=VMEM,
+        out_shape=jax.ShapeDtypeStruct((rows, width), jnp.float32),
+        scratch_shapes=[
+            pltpu.VMEM((depth, width), jnp.bfloat16),
+            pltpu.SemaphoreType.DMA((chunks, 2)),
+        ],
+        compiler_params=params(16),
+        cost_estimate=COST,
+        name="output_near",
+    )(*lefts, *pieces)
+
+
+def output_kernel(runs, depth, chunks, at, *refs):
+    count = len({piece for piece, _, _, _ in runs})
+    lefts, pieces = refs[:2], refs[2 : 2 + count]
+    near, hidden, gain, out, weights, projected, staged, arrived, left_sem = refs[2 + count :]
     width = hidden.shape[1]
     step = width // chunks
-    lefts = []
-    for index, (part, piece) in enumerate(zip(pieces, weights)):
-        depth = piece.shape[0]
-        if depth == attended[part].shape[1]:
-            lefts.append(attended[part][...])
-        else:
-            lefts.append(attended[part][:, pl.ds(pl.multiple_of(at[index], HD), depth)])
+
+    def copies(chunk):
+        lanes = pl.ds(chunk * step, step)
+        return [
+            pltpu.make_async_copy(
+                pieces[piece].at[pl.ds(first, rows), lanes],
+                weights.at[pl.ds(pl.multiple_of(head * depth + at[index], 16), rows), lanes],
+                arrived.at[chunk, index],
+            )
+            for index, (piece, first, rows, head) in enumerate(runs)
+        ]
+
+    for chunk in range(chunks):
+        for copy in copies(chunk):
+            copy.start()
+    left = jnp.concatenate([part[...] for part in lefts], axis=1)
     square = jnp.zeros((hidden.shape[0], 128), jnp.float32)
     for chunk in range(chunks):
+        for copy in copies(chunk):
+            copy.wait()
         lanes = slice(chunk * step, chunk * step + step)
-        total = jnp.dot(lefts[0], weights[0][:, lanes], preferred_element_type=jnp.float32)
-        for left, piece in zip(lefts[1:], weights[1:]):
-            total = total + jnp.dot(left, piece[:, lanes], preferred_element_type=jnp.float32)
+        total = near[:, lanes] + jnp.dot(
+            left, weights[:, lanes], preferred_element_type=jnp.float32
+        )
         projected[:, lanes] = total
         for lane in range(0, step, 128):
-            piece = total[:, lane : lane + 128]
-            square = square + piece * piece
+            part = total[:, lane : lane + 128]
+            square = square + part * part
     mean = jnp.sum(square, axis=1, keepdims=True) / width
     scale = lax.rsqrt(mean + EPS)
+    stores = []
     for chunk in range(chunks):
         lanes = slice(chunk * step, chunk * step + step)
         normed = projected[:, lanes] * scale * gain[:, lanes]
-        out[:, lanes] = (hidden[:, lanes].astype(jnp.float32) + normed).astype(jnp.bfloat16)
-
-
-def output(attended, pieces, weights, places, hidden, gain):
+        staged[:, lanes] = (hidden[:, lanes].astype(jnp.float32) + normed).astype(jnp.bfloat16)
+        lanes = pl.ds(chunk * step, step)
+        stores.append(
+            pltpu.make_async_copy(staged.at[:, lanes], out.at[:, lanes], left_sem.at[chunk])
+        )
+        stores[-1].start()
+    for store in stores:
+        store.wait()
+
+
+def output(lefts, pieces, runs, places, near, hidden, gain):
     rows, width = hidden.shape
-    depth = sum(piece.shape[0] for piece in weights)
+    depth = lefts[0].shape[1]
+    chunks = 6
     return pl.pallas_call(
-        functools.partial(output_kernel, pieces, 6),
-        in_specs=[SMEM] + [VMEM] * (4 + len(weights) + 2),
-        out_specs=VMEM,
+        functools.partial(output_kernel, runs, depth, chunks),
+        in_specs=[SMEM] + [VMEM] * 2 + [ANY] * len(pieces) + [VMEM] * 3,
+        out_specs=ANY,
         out_shape=jax.ShapeDtypeStruct(hidden.shape, jnp.bfloat16),
-        scratch_shapes=[pltpu.VMEM((rows, width), jnp.float32)],
-        compiler_params=params(26),
-        cost_estimate=pl.CostEstimate(
-            flops=2 * rows * width * depth,
-            bytes_accessed=2 * width * (depth + 2 * rows),
-            transcendentals=0,
-        ),
+        scratch_shapes=[
+            pltpu.VMEM((2 * depth, width), jnp.bfloat16),
+            pltpu.VMEM((rows, width), jnp.float32),
+            pltpu.VMEM((rows, width), jnp.bfloat16),
+            pltpu.SemaphoreType.DMA((chunks, len(runs))),
+            pltpu.SemaphoreType.DMA((chunks,)),
+        ],
+        compiler_params=params(24),
+        cost_estimate=COST,
         name="output_norm",
-    )(places, *attended, *weights, hidden, gain.reshape(1, -1))
+    )(places, *lefts, *pieces, near, hidden, gain.reshape(1, -1))
 
 
 def rotary_tables(positions):
@@ -361,17 +421,48 @@
     return lax.optimization_barrier((array, *others))[0]
 
 
-def two_chips(hidden, pre_gain, post_gain, wq, wk, wv, w_out, block_of):
+def along_line(array):
+    up = lax.ppermute(array, "seq", [(0, 1), (1, 2), (2, 3)])
+    down = lax.ppermute(array, "seq", [(1, 0), (2, 1), (3, 2)])
+    across = lax.ppermute(array, "seq", [(0, 2), (1, 3), (2, 0), (3, 1)])
+    passed = lax.ppermute(across, "seq", [(1, 0), (2, 3)])
+    return [part[None] for part in (array, up, down, across, passed)]
+
+
+def four_by_four(hidden, pre_gain, post_gain, wq, wk, wv, w_out, block_of):
     rows = hidden.shape[0]
     block_rows = 2 * rows
-    cuts = [rows * 2 // 3, rows - rows * 2 // 3]
-    lines, group_count = lax.axis_size("seq"), lax.axis_size("groups")
+    cuts = [rows // 3 * 2, rows // 3]
     seq, tp, group = lax.axis_index("seq"), lax.axis_index("tp"), lax.axis_index("groups")
     chip, core = tp // 2, tp % 2
 
-    line = (seq - jnp.arange(lines, dtype=jnp.int32)) % lines
-    near_starts = lookup(block_of, 2 * line + chip) * block_rows
-    far_starts = lookup(block_of, 2 * line + 1 - chip) * block_rows
+    depth = w_out.shape[0]
+    part = depth // 4
+    sent = lax.dynamic_slice_in_dim(w_out, (group * 2 + seq % 2) * part, part, axis=0)
+    pair = lambda array: lax.ppermute(array, "seq", [(0, 1), (1, 0), (2, 3), (3, 2)])
+    w_first = flipped(sent, "tp", 2)
+    w_group, w_pair = shifted(w_first, "groups", 1), pair(w_first)
+    w_partner = flipped(w_out, "tp", 1)
+    place = [(group, seq), (1 - group, seq), (group, seq + 1), (1 - group, seq + 1)]
+    places = [(at * 2 + line % 2) * part for at, line in place]
+    places = jnp.stack(places[:3] * 2 + places[3:] * 2).astype(jnp.int32)
+    runs = [(head, at * part, part, head) for head in range(2) for at in range(3)]
+    runs += [(2, 0, part, 0), (3, 0, part, 1)]
+
+    third = rows // 3
+    own = [
+        norm(hidden, pre_gain, at * third, third)
+        for at in range(3)
+    ]
+    away = [flipped(chunk, "tp", 2) for chunk in (after(own[0], w_first), own[1], own[2])]
+    partner = [flipped(chunk, "tp", 1) for chunk in own]
+    w_kv = jnp.concatenate([wk, wv], axis=1)
+
+    line = jnp.stack([seq, seq - 1, seq + 1, (seq + 2) % 4, 3 - seq])
+    valid = (line >= 0) & (line < 4) & (jnp.arange(5) < jnp.where((seq == 1) | (seq == 2), 4, 5))
+    place_of = lambda side: lookup(block_of, 2 * line + side) * block_rows
+    near_starts = jnp.where(valid, place_of(chip), NEVER)
+    far_starts = jnp.where(valid, place_of(1 - chip), NEVER)
     place = []
     for first, size in zip((0, cuts[0]), cuts):
         run = first + jnp.arange(size, dtype=jnp.int32)
@@ -381,23 +472,20 @@
         jnp.concatenate([near_starts[0] + place, far_starts[0] + place])
     )
     first, last = 2 * cuts[0], block_rows
-
-    own = [norm(hidden, pre_gain, 0, cuts[0]), norm(hidden, pre_gain, cuts[0], cuts[1])]
-    away = [flipped(chunk, "tp", 2) for chunk in own]
-    partner = [flipped(chunk, "tp", 1) for chunk in own]
-    weights = jnp.concatenate([wq, wk, wv], axis=1)
-
-    q_near, kv_near = qkv(
-        [own[0], partner[0], own[1], partner[1]],
-        weights,
-        cosine[:block_rows],
-        sine[:block_rows],
-    )
-    near = [kv_near] + [shifted(kv_near, "seq", by) for by in range(1, lines)]
-    near = [part[None] for part in near]
     column, row = place[:, None], place[None, :]
     head, tail = slice(0, first), slice(first, last)
-    others = list(range(1, lines))
+    others, everyone = list(range(1, 5)), list(range(5))
+
+    def project(parts, span):
+        return qkv(parts, wq, w_kv, cosine[span], sine[span])
+
+    q_near, kv_near = project(
+        [after(own[0], w_partner), own[1], *partner[:2], own[2], partner[2]],
+        slice(0, block_rows),
+    )
+    near = along_line(after(kv_near, w_group, w_pair, away[0]))
+    w_last = shifted(after(w_pair, *near[1:4]), "groups", 1)
+
     (near_state,) = attention(
         [Step(0, 0, others, same=0)],
         [q_near],
@@ -409,41 +497,40 @@
         [None],
     )
 
-    def project(chunk, span):
-        other = flipped(chunk, "tp", 1)
-        at = slice(block_rows + span.start, block_rows + span.stop)
-        return qkv([chunk, other], weights, cosine[at], sine[at])
-
-    away[0] = after(away[0], *near_state)
-    q_head, kv_head = project(away[0], head)
-    far_head = [kv_head] + [shifted(kv_head, "seq", by) for by in range(1, lines)]
-    far_head = [part[None] for part in far_head]
-
-    half = w_out.shape[0] // group_count
-    sent = lax.dynamic_slice_in_dim(w_out, group * half, half, axis=0)
-    sent = after(sent, kv_head)
-    w_far = [flipped(sent, "tp", 2)]
-    w_far += [shifted(w_far[0], "groups", by) for by in range(1, group_count)]
-    w_partner = flipped(after(w_out, kv_near), "tp", 1)
-    w_cross = [flipped(piece, "tp", 1) for piece in w_far]
-
-    away[1] = after(away[1], kv_head)
-    q_tail, kv_tail = project(away[1], tail)
-    far_tail = [kv_tail] + [shifted(kv_tail, "seq", by) for by in range(1, lines)]
-    far_tail = [part[None] for part in far_tail]
+    far_span = lambda span: slice(block_rows + span.start, block_rows + span.stop)
+    away[1] = after(away[1], *near_state)
+    heads = away[:2] + [flipped(chunk, "tp", 1) for chunk in away[:2]]
+    q_head, kv_head = project(heads, far_span(head))
+    far_head = along_line(kv_head)
+    w_far = jnp.concatenate([w_first, w_group, w_pair], axis=0)
+    w_cross = flipped(w_far, "tp", 1)
+    q_head = after(q_head, w_cross)
+    (head_state,) = attention(
+        [Step(0, 1, [], same=0), Step(0, 0, everyone)],
+        [q_head],
+        far_starts[:1],
+        [column[head]],
+        [near, far_head[:1]],
+        jnp.concatenate([near_starts, far_starts[:1]]),
+        [row, row[:, head]],
+        [None],
+    )
+
+    away[2] = after(away[2], *head_state, *far_head[1:4], w_last)
+    w_last_cross = flipped(w_last, "tp", 1)
+    q_tail, kv_tail = project([away[2], flipped(away[2], "tp", 1)], far_span(tail))
+    far_tail = along_line(kv_tail)
 
     q_starts = jnp.stack([near_starts[0], far_starts[0], far_starts[0]])
     qs = [q_near, q_head, q_tail]
     q_places = [column, column[head], column[tail]]
-    everyone = list(range(lines))
     state = attention(
         [
-            Step(1, 1, others, same=0),
             Step(2, 2, [], same=0),
-            Step(0, 1, everyone),
-            Step(1, 0, everyone),
             Step(2, 0, everyone),
             Step(2, 1, others, same=0),
+            Step(0, 1, everyone),
+            Step(1, 1, others),
         ],
         qs,
         q_starts,
@@ -451,7 +538,7 @@
         [near, far_head, far_tail[:1]],
         jnp.concatenate([near_starts, far_starts, far_starts[:1]]),
         [row, row[:, head], row[:, tail]],
-        [near_state, None, None],
+        [near_state, head_state, None],
     )
     to = lambda half: [(0, half * cuts[0], cuts[0]), (0, first + half * cuts[1], cuts[1])]
     over = lambda half: [(1, half * cuts[0], cuts[0]), (2, half * cuts[1], cuts[1])]
@@ -470,17 +557,17 @@
         state,
         final=[to(0), to(1), over(0), over(1)],
     )
-    gathered = [
-        mine,
-        flipped(partners, "tp", 1),
-        flipped(same, "tp", 2),
-        flipped(cross, "tp", 3),
-    ]
-    order = [(group - by) % group_count * half for by in range(group_count)]
-    places = jnp.stack([jnp.asarray(at, jnp.int32) for at in [0, 0] + order + order])
-    pieces = [0, 1] + [2] * group_count + [3] * group_count
+    cross = flipped(cross, "tp", 3)
+    same = flipped(same, "tp", 2)
+    near_sum = output_near([mine, flipped(partners, "tp", 1)], [w_out, w_partner])
     return output(
-        gathered, pieces, [w_out, w_partner] + w_far + w_cross, places, hidden, post_gain
+        [same, cross],
+        [w_far, w_cross, w_last, w_last_cross],
+        runs,
+        places,
+        near_sum,
+        hidden,
+        post_gain,
     )
 
 
@@ -495,11 +582,11 @@
     block = (2 * line[:, None] + jnp.arange(2, dtype=jnp.int32)).reshape(-1)
     starts = lookup(block_of, block) * block_rows
     cosine, sine = rotary_tables((starts[:2, None] + place).reshape(-1))
-    weights = jnp.concatenate([wq, wk, wv], axis=1)
+    w_kv = jnp.concatenate([wk, wv], axis=1)
     qs, keys_values = [], []
     for at in range(2):
         span = slice(at * block_rows, (at + 1) * block_rows)
-        q, kv = qkv([normed[span]], weights, cosine[span], sine[span])
+        q, kv = qkv([normed[span]], wq, w_kv, cosine[span], sine[span])
         qs.append(q)
         keys_values.append(kv)
     kv = lax.all_gather(jnp.stack(keys_values), "seq")[line].reshape(-1, block_rows, 2 * HD)
@@ -531,7 +618,7 @@
 
 def solution(mesh):
     return jax.shard_map(
-        two_chips if mesh.shape["tp"] == 4 else any_count,
+        four_by_four if tuple(mesh.shape[name] for name in ("groups", "tp", "seq")) == (2, 4, 4) else any_count,
         mesh=mesh,
         in_specs=(
             P(("groups", "seq", "tp"), None),

time: 169 us -> 162 us (0.959)
  the two profiles are of different devices: /device:TPU:0 before, /device:TPU:17 now
where the time goes in v3:
time: 162 us; the launch traced here: 160 us
  starting transfers between devices  53.2 us (33%)
  Pallas kernels  41.6 us (26%)
  waiting for transfers between devices  33.5 us (21%)
  local copies, waits for them, and re-layouts  25.5 us (16%)
  other arithmetic  5.15 us (3%)
    pallas_call x4, Pallas kernels, attention(): pl.pallas_call(functools.partial(attention_kernel, plan, fresh, final, si...  20.3 us
    ppermute x16, waiting for transfers between devices, flipped(): return lax.ppermute(array, axis, [(i, i ^ bit) for i in range(size)])  19 us
    unnamed x97, local copies, waits for them, and re-layouts  18.5 us
    ppermute x16, starting transfers between devices, flipped(): return lax.ppermute(array, axis, [(i, i ^ bit) for i in range(size)])  17 us
    ppermute x3, starting transfers between devices, along_line(): passed = lax.ppermute(across, 'seq', [(1, 0), (2, 3)])  15.6 us
    ppermute x3, starting transfers between devices, along_line(): up = lax.ppermute(array, 'seq', [(0, 1), (1, 2), (2, 3)])  11 us
    ppermute x2, waiting for transfers between devices, shifted(): lax.ppermute(array, axis, [(i, (i + by) % size) for i in range(size)])  9.55 us
    pallas_call x3, Pallas kernels, qkv(): pl.pallas_call(functools.partial(qkv_kernel, len(parts), heads), in_specs...  9.03 us
  transfers between devices with their start and end apart: 31, of which 8 were waited for; matrix products, arithmetic and copies ran while one was open for 9% of the time, Pallas kernels for 22%

profile of v3, /device:TPU:17, one launch (start us, length us, event | category | flops | bytes accessed | tf_op | source)
XLA Modules:
  0.0 159.9 jit_solution(879837788205448617)
XLA Ops:
  4.9 1.9 %constant_dynamic-slice_fusion = bf16[64,4608]{1,0:T(8,128)(2,1)} fusion(bf16[256,4608]{1,0:T(8,128)(2,1)} %refs_2_.3, s32[]{:T(128)S(6)} %select_n.60), kind=kLoop, calls=%fused_computation.46 | loop fusion | bytes 1179652 | tf_op jit(solution)/shard_map/dynamic_slice | solution.py:441
  8.1 1.5 constant_dynamic-update-slice_fusion.1
  10.0 1.7 %constant_dynamic-update-slice_fusion.refs_7_.refs_5_.refs_3_ = bf16[4608,256]{1,0:T(8,128)(2,1)S(1)} fusion(bf16[4608,256]{1,0:T(8,128)(2,1)S(1)} %constant_dynamic-update-slice_fusion.1, bf16[4608,128]{1,0:T(8,128)(2,1)} %param.13), kind=kLoop, calls=%fused_computation.17 | loop fusion | bytes 2359296 | tf_op jit(solution)/shard_map/concatenate | solution.py:459
  11.7 10.5 %collective-permute-done.4 = bf16[64,4608]{1,0:T(8,128)(2,1)} collective-permute-done((bf16[64,4608]{1,0:T(8,128)(2,1)}, bf16[64,4608]{1,0:T(8,128)(2,1)}, u32[]{:S(2)}, u32[]{:S(2)}) %collective-permute-start.4) | collective-permute-done | bytes 589856 | tf_op jit(solution)/shard_map/ppermute | solution.py:412
  26.9 9.5 %collective-permute-done.7 = bf16[64,4608]{1,0:T(8,128)(2,1)S(1)} collective-permute-done((bf16[64,4608]{1,0:T(8,128)(2,1)}, bf16[64,4608]{1,0:T(8,128)(2,1)S(1)}, u32[]{:S(2)}, u32[]{:S(2)}) %collective-permute-start.7) | collective-permute-done | bytes 589856 | tf_op jit(solution)/shard_map/ppermute | solution.py:417
  36.4 1.6 %collective-permute-start.3 = (bf16[64,4608]{1,0:T(8,128)(2,1)}, bf16[64,4608]{1,0:T(8,128)(2,1)S(1)}, u32[]{:S(2)}, u32[]{:S(2)}) collective-permute-start(bf16[64,4608]{1,0:T(8,128)(2,1)} %norm_rows.5.refs_4_), channel_id=1, source_target_pairs={{0,4},{4,0},{8,12},{12,8},{1,5},{5,1},{9,13},{13,9},{2,6},{6,2},{1... | collective-permute-start | bytes 1769480 | tf_op jit(solution)/shard_map/ppermute | solution.py:412
  39.8 1.9 %collective-permute-start.15 = (bf16[192,4608]{1,0:T(8,128)(2,1)S(1)}, bf16[192,4608]{1,0:T(8,128)(2,1)S(1)}, u32[]{:S(2)}, u32[]{:S(2)}) collective-permute-start(bf16[192,4608]{1,0:T(8,128)(2,1)S(1)} %constant_dynamic-update-slice_fusion.2.refs_2_), channel_id=1, source_target_pairs={{0,4},{4,0},{8,12},{12,8},{1,5},{5,1},{9,13},{13,9},{2,6},{6,2},{1... | collective-permute-start | bytes 5308424 | tf_op jit(solution)/shard_map/ppermute | solution.py:412
  45.2 3.8 %qkv.3 = (bf16[2,384,128]{2,1,0:T(8,128)(2,1)S(1)}, bf16[384,256]{1,0:T(8,128)(2,1)S(1)}) custom-call(bf16[64,4608]{1,0:T(8,128)(2,1)} %norm_rows.3.refs_0_, bf16[64,4608]{1,0:T(8,128)(2,1)S(1)} %norm_rows.4.refs_1_, bf16[64,4608]{1,0:T(8,128)(2,1)} %collective-permute-done.1.refs_2_, bf16[64,4608]{1,0:T(8,128)(2,1)} %collective-permute-done.2.refs_3_, ...), custom_call_target="tpu_custom_call" | custom-call | flops 1 | bytes 1 | tf_op jit(solution)/shard_map/qkv/pallas_call | solution.py:87
  49.0 8.0 %collective-permute-done.5.refs_0_ = bf16[64,4608]{1,0:T(8,128)(2,1)S(1)} collective-permute-done((bf16[64,4608]{1,0:T(8,128)(2,1)}, bf16[64,4608]{1,0:T(8,128)(2,1)S(1)}, u32[]{:S(2)}, u32[]{:S(2)}) %collective-permute-start.5) | collective-permute-done | bytes 589856 | tf_op jit(solution)/shard_map/ppermute | solution.py:412
  57.1 3.2 %collective-permute-start.9 = (bf16[384,256]{1,0:T(8,128)(2,1)S(1)}, bf16[384,256]{1,0:T(8,128)(2,1)S(1)}, u32[]{:S(2)}, u32[]{:S(2)}) collective-permute-start(bf16[384,256]{1,0:T(8,128)(2,1)S(1)} %get-tuple-element.36), channel_id=1, source_target_pairs={{0,1},{1,2},{2,3},{4,5},{5,6},{6,7},{8,9},{9,10},{10,11},{12,13},{... | collective-permute-start | bytes 589832 | tf_op jit(solution)/shard_map/ppermute | solution.py:425
  60.3 3.0 %collective-permute-start.10 = (bf16[384,256]{1,0:T(8,128)(2,1)S(1)}, bf16[384,256]{1,0:T(8,128)(2,1)S(1)}, u32[]{:S(2)}, u32[]{:S(2)}) collective-permute-start(bf16[384,256]{1,0:T(8,128)(2,1)S(1)} %get-tuple-element.36), channel_id=1, source_target_pairs={{1,0},{2,1},{3,2},{5,4},{6,5},{7,6},{9,8},{10,9},{11,10},{13,12},{... | collective-permute-start | bytes 589832 | tf_op jit(solution)/shard_map/ppermute | solution.py:426
  63.4 1.5 collective-permute-done.11
  64.9 7.3 %collective-permute-start.12 = (bf16[384,256]{1,0:T(8,128)(2,1)S(1)}, bf16[384,256]{1,0:T(8,128)(2,1)S(1)}, u32[]{:S(2)}, u32[]{:S(2)}) collective-permute-start(bf16[384,256]{1,0:T(8,128)(2,1)S(1)} %collective-permute-done.11), channel_id=1, source_target_pairs={{1,0},{2,3},{5,4},{6,7},{9,8},{10,11},{13,12},{14,15},{17,16},{18,... | collective-permute-start | bytes 589832 | tf_op jit(solution)/shard_map/ppermute | solution.py:428
  73.7 2.0 %collective-permute-done.12 = bf16[384,256]{1,0:T(8,128)(2,1)S(1)} collective-permute-done((bf16[384,256]{1,0:T(8,128)(2,1)S(1)}, bf16[384,256]{1,0:T(8,128)(2,1)S(1)}, u32[]{:S(2)}, u32[]{:S(2)}) %collective-permute-start.12) | collective-permute-done | bytes 196640 | tf_op jit(solution)/shard_map/ppermute | solution.py:428
  75.8 2.9 %attention.4 = (f32[768,128]{1,0:T(8,128)S(1)}, f32[768,256]{1,0:T(8,128)S(1)}) custom-call(s32[1]{0:T(128)S(1)} %bitcast.56, s32[5]{0:T(128)S(1)} %get-tuple-element.67.refs_1_, bf16[2,384,128]{2,1,0:T(8,128)(2,1)S(1)} %get-tuple-element.33.refs_2_, s32[384,1]{1,0:T(8,128)S(1)} %broadcast_in_dim.92.refs_3_.refs_5_, ...), custom_call_target="tpu_custom_call" | custom-call | flops 1 | bytes 1 | tf_op jit(solution)/shard_map/attention/pallas_call | solution.py:258
  78.7 1.5 collective-permute-start.14
  80.2 3.2 %collective-permute-start.16 = (bf16[64,4608]{1,0:T(8,128)(2,1)}, bf16[64,4608]{1,0:T(8,128)(2,1)}, u32[]{:S(2)}, u32[]{:S(2)}) collective-permute-start(bf16[64,4608]{1,0:T(8,128)(2,1)} %norm_rows.5.refs_4_), channel_id=1, source_target_pairs={{0,8},{4,12},{8,0},{12,4},{1,9},{5,13},{9,1},{13,5},{2,10},{6,14},... | collective-permute-start | bytes 1769480 | tf_op jit(solution)/shard_map/ppermute | solution.py:412
  84.0 2.6 %qkv.4 = (bf16[2,256,128]{2,1,0:T(8,128)(2,1)S(1)}, bf16[256,256]{1,0:T(8,128)(2,1)}) custom-call(bf16[64,4608]{1,0:T(8,128)(2,1)S(1)} %collective-permute-done.5.refs_0_, bf16[64,4608]{1,0:T(8,128)(2,1)S(1)} %collective-permute-done.6.refs_1_, bf16[64,4608]{1,0:T(8,128)(2,1)S(1)} %collective-permute-done.13.refs_2_, ...), custom_call_target="tpu_custom_call" | custom-call | flops 1 | bytes 1 | tf_op jit(solution)/shard_map/qkv/pallas_call | solution.py:87
  87.3 3.9 %collective-permute-start.17 = (bf16[256,256]{1,0:T(8,128)(2,1)}, bf16[256,256]{1,0:T(8,128)(2,1)}, u32[]{:S(2)}, u32[]{:S(2)}) collective-permute-start(bf16[256,256]{1,0:T(8,128)(2,1)} %get-tuple-element.42), channel_id=1, source_target_pairs={{0,1},{1,2},{2,3},{4,5},{5,6},{6,7},{8,9},{9,10},{10,11},{12,13},{... | collective-permute-start | bytes 393224 | tf_op jit(solution)/shard_map/ppermute | solution.py:425
  91.2 1.9 %collective-permute-start.18 = (bf16[256,256]{1,0:T(8,128)(2,1)}, bf16[256,256]{1,0:T(8,128)(2,1)}, u32[]{:S(2)}, u32[]{:S(2)}) collective-permute-start(bf16[256,256]{1,0:T(8,128)(2,1)} %get-tuple-element.42), channel_id=1, source_target_pairs={{1,0},{2,1},{3,2},{5,4},{6,5},{7,6},{9,8},{10,9},{11,10},{13,12},{... | collective-permute-start | bytes 393224 | tf_op jit(solution)/shard_map/ppermute | solution.py:426
  96.7 6.0 %attention.5 = (f32[512,128]{1,0:T(8,128)S(1)}, f32[512,256]{1,0:T(8,128)S(1)}) custom-call(s32[1]{0:T(128)S(1)} %bitcast.52, s32[6]{0:T(128)S(1)} %pad_add_fusion.3.refs_1_, bf16[2,256,128]{2,1,0:T(8,128)(2,1)S(1)} %copy-done.20, s32[256,1]{1,0:T(8,128)S(1)} %copy.20.refs_3_.refs_6_, s32[1,384]{1,0:T(1,128)S(1)} %broadcast_in_dim.76.refs_4_.refs_8_, ...), custom_call_target="tpu_custom_call" | custom-call | flops 1 | bytes 1 | tf_op jit(solution)/shard_map/attention/pallas_call | solution.py:258
  106.2 5.0 %collective-permute-start.26 = (bf16[256,256]{1,0:T(8,128)(2,1)}, bf16[256,256]{1,0:T(8,128)(2,1)}, u32[]{:S(2)}, u32[]{:S(2)}) collective-permute-start(bf16[256,256]{1,0:T(8,128)(2,1)} %collective-permute-done.19), channel_id=1, source_target_pairs={{1,0},{2,3},{5,4},{6,7},{9,8},{10,11},{13,12},{14,15},{17,16},{18,... | collective-permute-start | bytes 393224 | tf_op jit(solution)/shard_map/ppermute | solution.py:428
  111.1 2.6 %qkv.5 = (bf16[2,128,128]{2,1,0:T(8,128)(2,1)S(1)}, bf16[128,256]{1,0:T(8,128)(2,1)}) custom-call(bf16[64,4608]{1,0:T(8,128)(2,1)} %collective-permute-done.16.refs_0_, bf16[64,4608]{1,0:T(8,128)(2,1)S(1)} %collective-permute-done.21.refs_1_, bf16[4608,256]{1,0:T(8,128)(2,1)S(1)} %copy-done.4, ...), custom_call_target="tpu_custom_call" | custom-call | flops 1 | bytes 1 | tf_op jit(solution)/shard_map/qkv/pallas_call | solution.py:87
  114.6 3.9 %collective-permute-start.22 = (bf16[128,256]{1,0:T(8,128)(2,1)}, bf16[128,256]{1,0:T(8,128)(2,1)S(1)}, u32[]{:S(2)}, u32[]{:S(2)}) collective-permute-start(bf16[128,256]{1,0:T(8,128)(2,1)} %get-tuple-element.48), channel_id=1, source_target_pairs={{0,1},{1,2},{2,3},{4,5},{5,6},{6,7},{8,9},{9,10},{10,11},{12,13},{... | collective-permute-start | bytes 196616 | tf_op jit(solution)/shard_map/ppermute | solution.py:425
  118.5 1.9 %collective-permute-start.23 = (bf16[128,256]{1,0:T(8,128)(2,1)}, bf16[128,256]{1,0:T(8,128)(2,1)S(1)}, u32[]{:S(2)}, u32[]{:S(2)}) collective-permute-start(bf16[128,256]{1,0:T(8,128)(2,1)} %get-tuple-element.48), channel_id=1, source_target_pairs={{1,0},{2,1},{3,2},{5,4},{6,5},{7,6},{9,8},{10,9},{11,10},{13,12},{... | collective-permute-start | bytes 196616 | tf_op jit(solution)/shard_map/ppermute | solution.py:426
  120.4 3.4 %collective-permute-start.25 = (bf16[128,256]{1,0:T(8,128)(2,1)S(1)}, bf16[128,256]{1,0:T(8,128)(2,1)S(1)}, u32[]{:S(2)}, u32[]{:S(2)}) collective-permute-start(bf16[128,256]{1,0:T(8,128)(2,1)S(1)} %collective-permute-done.24), channel_id=1, source_target_pairs={{1,0},{2,3},{5,4},{6,7},{9,8},{10,11},{13,12},{14,15},{17,16},{18,... | collective-permute-start | bytes 196616 | tf_op jit(solution)/shard_map/ppermute | solution.py:428
  132.3 7.9 %attention.6 = (f32[768,128]{1,0:T(8,128)S(1)}, f32[768,256]{1,0:T(8,128)S(1)}, f32[512,128]{1,0:T(8,128)S(1)}, f32[512,256]{1,0:T(8,128)S(1)}, f32[256,128]{1,0:T(8,128)S(1)}, /*index=5*/f32[256,256]{1,0:T(8,128)S(1)}) custom-call(s32[3]{0:T(128)S(1)} %copy-done.36, s32[11]{0:T(128)S(1)} %pad_add_fusion.4.refs_1_, bf16[2,384,128]{2,1,0:T(8,128)(2,1)S(1)} %copy-done.16, ...), custom_call_target="tpu_custom_call" | custom-call | flops 1 | bytes 1 | tf_op jit(solution)/shard_map/attention/pallas_call | solution.py:258
  141.8 3.5 %attention.7 = (bf16[192,256]{1,0:T(8,128)(2,1)S(1)}, bf16[192,256]{1,0:T(8,128)(2,1)S(1)}, bf16[192,256]{1,0:T(8,128)(2,1)S(1)}, bf16[192,256]{1,0:T(8,128)(2,1)S(1)}) custom-call(s32[3]{0:T(128)S(1)} %copy-done.36, s32[5]{0:T(128)S(1)} %get-tuple-element.68.refs_1_, bf16[2,384,128]{2,1,0:T(8,128)(2,1)S(1)} %copy-done.16, ...), custom_call_target="tpu_custom_call" | custom-call | flops 1 | bytes 1 | tf_op jit(solution)/shard_map/attention/pallas_call | solution.py:258
  145.3 1.6 %collective-permute-start.30 = (bf16[192,256]{1,0:T(8,128)(2,1)S(1)}, bf16[192,256]{1,0:T(8,128)(2,1)S(1)}, u32[]{:S(2)}, u32[]{:S(2)}) collective-permute-start(bf16[192,256]{1,0:T(8,128)(2,1)S(1)} %get-tuple-element.58), channel_id=1, source_target_pairs={{0,4},{4,0},{8,12},{12,8},{1,5},{5,1},{9,13},{13,9},{2,6},{6,2},{1... | collective-permute-start | bytes 294920 | tf_op jit(solution)/shard_map/ppermute | solution.py:412
  146.9 1.7 %collective-permute-start.28 = (bf16[192,256]{1,0:T(8,128)(2,1)S(1)}, bf16[192,256]{1,0:T(8,128)(2,1)S(1)}, u32[]{:S(2)}, u32[]{:S(2)}) collective-permute-start(bf16[192,256]{1,0:T(8,128)(2,1)S(1)} %get-tuple-element.56), channel_id=1, source_target_pairs={{0,12},{4,8},{8,4},{12,0},{1,13},{5,9},{9,5},{13,1},{2,14},{6,10},... | collective-permute-start | bytes 294920 | tf_op jit(solution)/shard_map/ppermute | solution.py:412
  149.5 3.5 %output_near.1.refs_6_ = f32[192,4608]{1,0:T(8,128)S(1)} custom-call(bf16[192,256]{1,0:T(8,128)(2,1)S(1)} %get-tuple-element.57.refs_0_, bf16[192,256]{1,0:T(8,128)(2,1)S(1)} %collective-permute-done.30.refs_1_, bf16[256,4608]{1,0:T(8,128)(2,1)S(1)} %copy-done.5, bf16[256,4608]{1,0:T(8,128)(2,1)} %collective-permute-done.refs_3_), custom_call_target="tpu_custom_call" | custom-call | flops 1 | bytes 1 | tf_op jit(solution)/shard_map/output_near/pallas_call | solution.py:308
  153.6 6.1 %output_norm.1 = bf16[192,4608]{1,0:T(8,128)(2,1)} custom-call(s32[8]{0:T(128)S(1)} %stack.44.at, bf16[192,256]{1,0:T(8,128)(2,1)S(1)} %collective-permute-done.27.refs_0_, bf16[192,256]{1,0:T(8,128)(2,1)S(1)} %collective-permute-done.28.refs_1_, bf16[192,4608]{1,0:T(8,128)(2,1)S(1)} %copy-done.7, bf16[192,4608]{1,0:T(8,128)(2,1)S(1)} %copy-done.18, ...), custom_call_target="tpu_custom_call" | custom-call | flops 1 | bytes 1 | tf_op jit(solution)/shard_map/output_norm/pallas_call | solution.py:377
  (172 shorter events, 38.3 us)
Async XLA Ops:
  0.0 44.6 %collective-permute-start = (bf16[256,4608]{1,0:T(8,128)(2,1)}, bf16[256,4608]{1,0:T(8,128)(2,1)}, u32[]{:S(2)}, u32[]{:S(2)}) collective-permute-start(bf16[256,4608]{1,0:T(8,128)(2,1)} %refs_2_.3), channel_id=1, source_target_pairs={{0,4},{4,0},{8,12},{12,8},{1,5},{5,1},{9,13},{13,9},{2,6},{6,2},{1... | collective-permute-start | bytes 7077896 | tf_op jit(solution)/shard_map/ppermute | solution.py:412
  4.0 37.8 %collective-permute-start.1 = (bf16[64,4608]{1,0:T(8,128)(2,1)}, bf16[64,4608]{1,0:T(8,128)(2,1)}, u32[]{:S(2)}, u32[]{:S(2)}) collective-permute-start(bf16[64,4608]{1,0:T(8,128)(2,1)} %norm_rows.3.refs_0_), channel_id=1, source_target_pairs={{0,4},{4,0},{8,12},{12,8},{1,5},{5,1},{9,13},{13,9},{2,6},{6,2},{1... | collective-permute-start | bytes 1769480 | tf_op jit(solution)/shard_map/ppermute | solution.py:412
  4.4 40.8 %collective-permute-start.2 = (bf16[64,4608]{1,0:T(8,128)(2,1)S(1)}, bf16[64,4608]{1,0:T(8,128)(2,1)}, u32[]{:S(2)}, u32[]{:S(2)}) collective-permute-start(bf16[64,4608]{1,0:T(8,128)(2,1)S(1)} %norm_rows.4.refs_1_), channel_id=1, source_target_pairs={{0,4},{4,0},{8,12},{12,8},{1,5},{5,1},{9,13},{13,9},{2,6},{6,2},{1... | collective-permute-start | bytes 1769480 | tf_op jit(solution)/shard_map/ppermute | solution.py:412
  6.9 15.2 %collective-permute-start.4 = (bf16[64,4608]{1,0:T(8,128)(2,1)}, bf16[64,4608]{1,0:T(8,128)(2,1)}, u32[]{:S(2)}, u32[]{:S(2)}) collective-permute-start(bf16[64,4608]{1,0:T(8,128)(2,1)} %constant_dynamic-slice_fusion), channel_id=1, source_target_pairs={{0,8},{4,12},{8,0},{12,4},{1,9},{5,13},{9,1},{13,5},{2,10},{6,14},... | collective-permute-start | bytes 1769480 | tf_op jit(solution)/shard_map/ppermute | solution.py:412
  22.1 14.3 %collective-permute-start.7 = (bf16[64,4608]{1,0:T(8,128)(2,1)}, bf16[64,4608]{1,0:T(8,128)(2,1)S(1)}, u32[]{:S(2)}, u32[]{:S(2)}) collective-permute-start(bf16[64,4608]{1,0:T(8,128)(2,1)} %collective-permute-done.4), channel_id=1, source_target_pairs={{0,16},{16,0},{1,17},{17,1},{2,18},{18,2},{3,19},{19,3},{4,20},{20... | collective-permute-start | bytes 1769480 | tf_op jit(solution)/shard_map/ppermute | solution.py:417
  24.5 14.0 %collective-permute-start.8 = (bf16[64,4608]{1,0:T(8,128)(2,1)}, bf16[64,4608]{1,0:T(8,128)(2,1)}, u32[]{:S(2)}, u32[]{:S(2)}) collective-permute-start(bf16[64,4608]{1,0:T(8,128)(2,1)} %collective-permute-done.4), channel_id=1, source_target_pairs={{0,1},{1,0},{2,3},{3,2},{4,5},{5,4},{6,7},{7,6},{8,9},{9,8},{10,11... | collective-permute-start | bytes 1769480 | tf_op jit(solution)/shard_map/ppermute | solution.py:442
  36.4 8.8 %collective-permute-start.3 = (bf16[64,4608]{1,0:T(8,128)(2,1)}, bf16[64,4608]{1,0:T(8,128)(2,1)S(1)}, u32[]{:S(2)}, u32[]{:S(2)}) collective-permute-start(bf16[64,4608]{1,0:T(8,128)(2,1)} %norm_rows.5.refs_4_), channel_id=1, source_target_pairs={{0,4},{4,0},{8,12},{12,8},{1,5},{5,1},{9,13},{13,9},{2,6},{6,2},{1... | collective-permute-start | bytes 1769480 | tf_op jit(solution)/shard_map/ppermute | solution.py:412
  39.8 53.4 %collective-permute-start.15 = (bf16[192,4608]{1,0:T(8,128)(2,1)S(1)}, bf16[192,4608]{1,0:T(8,128)(2,1)S(1)}, u32[]{:S(2)}, u32[]{:S(2)}) collective-permute-start(bf16[192,4608]{1,0:T(8,128)(2,1)S(1)} %constant_dynamic-update-slice_fusion.2.refs_2_), channel_id=1, source_target_pairs={{0,4},{4,0},{8,12},{12,8},{1,5},{5,1},{9,13},{13,9},{2,6},{6,2},{1... | collective-permute-start | bytes 5308424 | tf_op jit(solution)/shard_map/ppermute | solution.py:412
  41.8 15.2 %collective-permute-start.5 = (bf16[64,4608]{1,0:T(8,128)(2,1)}, bf16[64,4608]{1,0:T(8,128)(2,1)S(1)}, u32[]{:S(2)}, u32[]{:S(2)}) collective-permute-start(bf16[64,4608]{1,0:T(8,128)(2,1)} %norm_rows.3.refs_0_), channel_id=1, source_target_pairs={{0,8},{4,12},{8,0},{12,4},{1,9},{5,13},{9,1},{13,5},{2,10},{6,14},... | collective-permute-start | bytes 1769480 | tf_op jit(solution)/shard_map/ppermute | solution.py:412
  44.6 39.2 %copy-start.40 = (f32[768,64]{1,0:T(8,128)}, f32[768,64]{1,0:T(8,128)S(1)}, u32[]{:S(2)}) copy-start(f32[768,64]{1,0:T(8,128)S(1)} %get-tuple-element.61) | copy-start | bytes 589828
  44.7 34.0 %collective-permute-start.6 = (bf16[64,4608]{1,0:T(8,128)(2,1)S(1)}, bf16[64,4608]{1,0:T(8,128)(2,1)S(1)}, u32[]{:S(2)}, u32[]{:S(2)}) collective-permute-start(bf16[64,4608]{1,0:T(8,128)(2,1)S(1)} %norm_rows.4.refs_1_), channel_id=1, source_target_pairs={{0,8},{4,12},{8,0},{12,4},{1,9},{5,13},{9,1},{13,5},{2,10},{6,14},... | collective-permute-start | bytes 1769480 | tf_op jit(solution)/shard_map/ppermute | solution.py:412
  57.1 7.8 %collective-permute-start.11 = (bf16[384,256]{1,0:T(8,128)(2,1)S(1)}, bf16[384,256]{1,0:T(8,128)(2,1)S(1)}, u32[]{:S(2)}, u32[]{:S(2)}) collective-permute-start(bf16[384,256]{1,0:T(8,128)(2,1)S(1)} %get-tuple-element.36), channel_id=1, source_target_pairs={{0,2},{1,3},{2,0},{3,1},{4,6},{5,7},{6,4},{7,5},{8,10},{9,11},{10,... | collective-permute-start | bytes 589832 | tf_op jit(solution)/shard_map/ppermute | solution.py:427
  57.1 16.1 %collective-permute-start.9 = (bf16[384,256]{1,0:T(8,128)(2,1)S(1)}, bf16[384,256]{1,0:T(8,128)(2,1)S(1)}, u32[]{:S(2)}, u32[]{:S(2)}) collective-permute-start(bf16[384,256]{1,0:T(8,128)(2,1)S(1)} %get-tuple-element.36), channel_id=1, source_target_pairs={{0,1},{1,2},{2,3},{4,5},{5,6},{6,7},{8,9},{9,10},{10,11},{12,13},{... | collective-permute-start | bytes 589832 | tf_op jit(solution)/shard_map/ppermute | solution.py:425
  60.3 13.4 %collective-permute-start.10 = (bf16[384,256]{1,0:T(8,128)(2,1)S(1)}, bf16[384,256]{1,0:T(8,128)(2,1)S(1)}, u32[]{:S(2)}, u32[]{:S(2)}) collective-permute-start(bf16[384,256]{1,0:T(8,128)(2,1)S(1)} %get-tuple-element.36), channel_id=1, source_target_pairs={{1,0},{2,1},{3,2},{5,4},{6,5},{7,6},{9,8},{10,9},{11,10},{13,12},{... | collective-permute-start | bytes 589832 | tf_op jit(solution)/shard_map/ppermute | solution.py:426
  64.9 10.9 %collective-permute-start.12 = (bf16[384,256]{1,0:T(8,128)(2,1)S(1)}, bf16[384,256]{1,0:T(8,128)(2,1)S(1)}, u32[]{:S(2)}, u32[]{:S(2)}) collective-permute-start(bf16[384,256]{1,0:T(8,128)(2,1)S(1)} %collective-permute-done.11), channel_id=1, source_target_pairs={{1,0},{2,3},{5,4},{6,7},{9,8},{10,11},{13,12},{14,15},{17,16},{18,... | collective-permute-start | bytes 589832 | tf_op jit(solution)/shard_map/ppermute | solution.py:428
  73.2 10.7 %collective-permute-start.13 = (bf16[64,4608]{1,0:T(8,128)(2,1)S(1)}, bf16[64,4608]{1,0:T(8,128)(2,1)S(1)}, u32[]{:S(2)}, u32[]{:S(2)}) collective-permute-start(bf16[64,4608]{1,0:T(8,128)(2,1)S(1)} %collective-permute-done.5.refs_0_), channel_id=1, source_target_pairs={{0,4},{4,0},{8,12},{12,8},{1,5},{5,1},{9,13},{13,9},{2,6},{6,2},{1... | collective-permute-start | bytes 1769480 | tf_op jit(solution)/shard_map/ppermute | solution.py:412
  78.7 5.3 %collective-permute-start.14 = (bf16[64,4608]{1,0:T(8,128)(2,1)S(1)}, bf16[64,4608]{1,0:T(8,128)(2,1)S(1)}, u32[]{:S(2)}, u32[]{:S(2)}) collective-permute-start(bf16[64,4608]{1,0:T(8,128)(2,1)S(1)} %collective-permute-done.6.refs_1_), channel_id=1, source_target_pairs={{0,4},{4,0},{8,12},{12,8},{1,5},{5,1},{9,13},{13,9},{2,6},{6,2},{1... | collective-permute-start | bytes 1769480 | tf_op jit(solution)/shard_map/ppermute | solution.py:412
  80.2 22.5 %collective-permute-start.16 = (bf16[64,4608]{1,0:T(8,128)(2,1)}, bf16[64,4608]{1,0:T(8,128)(2,1)}, u32[]{:S(2)}, u32[]{:S(2)}) collective-permute-start(bf16[64,4608]{1,0:T(8,128)(2,1)} %norm_rows.5.refs_4_), channel_id=1, source_target_pairs={{0,8},{4,12},{8,0},{12,4},{1,9},{5,13},{9,1},{13,5},{2,10},{6,14},... | collective-permute-start | bytes 1769480 | tf_op jit(solution)/shard_map/ppermute | solution.py:412
  83.4 19.2 %collective-permute-start.20 = (bf16[64,4608]{1,0:T(8,128)(2,1)}, bf16[64,4608]{1,0:T(8,128)(2,1)}, u32[]{:S(2)}, u32[]{:S(2)}) collective-permute-start(bf16[64,4608]{1,0:T(8,128)(2,1)} %collective-permute-done.8), channel_id=1, source_target_pairs={{0,16},{16,0},{1,17},{17,1},{2,18},{18,2},{3,19},{19,3},{4,20},{20... | collective-permute-start | bytes 1769480 | tf_op jit(solution)/shard_map/ppermute | solution.py:417
  87.3 15.4 %collective-permute-start.17 = (bf16[256,256]{1,0:T(8,128)(2,1)}, bf16[256,256]{1,0:T(8,128)(2,1)}, u32[]{:S(2)}, u32[]{:S(2)}) collective-permute-start(bf16[256,256]{1,0:T(8,128)(2,1)} %get-tuple-element.42), channel_id=1, source_target_pairs={{0,1},{1,2},{2,3},{4,5},{5,6},{6,7},{8,9},{9,10},{10,11},{12,13},{... | collective-permute-start | bytes 393224 | tf_op jit(solution)/shard_map/ppermute | solution.py:425
  91.2 11.5 %collective-permute-start.18 = (bf16[256,256]{1,0:T(8,128)(2,1)}, bf16[256,256]{1,0:T(8,128)(2,1)}, u32[]{:S(2)}, u32[]{:S(2)}) collective-permute-start(bf16[256,256]{1,0:T(8,128)(2,1)} %get-tuple-element.42), channel_id=1, source_target_pairs={{1,0},{2,1},{3,2},{5,4},{6,5},{7,6},{9,8},{10,9},{11,10},{13,12},{... | collective-permute-start | bytes 393224 | tf_op jit(solution)/shard_map/ppermute | solution.py:426
  94.4 8.3 %collective-permute-start.19 = (bf16[256,256]{1,0:T(8,128)(2,1)}, bf16[256,256]{1,0:T(8,128)(2,1)}, u32[]{:S(2)}, u32[]{:S(2)}) collective-permute-start(bf16[256,256]{1,0:T(8,128)(2,1)} %get-tuple-element.42), channel_id=1, source_target_pairs={{0,2},{1,3},{2,0},{3,1},{4,6},{5,7},{6,4},{7,5},{8,10},{9,11},{10,... | collective-permute-start | bytes 393224 | tf_op jit(solution)/shard_map/ppermute | solution.py:427
  102.7 8.4 %collective-permute-start.21 = (bf16[64,4608]{1,0:T(8,128)(2,1)}, bf16[64,4608]{1,0:T(8,128)(2,1)S(1)}, u32[]{:S(2)}, u32[]{:S(2)}) collective-permute-start(bf16[64,4608]{1,0:T(8,128)(2,1)} %collective-permute-done.16.refs_0_), channel_id=1, source_target_pairs={{0,4},{4,0},{8,12},{12,8},{1,5},{5,1},{9,13},{13,9},{2,6},{6,2},{1... | collective-permute-start | bytes 1769480 | tf_op jit(solution)/shard_map/ppermute | solution.py:412
  103.5 49.6 %collective-permute-start.29 = (bf16[64,4608]{1,0:T(8,128)(2,1)}, bf16[64,4608]{1,0:T(8,128)(2,1)}, u32[]{:S(2)}, u32[]{:S(2)}) collective-permute-start(bf16[64,4608]{1,0:T(8,128)(2,1)} %collective-permute-done.20.refs_4_), channel_id=1, source_target_pairs={{0,4},{4,0},{8,12},{12,8},{1,5},{5,1},{9,13},{13,9},{2,6},{6,2},{1... | collective-permute-start | bytes 1769480 | tf_op jit(solution)/shard_map/ppermute | solution.py:412
  106.2 17.7 %collective-permute-start.26 = (bf16[256,256]{1,0:T(8,128)(2,1)}, bf16[256,256]{1,0:T(8,128)(2,1)}, u32[]{:S(2)}, u32[]{:S(2)}) collective-permute-start(bf16[256,256]{1,0:T(8,128)(2,1)} %collective-permute-done.19), channel_id=1, source_target_pairs={{1,0},{2,3},{5,4},{6,7},{9,8},{10,11},{13,12},{14,15},{17,16},{18,... | collective-permute-start | bytes 393224 | tf_op jit(solution)/shard_map/ppermute | solution.py:428
  114.4 6.0 %collective-permute-start.24 = (bf16[128,256]{1,0:T(8,128)(2,1)}, bf16[128,256]{1,0:T(8,128)(2,1)S(1)}, u32[]{:S(2)}, u32[]{:S(2)}) collective-permute-start(bf16[128,256]{1,0:T(8,128)(2,1)} %get-tuple-element.48), channel_id=1, source_target_pairs={{0,2},{1,3},{2,0},{3,1},{4,6},{5,7},{6,4},{7,5},{8,10},{9,11},{10,... | collective-permute-start | bytes 196616 | tf_op jit(solution)/shard_map/ppermute | solution.py:427
  114.6 25.7 %collective-permute-start.22 = (bf16[128,256]{1,0:T(8,128)(2,1)}, bf16[128,256]{1,0:T(8,128)(2,1)S(1)}, u32[]{:S(2)}, u32[]{:S(2)}) collective-permute-start(bf16[128,256]{1,0:T(8,128)(2,1)} %get-tuple-element.48), channel_id=1, source_target_pairs={{0,1},{1,2},{2,3},{4,5},{5,6},{6,7},{8,9},{9,10},{10,11},{12,13},{... | collective-permute-start | bytes 196616 | tf_op jit(solution)/shard_map/ppermute | solution.py:425
  118.5 21.8 %collective-permute-start.23 = (bf16[128,256]{1,0:T(8,128)(2,1)}, bf16[128,256]{1,0:T(8,128)(2,1)S(1)}, u32[]{:S(2)}, u32[]{:S(2)}) collective-permute-start(bf16[128,256]{1,0:T(8,128)(2,1)} %get-tuple-element.48), channel_id=1, source_target_pairs={{1,0},{2,1},{3,2},{5,4},{6,5},{7,6},{9,8},{10,9},{11,10},{13,12},{... | collective-permute-start | bytes 196616 | tf_op jit(solution)/shard_map/ppermute | solution.py:426
  120.4 19.8 %collective-permute-start.25 = (bf16[128,256]{1,0:T(8,128)(2,1)S(1)}, bf16[128,256]{1,0:T(8,128)(2,1)S(1)}, u32[]{:S(2)}, u32[]{:S(2)}) collective-permute-start(bf16[128,256]{1,0:T(8,128)(2,1)S(1)} %collective-permute-done.24), channel_id=1, source_target_pairs={{1,0},{2,3},{5,4},{6,7},{9,8},{10,11},{13,12},{14,15},{17,16},{18,... | collective-permute-start | bytes 196616 | tf_op jit(solution)/shard_map/ppermute | solution.py:428
  145.3 4.2 %collective-permute-start.30 = (bf16[192,256]{1,0:T(8,128)(2,1)S(1)}, bf16[192,256]{1,0:T(8,128)(2,1)S(1)}, u32[]{:S(2)}, u32[]{:S(2)}) collective-permute-start(bf16[192,256]{1,0:T(8,128)(2,1)S(1)} %get-tuple-element.58), channel_id=1, source_target_pairs={{0,4},{4,0},{8,12},{12,8},{1,5},{5,1},{9,13},{13,9},{2,6},{6,2},{1... | collective-permute-start | bytes 294920 | tf_op jit(solution)/shard_map/ppermute | solution.py:412
  146.9 6.1 %collective-permute-start.27 = (bf16[192,256]{1,0:T(8,128)(2,1)S(1)}, bf16[192,256]{1,0:T(8,128)(2,1)S(1)}, u32[]{:S(2)}, u32[]{:S(2)}) collective-permute-start(bf16[192,256]{1,0:T(8,128)(2,1)S(1)} %get-tuple-element.55), channel_id=1, source_target_pairs={{0,8},{4,12},{8,0},{12,4},{1,9},{5,13},{9,1},{13,5},{2,10},{6,14},... | collective-permute-start | bytes 294920 | tf_op jit(solution)/shard_map/ppermute | solution.py:412
  146.9 6.6 %collective-permute-start.28 = (bf16[192,256]{1,0:T(8,128)(2,1)S(1)}, bf16[192,256]{1,0:T(8,128)(2,1)S(1)}, u32[]{:S(2)}, u32[]{:S(2)}) collective-permute-start(bf16[192,256]{1,0:T(8,128)(2,1)S(1)} %get-tuple-element.56), channel_id=1, source_target_pairs={{0,12},{4,8},{8,4},{12,0},{1,13},{5,9},{9,5},{13,1},{2,14},{6,10},... | collective-permute-start | bytes 294920 | tf_op jit(solution)/shard_map/ppermute | solution.py:412
  (46 other events, 415.4 us)

commit v4 on v0

v4 whole, which is shorter than its diff:
```python
import functools
import math

import jax
import jax.numpy as jnp
from jax import lax
from jax.experimental import pallas as pl
from jax.experimental.pallas import tpu as pltpu
from jax.sharding import PartitionSpec as P

HD = 128
ATT_SCALAR = 144
EPS = 1e-6
MIB = 1024 * 1024
HIDDEN = -1e30
COST = pl.CostEstimate(flops=1, bytes_accessed=1, transcendentals=0)

ANY = pl.BlockSpec(memory_space=pl.ANY)
HBM = pl.BlockSpec(memory_space=pltpu.HBM)
VMEM = pl.BlockSpec(memory_space=pltpu.VMEM)
SMEM = pl.BlockSpec(memory_space=pltpu.SMEM)


class Came:
    def __init__(self, array):
        self.array, self.shape = array, array.shape


def call(kernel, name, mib, in_specs, out_shape, scratch, *args, out=HBM):
    in_specs, pinned = list(in_specs), []
    for at, arg in enumerate(args):
        if isinstance(arg, Came):
            arg, in_specs[at] = arg.array, ANY
        elif in_specs[at] is not SMEM:
            arg = pltpu.with_memory_space_constraint(arg, in_specs[at].memory_space)
        pinned.append(arg)
    return pl.pallas_call(
        kernel,
        in_specs=in_specs,
        out_specs=[out] * len(out_shape),
        out_shape=[out.memory_space(shape, dtype) for shape, dtype in out_shape],
        scratch_shapes=scratch,
        compiler_params=pltpu.CompilerParams(vmem_limit_bytes=mib * MIB),
        cost_estimate=COST,
        name=name,
    )(*pinned)


class Copies:
    def __init__(self, semaphores):
        self.semaphores, self.used = semaphores, 0

    def start(self, source, target):
        copy = pltpu.make_async_copy(source, target, self.semaphores.at[self.used])
        self.used += 1
        copy.start()
        return copy


def norm_kernel(cuts, pieces, table, hidden, gain, w_out, *refs):
    whole, parts = refs[0], refs[1 : 1 + len(cuts)]
    w_piece, rows, staged, semaphores = refs[1 + len(cuts) :]
    copies = Copies(semaphores)
    count, width = hidden.shape
    step = count // pieces
    spans = [pl.ds(at * step, step) for at in range(pieces)]
    ins = [copies.start(hidden.at[span], rows.at[span]) for span in spans]
    size = w_piece.shape[0]
    first = pl.multiple_of(table[1] * size, size)
    outs = [copies.start(w_out.at[pl.ds(first, size)], w_piece)]
    scale = gain[...]
    for at, span in enumerate(spans):
        ins[at].wait()
        x = rows[span, :].astype(jnp.float32)
        square = x * x
        folded = square[:, :128]
        for lane in range(128, width, 128):
            folded = folded + square[:, lane : lane + 128]
        mean = jnp.sum(folded, axis=1, keepdims=True) / width
        staged[span, :] = (x * lax.rsqrt(mean + EPS) * scale).astype(jnp.bfloat16)
        outs.append(copies.start(staged.at[span], whole.at[span]))
        begin = 0
        for cut, part in zip(cuts, parts):
            if begin <= at * step < begin + cut:
                inside = pl.ds(at * step - begin, step)
                outs.append(copies.start(staged.at[span], part.at[inside]))
            begin += cut
    for copy in outs:
        copy.wait()


def norm(table, hidden, gain, w_out, cuts, share, pieces=3):
    rows, width = hidden.shape
    bf16 = jnp.bfloat16
    out_shape = [((rows, width), bf16)] + [((cut, width), bf16) for cut in cuts]
    return call(
        functools.partial(norm_kernel, cuts, pieces),
        "norm_rows",
        12,
        [SMEM, HBM, VMEM, HBM],
        out_shape + [((share, width), bf16)],
        [
            pltpu.VMEM((rows, width), bf16),
            pltpu.VMEM((rows, width), bf16),
            pltpu.SemaphoreType.DMA((1 + 3 * pieces,)),
        ],
        table,
        hidden,
        gain.reshape(1, -1),
        w_out,
    )


def qkv_kernel(runs, first, chunks, *refs):
    parts = refs[: len(runs)]
    wq, wk, wv, trig, q_out, kv_out = refs[len(runs) : len(runs) + 6]
    rows, weights, angles, q, kv, semaphores = refs[len(runs) + 6 :]
    copies = Copies(semaphores)
    total, width = rows.shape
    depth = width // chunks
    queries = wq.shape[1]
    waits = []
    for chunk in range(chunks):
        lanes = pl.ds(chunk * depth, depth)
        here, put = [], 0
        for part, (begin, count) in zip(parts, runs):
            source = part.at[pl.ds(begin, count), lanes]
            here.append(copies.start(source, rows.at[pl.ds(put, count), lanes]))
            put += count
        column = 0
        for weight in (wq, wk, wv):
            target = weights.at[lanes, pl.ds(column, weight.shape[1])]
            here.append(copies.start(weight.at[lanes], target))
            column += weight.shape[1]
        waits.append(here)
    waits[-1].append(copies.start(trig.at[pl.ds(first, total)], angles))
    product = None
    for chunk in range(chunks):
        for copy in waits[chunk]:
            copy.wait()
        lanes = slice(chunk * depth, (chunk + 1) * depth)
        term = jnp.dot(rows[:, lanes], weights[lanes, :], preferred_element_type=jnp.float32)
        product = term if product is None else product + term
    cos, sin = angles[:, :HD], angles[:, HD:]

    def rotated(at):
        y = product[:, at : at + HD]
        return y * cos + pltpu.roll(y, HD // 2, 1) * sin

    factor = ATT_SCALAR ** (-0.5) * math.log2(math.e)
    kv[:, :HD] = rotated(queries).astype(jnp.bfloat16)
    kv[:, HD:] = product[:, queries + HD :].astype(jnp.bfloat16)
    outs = [copies.start(kv, kv_out)]
    for head in range(queries // HD):
        q[head] = (rotated(head * HD) * factor).astype(jnp.bfloat16)
    outs.append(copies.start(q, q_out))
    for copy in outs:
        copy.wait()


def qkv(parts, weights, trig, first, chunks=4):
    total = sum(count for _, _, count in parts)
    width, queries = weights[0].shape
    bf16 = jnp.bfloat16
    heads = queries // HD
    runs = [(begin, count) for _, begin, count in parts]
    return call(
        functools.partial(qkv_kernel, runs, first, chunks),
        "qkv",
        24,
        [HBM] * (len(parts) + 4),
        [((heads, total, HD), bf16), ((total, 2 * HD), bf16)],
        [
            pltpu.VMEM((total, width), bf16),
            pltpu.VMEM((width, queries + 2 * HD), bf16),
            pltpu.VMEM((total, 2 * HD), jnp.float32),
            pltpu.VMEM((heads, total, HD), bf16),
            pltpu.VMEM((total, 2 * HD), bf16),
            pltpu.SemaphoreType.DMA((chunks * (len(parts) + 3) + 3,)),
        ],
        *[array for array, _, _ in parts],
        *weights,
        trig,
    )


class Step:
    def __init__(self, q, group, slots, same=None, merged=False):
        self.q, self.group, self.slots = q, group, slots
        self.same, self.merged = same, merged


class Chunk:
    def __init__(self, at, runs, share):
        self.at, self.runs, self.share = at, runs, share

    def places(self, core, axis, first, size):
        shape = (size, 1) if axis == 0 else (1, size)
        index = first + lax.broadcasted_iota(jnp.int32, shape, axis)
        result, begin = index, 0
        for which, offset, rows in self.runs:
            base = (core if which == 0 else 1 - core) * self.share + offset - begin
            inside = (index >= begin) & (index < begin + rows)
            result = jnp.where(inside, index + base, result)
            begin += rows
        return result


def attention_kernel(plan, q_chunks, k_chunks, group_parts, fresh, final, table, *refs):
    refs = list(refs)
    take = lambda n: [refs.pop(0) for _ in range(n)]
    count = len(q_chunks)
    q_refs = take(count)
    kv_parts = [take(n) for n in group_parts]
    old = {q: take(2) for q in range(count) if q not in fresh}
    outs = take(len(final) if final else 2 * count)
    qs, kvs = take(count), take(len(group_parts))
    if final:
        states, staged = [take(2) for _ in range(count)], take(len(final))
    else:
        states = [outs[2 * q : 2 * q + 2] for q in range(count)]
    (semaphores,) = refs
    copies = Copies(semaphores)
    core = table[0]
    waits = {}
    for at, (source, target) in enumerate(zip(q_refs, qs)):
        waits["q", at] = [copies.start(source, target)]
    for group, (parts, kv) in enumerate(zip(kv_parts, kvs)):
        each = kv.shape[0] // len(parts)
        waits["kv", group] = [
            copies.start(part, kv.at[pl.ds(slot * each, each)])
            for slot, part in enumerate(parts)
        ]
    def ready(*key):
        for copy in waits.pop(key, []):
            copy.wait()

    def attend(q, keys_values, begin, visible=None, bias=None):
        q_ref, (peak, acc) = qs[q], states[q]
        heads, rows, _ = q_ref.shape
        keys, values = keys_values[:, :HD], keys_values[:, HD:]
        values = jnp.concatenate([values, jnp.ones_like(values)], axis=1)
        count = keys.shape[0]
        tile = min(rows, 128)
        for first in range(0, rows, tile):
            q_tile = q_ref[:, first : first + tile, :].reshape(heads * tile, HD)
            scores = lax.dot_general(
                q_tile, keys, (((1,), (1,)), ((), ())), preferred_element_type=jnp.float32
            )
            if visible is not None:
                seen = jnp.concatenate([visible(first, tile)] * heads, axis=0)
                scores = jnp.where(seen, scores, HIDDEN)
            if bias is not None:
                scores = scores + bias
            top = jnp.max(scores, axis=1, keepdims=True)
            top = jnp.broadcast_to(top, (heads * tile, HD))
            span = pl.ds(first * heads, heads * tile)
            if not begin:
                before = peak[span, :]
                top = jnp.maximum(before, top)
            wide = jnp.concatenate([top] * (count // HD), axis=1)
            weights = jnp.exp2(scores - wide).astype(jnp.bfloat16)
            summed = jnp.dot(weights, values, preferred_element_type=jnp.float32)
            if not begin:
                fade = jnp.exp2(before - top)
                summed = summed + acc[span, :] * jnp.concatenate([fade, fade], axis=1)
            acc[span, :] = summed
            peak[span, :] = top

    begun = set(range(count)) - set(fresh)
    for q, held in old.items():
        for source, target in zip(held, states[q]):
            target[...] = source[...]
    for step in plan:
        q, group, kv = step.q, step.group, kvs[step.group]
        q_chunk, k_chunk = q_chunks[q], k_chunks[group]
        ready("q", q)
        ready("kv", group)
        if step.same is not None:
            keys_at = k_chunk.places(core, 1, 0, kv.shape[1])
            visible = lambda first, tile: keys_at <= q_chunk.places(core, 0, first, tile)
            attend(q, kv[step.same], q not in begun, visible=visible)
            begun.add(q)
        start = table[q_chunk.at]
        slots = step.slots
        if not slots:
            continue
        if step.merged:
            shown = [table[k_chunk.at + slot] < start for slot in slots]

            @pl.when(functools.reduce(jnp.logical_or, shown))
            def _():
                rows = kv.shape[1]
                bias = [
                    jnp.where(see, 0.0, HIDDEN) * jnp.ones((1, rows), jnp.float32)
                    for see in shown
                ]
                keys_values = kv[slots[0] : slots[-1] + 1].reshape(len(slots) * rows, 2 * HD)
                attend(q, keys_values, False, bias=jnp.concatenate(bias, axis=1))

        else:

            def one(slot, carry):
                @pl.when(table[k_chunk.at + slot] < start)
                def _():
                    attend(q, kv[slot], False)

                return carry

            lax.fori_loop(slots[0], slots[-1] + 1, one, 0)

    stores = []
    if final:
        for out, stage, spans in zip(outs, staged, final):
            put = 0
            for q, first, rows in spans:
                acc = states[q][1]
                heads, q_rows, _ = qs[q].shape
                tile = min(q_rows, 128)
                size = min(tile, rows)
                for head in range(heads):
                    for at in range(first, first + rows, size):
                        begin = at // tile * tile * heads + head * tile + at % tile
                        part = acc[begin : begin + size, :]
                        to = put + at - first
                        stage[to : to + size, head * HD : (head + 1) * HD] = (
                            part[:, :HD] / part[:, HD:]
                        ).astype(jnp.bfloat16)
                put += rows
            stores.append(copies.start(stage, out))
    for copy in stores:
        copy.wait()


def attention(plan, table, qs, q_chunks, groups, k_chunks, state, final=None):
    fresh = [at for at, held in enumerate(state) if held is None]
    held = [array for pair in state if pair is not None for array in pair]
    shapes = []
    for q in qs:
        heads, rows, _ = q.shape
        shapes += [(heads * rows, HD), (heads * rows, 2 * HD)]
    if final:
        width = qs[0].shape[0] * HD
        sums = [sum(rows for _, _, rows in spans) for spans in final]
        out_shape = [((rows, width), jnp.bfloat16) for rows in sums]
    else:
        out_shape = [(shape, jnp.float32) for shape in shapes]
    scratch = [pltpu.VMEM(q.shape, jnp.bfloat16) for q in qs]
    for parts in groups:
        slots = sum(part.shape[0] for part in parts)
        scratch.append(pltpu.VMEM((slots,) + parts[0].shape[1:], jnp.bfloat16))
    if final:
        scratch += [pltpu.VMEM(shape, jnp.float32) for shape in shapes]
        scratch += [pltpu.VMEM(shape, dtype) for shape, dtype in out_shape]
    parts = [part for parts in groups for part in parts]
    inputs = [*qs, *parts]
    sizes = [len(parts) for parts in groups]
    results = call(
        functools.partial(attention_kernel, plan, q_chunks, k_chunks, sizes, fresh, final),
        "attention",
        20,
        [SMEM] + [HBM] * len(inputs) + [VMEM] * len(held),
        out_shape,
        scratch + [pltpu.SemaphoreType.DMA((len(inputs) + len(out_shape),))],
        table,
        *inputs,
        *held,
        out=HBM if final else VMEM,
    )
    if final:
        return results
    return [tuple(results[2 * at : 2 * at + 2]) for at in range(len(qs))]


def fetch(copies, lefts, left, pieces, weights, chunks):
    columns = lefts[0].shape[1]
    depth, width = pieces[0].shape
    step = width // chunks
    first = [
        copies.start(part, left.at[:, pl.ds(at * columns, columns)])
        for at, part in enumerate(lefts)
    ]
    waits = []
    for chunk in range(chunks):
        lanes = pl.ds(chunk * step, step)
        waits.append(
            [
                copies.start(piece.at[:, lanes], weights.at[pl.ds(at * depth, depth), lanes])
                for at, piece in enumerate(pieces)
            ]
        )
    waits[0] += first
    return waits


def near_kernel(chunks, *refs):
    lefts, pieces = refs[:2], refs[2:4]
    out, left, weights, semaphores = refs[4:]
    copies = Copies(semaphores)
    waits = fetch(copies, lefts, left, pieces, weights, chunks)
    step = out.shape[1] // chunks
    for chunk in range(chunks):
        for copy in waits[chunk]:
            copy.wait()
        lanes = pl.ds(chunk * step, step)
        out[:, lanes] = jnp.dot(
            left[...], weights[:, lanes], preferred_element_type=jnp.float32
        ).astype(jnp.bfloat16)


def output_near(lefts, pieces, chunks=6):
    (rows, columns), (depth, width) = lefts[0].shape, pieces[0].shape
    bf16 = jnp.bfloat16
    return call(
        functools.partial(near_kernel, chunks),
        "output_near",
        16,
        [HBM] * 4,
        [((rows, width), bf16)],
        [
            pltpu.VMEM((rows, 2 * columns), bf16),
            pltpu.VMEM((2 * depth, width), bf16),
            pltpu.SemaphoreType.DMA((2 + 2 * chunks,)),
        ],
        *lefts,
        *pieces,
        out=VMEM,
    )[0]


def output_kernel(chunks, *refs):
    lefts, pieces = refs[:2], refs[2:4]
    hidden, near, gain, out, left, weights, held, projected, semaphores = refs[4:]
    copies = Copies(semaphores)
    waits = fetch(copies, lefts, left, pieces, weights, chunks)
    width = hidden.shape[1]
    step = width // chunks
    late = copies.start(hidden, held)
    square = jnp.zeros((hidden.shape[0], 128), jnp.float32)
    for chunk in range(chunks):
        for copy in waits[chunk]:
            copy.wait()
        lanes = pl.ds(chunk * step, step)
        total = near[:, lanes].astype(jnp.float32) + jnp.dot(
            left[...], weights[:, lanes], preferred_element_type=jnp.float32
        )
        projected[:, lanes] = total
        for lane in range(0, step, 128):
            part = total[:, lane : lane + 128]
            square = square + part * part
    mean = jnp.sum(square, axis=1, keepdims=True) / width
    scale = lax.rsqrt(mean + EPS)
    late.wait()
    stores = []
    for chunk in range(chunks):
        lanes = pl.ds(chunk * step, step)
        normed = projected[:, lanes] * scale * gain[:, lanes]
        held[:, lanes] = (held[:, lanes].astype(jnp.float32) + normed).astype(jnp.bfloat16)
        stores.append(copies.start(held.at[:, lanes], out.at[:, lanes]))
    for store in stores:
        store.wait()


def output(lefts, pieces, near, hidden, gain, chunks=6):
    rows, width = hidden.shape
    columns, depth = lefts[0].shape[1], pieces[0].shape[0]
    bf16 = jnp.bfloat16
    return call(
        functools.partial(output_kernel, chunks),
        "output_norm",
        24,
        [HBM] * 5 + [VMEM] * 2,
        [((rows, width), bf16)],
        [
            pltpu.VMEM((rows, 2 * columns), bf16),
            pltpu.VMEM((2 * depth, width), bf16),
            pltpu.VMEM((rows, width), bf16),
            pltpu.VMEM((rows, width), jnp.float32),
            pltpu.SemaphoreType.DMA((3 + 3 * chunks,)),
        ],
        *lefts,
        *pieces,
        hidden,
        near,
        gain,
    )[0]


def rotary_table(positions):
    half = HD // 2
    frequency = jnp.power(
        jnp.float32(10000.0), -jnp.arange(half, dtype=jnp.float32) * (2.0 / HD)
    )
    angles = positions.astype(jnp.float32)[:, None] * frequency[None, :]
    cos, sin = jnp.cos(angles), jnp.sin(angles)
    return jnp.concatenate([cos, cos, -sin, sin], axis=1)


def lookup(block_of, index):
    ids = jnp.arange(block_of.shape[0], dtype=jnp.int32)
    return jnp.sum(jnp.where(index[..., None] == ids, block_of, 0), axis=-1)


def flipped(array, axis, bit):
    size = lax.axis_size(axis)
    return lax.ppermute(array, axis, [(i, i ^ bit) for i in range(size)])


def along_line(array):
    size = lax.axis_size("seq")
    parts = [array[None]]
    for by in range(1, size):
        part = lax.ppermute(array, "seq", [(i, (i + by) % size) for i in range(size)])
        parts.append(Came(part[None]))
    return parts


def after(array, *others):
    return lax.optimization_barrier((array, *others))[0]


def two_chips(hidden, pre_gain, post_gain, wq, wk, wv, w_out, block_of):
    rows = hidden.shape[0]
    block_rows = 2 * rows
    cuts = [rows // 3 * 2, rows // 3]
    lines, groups = lax.axis_size("seq"), lax.axis_size("groups")
    seq, tp, group = lax.axis_index("seq"), lax.axis_index("tp"), lax.axis_index("groups")
    chip, core = tp // 2, tp % 2

    line = (seq - jnp.arange(lines, dtype=jnp.int32)) % lines
    near_starts = lookup(block_of, 2 * line + chip) * block_rows
    far_starts = lookup(block_of, 2 * line + 1 - chip) * block_rows
    scalars = jnp.stack([core, group * lines + seq]).astype(jnp.int32)
    table = jnp.concatenate([scalars, near_starts, far_starts])
    near_at, far_at = 2, 2 + lines

    share = w_out.shape[0] // (groups * lines)
    own, own_head, own_tail, w_piece = norm(table, hidden, pre_gain, w_out, cuts, share)
    partner = flipped(own, "tp", 1)
    w_piece = flipped(w_piece, "tp", 2)
    head, tail = flipped(own_head, "tp", 2), flipped(own_tail, "tp", 2)
    w_partner = flipped(w_out, "tp", 1)
    w_far = lax.all_gather(after(w_piece, partner), ("groups", "seq"), axis=0, tiled=True)

    run = [jnp.arange(size, dtype=jnp.int32) for size in cuts]
    place = [core * rows + run[0], (1 - core) * rows + run[0]]
    place += [core * rows + cuts[0] + run[1], (1 - core) * rows + cuts[0] + run[1]]
    place = jnp.concatenate(place)
    trig = rotary_table(jnp.concatenate([near_starts[0] + place, far_starts[0] + place]))
    weights = [wq, wk, wv]
    head_runs = [(0, 0, cuts[0]), (1, 0, cuts[0])]
    tail_runs = [(0, cuts[0], cuts[1]), (1, cuts[0], cuts[1])]
    near_chunk = Chunk(near_at, head_runs + tail_runs, rows)
    head_chunk, tail_chunk = Chunk(far_at, head_runs, rows), Chunk(far_at, tail_runs, rows)
    others, everyone = list(range(1, lines)), list(range(lines))

    q_near, kv_near = qkv(
        [
            (own, 0, cuts[0]),
            (Came(partner), 0, cuts[0]),
            (own, cuts[0], cuts[1]),
            (Came(partner), cuts[0], cuts[1]),
        ],
        weights,
        trig,
        0,
    )
    near = along_line(kv_near)
    (near_state,) = attention(
        [Step(0, 0, others, same=0)], table, [q_near], [near_chunk], [near], [near_chunk], [None]
    )

    head = after(head, *near_state, w_partner)
    q_head, kv_head = qkv(
        [(Came(head), 0, cuts[0]), (Came(flipped(head, "tp", 1)), 0, cuts[0])],
        weights,
        trig,
        block_rows,
    )
    far_head = along_line(kv_head)
    (head_state,) = attention(
        [Step(0, 1, [], same=0), Step(0, 0, everyone)],
        table,
        [q_head],
        [head_chunk],
        [near, far_head[:1]],
        [near_chunk, head_chunk],
        [None],
    )

    tail = after(tail, *head_state, *[part.array for part in far_head[1:]])
    q_tail, kv_tail = qkv(
        [(Came(tail), 0, cuts[1]), (Came(flipped(tail, "tp", 1)), 0, cuts[1])],
        weights,
        trig,
        block_rows + 2 * cuts[0],
    )
    far_tail = along_line(kv_tail)
    qs, q_chunks = [q_near, q_head, q_tail], [near_chunk, head_chunk, tail_chunk]
    state = attention(
        [
            Step(2, 2, [], same=0),
            Step(2, 0, everyone),
            Step(2, 1, others, same=0),
            Step(0, 1, everyone),
            Step(1, 1, others),
        ],
        table,
        qs,
        q_chunks,
        [near, far_head, far_tail[:1]],
        [near_chunk, head_chunk, tail_chunk],
        [near_state, head_state, None],
    )
    first = 2 * cuts[0]
    to = lambda half: [(0, half * cuts[0], cuts[0]), (0, first + half * cuts[1], cuts[1])]
    over = lambda half: [(1, half * cuts[0], cuts[0]), (2, half * cuts[1], cuts[1])]
    mine, partners, same, cross = attention(
        [
            Step(1, 0, others, same=0, merged=True),
            Step(2, 0, others, merged=True),
            Step(0, 0, everyone, merged=True),
        ],
        table,
        qs,
        q_chunks,
        [far_tail],
        [tail_chunk],
        state,
        final=[to(0), to(1), over(0), over(1)],
    )
    cross, same = flipped(cross, "tp", 3), flipped(same, "tp", 2)
    near_sum = output_near([mine, Came(flipped(partners, "tp", 1))], [w_out, Came(w_partner)])
    w_cross = flipped(after(w_far, mine), "tp", 1)
    return output(
        [Came(same), Came(cross)],
        [Came(w_far), Came(w_cross)],
        near_sum,
        hidden,
        post_gain.reshape(1, -1),
    )


def any_count(hidden, pre_gain, post_gain, wq, wk, wv, w_out, block_of):
    rows = hidden.shape[0]
    lines = lax.axis_size("seq")
    line = (lax.axis_index("seq") - jnp.arange(lines, dtype=jnp.int32)) % lines
    block = (2 * line[:, None] + jnp.arange(2, dtype=jnp.int32)).reshape(-1)
    block_rows = rows * lax.axis_size("tp") // 2
    starts = lookup(block_of, block) * block_rows
    table = jnp.concatenate([jnp.zeros(2, jnp.int32), starts])
    normed = norm(table, hidden, pre_gain, w_out, [], 16, 1)[0]
    normed = lax.all_gather(normed, "tp", axis=0, tiled=True)
    place = jnp.arange(block_rows, dtype=jnp.int32)
    trig = rotary_table((starts[:2, None] + place).reshape(-1))
    qs, keys_values = [], []
    for at in range(2):
        first = at * block_rows
        q, kv = qkv([(normed, first, block_rows)], [wq, wk, wv], trig, first)
        qs.append(q)
        keys_values.append(kv)
    kv = lax.all_gather(jnp.stack(keys_values), "seq")[line].reshape(-1, block_rows, 2 * HD)
    rest = list(range(2, 2 * lines))
    runs = [(0, 0, block_rows)]
    attended = attention(
        [Step(0, 0, [1], same=0), Step(1, 0, [0], same=1), Step(0, 0, rest), Step(1, 0, rest)],
        table,
        qs,
        [Chunk(2, runs, 0), Chunk(3, runs, 0)],
        [[kv]],
        [Chunk(2, runs, 0)],
        [None, None],
        final=[[(0, 0, block_rows), (1, 0, block_rows)]],
    )[0]
    partial = jnp.dot(attended, w_out, preferred_element_type=jnp.float32)
    summed = lax.psum_scatter(
        partial.astype(jnp.bfloat16), "tp", scatter_dimension=0, tiled=True
    ).astype(jnp.float32)
    mean = jnp.mean(summed * summed, axis=-1, keepdims=True)
    projected = summed * lax.rsqrt(mean + EPS) * post_gain
    return (hidden.astype(jnp.float32) + projected).astype(jnp.bfloat16)


def solution(mesh):
    return jax.shard_map(
        two_chips if mesh.shape["tp"] == 4 else any_count,
        mesh=mesh,
        in_specs=(
            P(("groups", "seq", "tp"), None),
            P(),
            P(),
            P(None, "tp"),
            P(None, "tp"),
            P(None, "tp"),
            P("tp", None),
            P(),
        ),
        out_specs=P(("groups", "seq", "tp"), None),
        check_vma=False,
    )
```

time: 273 us -> 146 us (0.53)
  matrix products: 67.3 us -> 0 us
  waiting for transfers between devices: 113 us -> 50.3 us
  Pallas kernels: 0 us -> 53.2 us
  blocking collectives: 38.7 us -> 0 us
  starting transfers between devices: 0.04 us -> 24.6 us
  other arithmetic: 22.2 us -> 3.85 us
  local copies, waits for them, and re-layouts: 11.8 us -> 1.48 us
  loops' own time: 5.53 us -> 0 us
    dot_general x20 -> x0, matrix products: 67.3 us -> none  [the longest x8 24 us: update(): jnp.einsum('qhd,kd->hqk', queries, keys_block, preferred_element_type=jnp...]
    reduce_scatter x1 -> x0, waiting for transfers between devices: 62.6 us -> none  [body(): lax.psum_scatter(jnp.dot(attended, w_out, preferred_element_type=jnp.floa...]
    pallas_call x0 -> x10, Pallas kernels: none -> 53.2 us  [call(): pl.pallas_call(kernel, in_specs=in_specs, out_specs=[out] * len(out_shape...]
    all_gather x1, waiting for transfers between devices: 50.4 us -> 0.02 us  [two_chips(): lax.all_gather(after(w_piece, partner), ('groups', 'seq'), axis=0, tiled=...]
    ppermute x0 -> x20, waiting for transfers between devices: none -> 50.3 us  [the longest x9 34.1 us: along_line(): lax.ppermute(array, 'seq', [(i, (i + by) % size) for i in range(size)])]
    all_gather x2 -> x0, blocking collectives: 38.7 us -> none  [the longest x1 19.9 us: body(): lax.all_gather(keys_local, 'seq', axis=0, tiled=True)]
    ppermute x0 -> x20, starting transfers between devices: none -> 24.6 us  [the longest x9 17.3 us: along_line(): lax.ppermute(array, 'seq', [(i, (i + by) % size) for i in range(size)])]
    reduce_sum x19 -> x1, other arithmetic: 8.76 us -> 0.87 us  [lookup(): return jnp.sum(jnp.where(index[..., None] == ids, block_of, 0), axis=-1)]
  transfers between devices with their start and end apart: 2 -> 21, of which waited for: 2 -> 9; matrix products, arithmetic and copies ran while one was open for 1% -> 2% of each run, Pallas kernels for 0% -> 26%
where the time goes in v4:
time: 146 us; the launch traced here: 147 us
  Pallas kernels  53.2 us (36%)
  waiting for transfers between devices  50.3 us (34%)
  starting transfers between devices  24.6 us (17%)
  between operations  13.7 us (9%)
  other arithmetic  3.85 us (3%)
  local copies, waits for them, and re-layouts  1.48 us (1%)
    pallas_call x10, Pallas kernels, call(): pl.pallas_call(kernel, in_specs=in_specs, out_specs=[out] * len(out_shape...  53.2 us
    ppermute x9, waiting for transfers between devices, along_line(): lax.ppermute(array, 'seq', [(i, (i + by) % size) for i in range(size)])  34.1 us
    ppermute x9, starting transfers between devices, along_line(): lax.ppermute(array, 'seq', [(i, (i + by) % size) for i in range(size)])  17.3 us
    ppermute x11, waiting for transfers between devices, flipped(): return lax.ppermute(array, axis, [(i, i ^ bit) for i in range(size)])  16.2 us
    ppermute x11, starting transfers between devices, flipped(): return lax.ppermute(array, axis, [(i, i ^ bit) for i in range(size)])  7.34 us
  transfers between devices with their start and end apart: 21, of which 9 were waited for; matrix products, arithmetic and copies ran while one was open for 2% of the time, Pallas kernels for 26%

profile of v4, /device:TPU:0, one launch (start us, length us, event | category | flops | bytes accessed | tf_op | source)
XLA Modules:
  0.0 147.1 jit_solution(3294374053784220422)
XLA Ops:
  6.6 0.9 select_reduce_fusion.1
  8.3 10.7 %norm_rows.1 = (bf16[192,4608]{1,0:T(8,128)(2,1)}, bf16[128,4608]{1,0:T(8,128)(2,1)}, bf16[64,4608]{1,0:T(8,128)(2,1)}, bf16[32,4608]{1,0:T(8,128)(2,1)}) custom-call(s32[10]{0:T(128)S(1)} %pad_add_fusion.1.table, bf16[192,4608]{1,0:T(8,128)(2,1)} %refs_4_.7, f32[1,4608]{1,0:T(1,128)S(1)} %reshape.68.gain, bf16[256,4608]{1,0:T(8,128)(2,1)} %refs_2_.5), custom_call_target="tpu_custom_call" | custom-call | flops 1 | bytes 1 | tf_op jit(solution)/shard_map/norm_rows/pallas_call | solution.py:37
  19.5 2.6 %collective-permute-start.17 = (bf16[32,4608]{1,0:T(8,128)(2,1)}, bf16[32,4608]{1,0:T(8,128)(2,1)S(1)}, u32[]{:S(2)}, u32[]{:S(2)}) collective-permute-start(bf16[32,4608]{1,0:T(8,128)(2,1)} %get-tuple-element.56), channel_id=1, source_target_pairs={{0,8},{4,12},{8,0},{12,4},{1,9},{5,13},{9,1},{13,5},{2,10},{6,14},... | collective-permute-start | bytes 884744 | tf_op jit(solution)/shard_map/ppermute | solution.py:506
  22.2 7.6 %collective-permute-done.17 = bf16[32,4608]{1,0:T(8,128)(2,1)S(1)} collective-permute-done((bf16[32,4608]{1,0:T(8,128)(2,1)}, bf16[32,4608]{1,0:T(8,128)(2,1)S(1)}, u32[]{:S(2)}, u32[]{:S(2)}) %collective-permute-start.17) | collective-permute-done | bytes 294944 | tf_op jit(solution)/shard_map/ppermute | solution.py:506
  30.6 1.8 %collective-permute-start.1 = (bf16[128,4608]{1,0:T(8,128)(2,1)}, bf16[128,4608]{1,0:T(8,128)(2,1)S(1)}, u32[]{:S(2)}, u32[]{:S(2)}) collective-permute-start(bf16[128,4608]{1,0:T(8,128)(2,1)} %get-tuple-element.35), channel_id=1, source_target_pairs={{0,8},{4,12},{8,0},{12,4},{1,9},{5,13},{9,1},{13,5},{2,10},{6,14},... | collective-permute-start | bytes 3538952 | tf_op jit(solution)/shard_map/ppermute | solution.py:506
  32.6 1.5 multiply_cosine_fusion
  34.0 1.3 pad_maximum_fusion.refs_7_.refs_5_
  35.3 5.4 %qkv.3 = (bf16[2,384,128]{2,1,0:T(8,128)(2,1)}, bf16[384,256]{1,0:T(8,128)(2,1)}) custom-call(bf16[192,4608]{1,0:T(8,128)(2,1)} %get-tuple-element.33.refs_0_.refs_2_, bf16[192,4608]{1,0:T(8,128)(2,1)S(1)} %collective-permute-done.refs_1_.refs_3_, bf16[192,4608]{1,0:T(8,128)(2,1)} %get-tuple-element.33.refs_0_.refs_2_, ...), custom_call_target="tpu_custom_call" | custom-call | flops 1 | bytes 1 | tf_op jit(solution)/shard_map/qkv/pallas_call | solution.py:37
  40.8 1.6 %collective-permute-start.2 = (bf16[384,256]{1,0:T(8,128)(2,1)}, bf16[384,256]{1,0:T(8,128)(2,1)S(1)}, u32[]{:S(2)}, u32[]{:S(2)}) collective-permute-start(bf16[384,256]{1,0:T(8,128)(2,1)} %get-tuple-element.36), channel_id=1, source_target_pairs={{0,1},{1,2},{2,3},{3,0},{4,5},{5,6},{6,7},{7,4},{8,9},{9,10},{10,1... | collective-permute-start | bytes 589832 | tf_op jit(solution)/shard_map/ppermute | solution.py:513
  42.4 2.6 %collective-permute-start.3 = (bf16[384,256]{1,0:T(8,128)(2,1)}, bf16[384,256]{1,0:T(8,128)(2,1)S(1)}, u32[]{:S(2)}, u32[]{:S(2)}) collective-permute-start(bf16[384,256]{1,0:T(8,128)(2,1)} %get-tuple-element.36), channel_id=1, source_target_pairs={{0,2},{1,3},{2,0},{3,1},{4,6},{5,7},{6,4},{7,5},{8,10},{9,11},{10,... | collective-permute-start | bytes 589832 | tf_op jit(solution)/shard_map/ppermute | solution.py:513
  45.0 1.3 collective-permute-start.4
  46.4 8.2 %collective-permute-done.2 = bf16[384,256]{1,0:T(8,128)(2,1)S(1)} collective-permute-done((bf16[384,256]{1,0:T(8,128)(2,1)}, bf16[384,256]{1,0:T(8,128)(2,1)S(1)}, u32[]{:S(2)}, u32[]{:S(2)}) %collective-permute-start.2) | collective-permute-done | bytes 196640 | tf_op jit(solution)/shard_map/ppermute | solution.py:513
  54.5 11.9 %collective-permute-done.3 = bf16[384,256]{1,0:T(8,128)(2,1)S(1)} collective-permute-done((bf16[384,256]{1,0:T(8,128)(2,1)}, bf16[384,256]{1,0:T(8,128)(2,1)S(1)}, u32[]{:S(2)}, u32[]{:S(2)}) %collective-permute-start.3) | collective-permute-done | bytes 196640 | tf_op jit(solution)/shard_map/ppermute | solution.py:513
  66.5 5.6 %attention.4 = (f32[768,128]{1,0:T(8,128)S(1)}, f32[768,256]{1,0:T(8,128)S(1)}) custom-call(s32[10]{0:T(128)S(1)} %pad_add_fusion.1.table, bf16[2,384,128]{2,1,0:T(8,128)(2,1)} %get-tuple-element.34.refs_0_, bf16[1,384,256]{2,1,0:T(8,128)(2,1)} %bitcast.33, bf16[1,384,256]{2,1,0:T(8,128)(2,1)S(1)} %bitcast.18, bf16[1,384,256]{2,1,0:T(8,128)(2,1)S(1)} %bitcast.21, ...), custom_call_target="tpu_custom_call" | custom-call | flops 1 | bytes 1 | tf_op jit(solution)/shard_map/attention/pallas_call | solution.py:37
  72.2 2.7 %collective-permute-done.6.refs_1_ = bf16[128,4608]{1,0:T(8,128)(2,1)S(1)} collective-permute-done((bf16[128,4608]{1,0:T(8,128)(2,1)S(1)}, bf16[128,4608]{1,0:T(8,128)(2,1)S(1)}, u32[]{:S(2)}, u32[]{:S(2)}) %collective-permute-start.6) | collective-permute-done | bytes 1179680 | tf_op jit(solution)/shard_map/ppermute | solution.py:506
  75.0 4.3 %qkv.4 = (bf16[2,256,128]{2,1,0:T(8,128)(2,1)}, bf16[256,256]{1,0:T(8,128)(2,1)}) custom-call(bf16[128,4608]{1,0:T(8,128)(2,1)S(1)} %collective-permute-done.1.refs_0_, bf16[128,4608]{1,0:T(8,128)(2,1)S(1)} %collective-permute-done.6.refs_1_, bf16[4608,256]{1,0:T(8,128)(2,1)} %refs_2_.4, bf16[4608,128]{1,0:T(8,128)(2,1)} %refs_3_.3, ...), custom_call_target="tpu_custom_call" | custom-call | flops 1 | bytes 1 | tf_op jit(solution)/shard_map/qkv/pallas_call | solution.py:37
  79.3 2.3 %collective-permute-start.9 = (bf16[256,256]{1,0:T(8,128)(2,1)}, bf16[256,256]{1,0:T(8,128)(2,1)S(1)}, u32[]{:S(2)}, u32[]{:S(2)}) collective-permute-start(bf16[256,256]{1,0:T(8,128)(2,1)} %get-tuple-element.42), channel_id=1, source_target_pairs={{0,2},{1,3},{2,0},{3,1},{4,6},{5,7},{6,4},{7,5},{8,10},{9,11},{10,... | collective-permute-start | bytes 393224 | tf_op jit(solution)/shard_map/ppermute | solution.py:513
  81.6 2.0 %collective-permute-start.10 = (bf16[256,256]{1,0:T(8,128)(2,1)}, bf16[256,256]{1,0:T(8,128)(2,1)S(1)}, u32[]{:S(2)}, u32[]{:S(2)}) collective-permute-start(bf16[256,256]{1,0:T(8,128)(2,1)} %get-tuple-element.42), channel_id=1, source_target_pairs={{0,3},{1,0},{2,1},{3,2},{4,7},{5,4},{6,5},{7,6},{8,11},{9,8},{10,9... | collective-permute-start | bytes 393224 | tf_op jit(solution)/shard_map/ppermute | solution.py:513
  84.1 2.9 %attention.5 = (f32[512,128]{1,0:T(8,128)S(1)}, f32[512,256]{1,0:T(8,128)S(1)}) custom-call(s32[10]{0:T(128)S(1)} %pad_add_fusion.1.table, bf16[2,256,128]{2,1,0:T(8,128)(2,1)} %get-tuple-element.40.refs_0_.refs_1_, bf16[1,384,256]{2,1,0:T(8,128)(2,1)} %bitcast.34, bf16[1,384,256]{2,1,0:T(8,128)(2,1)S(1)} %bitcast.19, bf16[1,384,256]{2,1,0:T(8,128)(2,1)S(1)} %bitcast.22, ...), custom_call_target="tpu_custom_call" | custom-call | flops 1 | bytes 1 | tf_op jit(solution)/shard_map/attention/pallas_call | solution.py:37
  86.9 1.0 collective-permute-done.7.refs_0_
  87.9 7.6 %collective-permute-done.9 = bf16[256,256]{1,0:T(8,128)(2,1)S(1)} collective-permute-done((bf16[256,256]{1,0:T(8,128)(2,1)}, bf16[256,256]{1,0:T(8,128)(2,1)S(1)}, u32[]{:S(2)}, u32[]{:S(2)}) %collective-permute-start.9) | collective-permute-done | bytes 131104 | tf_op jit(solution)/shard_map/ppermute | solution.py:513
  95.5 6.4 %collective-permute-done.8 = bf16[256,256]{1,0:T(8,128)(2,1)S(1)} collective-permute-done((bf16[256,256]{1,0:T(8,128)(2,1)}, bf16[256,256]{1,0:T(8,128)(2,1)S(1)}, u32[]{:S(2)}, u32[]{:S(2)}) %collective-permute-start.8) | collective-permute-done | bytes 131104 | tf_op jit(solution)/shard_map/ppermute | solution.py:513
  101.9 2.0 %collective-permute-done.11.refs_1_ = bf16[64,4608]{1,0:T(8,128)(2,1)S(1)} collective-permute-done((bf16[64,4608]{1,0:T(8,128)(2,1)S(1)}, bf16[64,4608]{1,0:T(8,128)(2,1)S(1)}, u32[]{:S(2)}, u32[]{:S(2)}) %collective-permute-start.11) | collective-permute-done | bytes 589856 | tf_op jit(solution)/shard_map/ppermute | solution.py:506
  103.9 3.7 %qkv.5 = (bf16[2,128,128]{2,1,0:T(8,128)(2,1)}, bf16[128,256]{1,0:T(8,128)(2,1)}) custom-call(bf16[64,4608]{1,0:T(8,128)(2,1)S(1)} %collective-permute-done.7.refs_0_, bf16[64,4608]{1,0:T(8,128)(2,1)S(1)} %collective-permute-done.11.refs_1_, bf16[4608,256]{1,0:T(8,128)(2,1)} %refs_2_.4, bf16[4608,128]{1,0:T(8,128)(2,1)} %refs_3_.3, ...), custom_call_target="tpu_custom_call" | custom-call | flops 1 | bytes 1 | tf_op jit(solution)/shard_map/qkv/pallas_call | solution.py:37
  107.6 4.2 %collective-permute-start.12 = (bf16[128,256]{1,0:T(8,128)(2,1)}, bf16[128,256]{1,0:T(8,128)(2,1)S(1)}, u32[]{:S(2)}, u32[]{:S(2)}) collective-permute-start(bf16[128,256]{1,0:T(8,128)(2,1)} %get-tuple-element.47), channel_id=1, source_target_pairs={{0,1},{1,2},{2,3},{3,0},{4,5},{5,6},{6,7},{7,4},{8,9},{9,10},{10,1... | collective-permute-start | bytes 196616 | tf_op jit(solution)/shard_map/ppermute | solution.py:513
  111.8 2.6 %collective-permute-start.14 = (bf16[128,256]{1,0:T(8,128)(2,1)}, bf16[128,256]{1,0:T(8,128)(2,1)S(1)}, u32[]{:S(2)}, u32[]{:S(2)}) collective-permute-start(bf16[128,256]{1,0:T(8,128)(2,1)} %get-tuple-element.47), channel_id=1, source_target_pairs={{0,3},{1,0},{2,1},{3,2},{4,7},{5,4},{6,5},{7,6},{8,11},{9,8},{10,9... | collective-permute-start | bytes 196616 | tf_op jit(solution)/shard_map/ppermute | solution.py:513
  114.5 8.0 %attention.6 = (f32[768,128]{1,0:T(8,128)S(1)}, f32[768,256]{1,0:T(8,128)S(1)}, f32[512,128]{1,0:T(8,128)S(1)}, f32[512,256]{1,0:T(8,128)S(1)}, f32[256,128]{1,0:T(8,128)S(1)}, /*index=5*/f32[256,256]{1,0:T(8,128)S(1)}) custom-call(s32[10]{0:T(128)S(1)} %pad_add_fusion.1.table, bf16[2,384,128]{2,1,0:T(8,128)(2,1)} %get-tuple-element.34.refs_0_, ...), custom_call_target="tpu_custom_call" | custom-call | flops 1 | bytes 1 | tf_op jit(solution)/shard_map/attention/pallas_call | solution.py:37
  122.5 4.9 %attention.7 = (bf16[192,256]{1,0:T(8,128)(2,1)}, bf16[192,256]{1,0:T(8,128)(2,1)}, bf16[192,256]{1,0:T(8,128)(2,1)}, bf16[192,256]{1,0:T(8,128)(2,1)}) custom-call(s32[10]{0:T(128)S(1)} %pad_add_fusion.1.table, bf16[2,384,128]{2,1,0:T(8,128)(2,1)} %get-tuple-element.34.refs_0_, bf16[2,256,128]{2,1,0:T(8,128)(2,1)} %get-tuple-element.40.refs_0_.refs_1_, ...), custom_call_target="tpu_custom_call" | custom-call | flops 1 | bytes 1 | tf_op jit(solution)/shard_map/attention/pallas_call | solution.py:37
  128.0 1.5 %collective-permute-start.15 = (bf16[192,256]{1,0:T(8,128)(2,1)}, bf16[192,256]{1,0:T(8,128)(2,1)S(1)}, u32[]{:S(2)}, u32[]{:S(2)}) collective-permute-start(bf16[192,256]{1,0:T(8,128)(2,1)} %get-tuple-element.54), channel_id=1, source_target_pairs={{0,8},{4,12},{8,0},{12,4},{1,9},{5,13},{9,1},{13,5},{2,10},{6,14},... | collective-permute-start | bytes 294920 | tf_op jit(solution)/shard_map/ppermute | solution.py:506
  129.6 2.8 %collective-permute-done.19.refs_1_ = bf16[192,256]{1,0:T(8,128)(2,1)S(1)} collective-permute-done((bf16[192,256]{1,0:T(8,128)(2,1)}, bf16[192,256]{1,0:T(8,128)(2,1)S(1)}, u32[]{:S(2)}, u32[]{:S(2)}) %collective-permute-start.19) | collective-permute-done | bytes 98336 | tf_op jit(solution)/shard_map/ppermute | solution.py:506
  132.4 3.6 %output_near.1.refs_5_ = bf16[192,4608]{1,0:T(8,128)(2,1)S(1)} custom-call(bf16[192,256]{1,0:T(8,128)(2,1)} %get-tuple-element.58.refs_0_, bf16[192,256]{1,0:T(8,128)(2,1)S(1)} %collective-permute-done.19.refs_1_, bf16[256,4608]{1,0:T(8,128)(2,1)} %refs_2_.5, bf16[256,4608]{1,0:T(8,128)(2,1)} %collective-permute-done.5.refs_3_), custom_call_target="tpu_custom_call" | custom-call | flops 1 | bytes 1 | tf_op jit(solution)/shard_map/output_near/pallas_call | solution.py:37
  136.0 4.2 %output_norm.1 = bf16[192,4608]{1,0:T(8,128)(2,1)} custom-call(bf16[192,256]{1,0:T(8,128)(2,1)S(1)} %collective-permute-done.15.refs_0_, bf16[192,256]{1,0:T(8,128)(2,1)S(1)} %collective-permute-done.16.refs_1_, bf16[256,4608]{1,0:T(8,128)(2,1)S(1)} %copy-done, bf16[256,4608]{1,0:T(8,128)(2,1)S(1)} %collective-permute-done.18.refs_3_, ...), custom_call_target="tpu_custom_call" | custom-call | flops 1 | bytes 1 | tf_op jit(solution)/shard_map/output_norm/pallas_call | solution.py:37
  (43 shorter events, 3.7 us)
Async XLA Ops:
  6.5 120.9 %all-gather.2.cloned.1.call-start = ((), (), s32[]{:S(2)}) async-start(), calls=%async_computation | async-start | bytes 2654208 | tf_op jit(solution)/shard_map/all_gather | solution.py:543
  19.0 10.9 %collective-permute-start = (bf16[192,4608]{1,0:T(8,128)(2,1)}, bf16[192,4608]{1,0:T(8,128)(2,1)S(1)}, u32[]{:S(2)}, u32[]{:S(2)}) collective-permute-start(bf16[192,4608]{1,0:T(8,128)(2,1)} %get-tuple-element.33.refs_0_.refs_2_), channel_id=1, source_target_pairs={{0,4},{4,0},{8,12},{12,8},{1,5},{5,1},{9,13},{13,9},{2,6},{6,2},{1... | collective-permute-start | bytes 5308424 | tf_op jit(solution)/shard_map/ppermute | solution.py:506
  19.5 10.4 %collective-permute-start.17 = (bf16[32,4608]{1,0:T(8,128)(2,1)}, bf16[32,4608]{1,0:T(8,128)(2,1)S(1)}, u32[]{:S(2)}, u32[]{:S(2)}) collective-permute-start(bf16[32,4608]{1,0:T(8,128)(2,1)} %get-tuple-element.56), channel_id=1, source_target_pairs={{0,8},{4,12},{8,0},{12,4},{1,9},{5,13},{9,1},{13,5},{2,10},{6,14},... | collective-permute-start | bytes 884744 | tf_op jit(solution)/shard_map/ppermute | solution.py:506
  22.1 50.0 %collective-permute-start.5 = (bf16[256,4608]{1,0:T(8,128)(2,1)}, bf16[256,4608]{1,0:T(8,128)(2,1)}, u32[]{:S(2)}, u32[]{:S(2)}) collective-permute-start(bf16[256,4608]{1,0:T(8,128)(2,1)} %refs_2_.5), channel_id=1, source_target_pairs={{0,4},{4,0},{8,12},{12,8},{1,5},{5,1},{9,13},{13,9},{2,6},{6,2},{1... | collective-permute-start | bytes 7077896 | tf_op jit(solution)/shard_map/ppermute | solution.py:506
  29.9 0.7 copy-start.1
  30.6 41.4 %collective-permute-start.1 = (bf16[128,4608]{1,0:T(8,128)(2,1)}, bf16[128,4608]{1,0:T(8,128)(2,1)S(1)}, u32[]{:S(2)}, u32[]{:S(2)}) collective-permute-start(bf16[128,4608]{1,0:T(8,128)(2,1)} %get-tuple-element.35), channel_id=1, source_target_pairs={{0,8},{4,12},{8,0},{12,4},{1,9},{5,13},{9,1},{13,5},{2,10},{6,14},... | collective-permute-start | bytes 3538952 | tf_op jit(solution)/shard_map/ppermute | solution.py:506
  35.3 36.8 %copy-start.3 = (bf16[64,4608]{1,0:T(8,128)(2,1)S(1)}, bf16[64,4608]{1,0:T(8,128)(2,1)}, u32[]{:S(2)}) copy-start(bf16[64,4608]{1,0:T(8,128)(2,1)} %get-tuple-element.41) | copy-start | bytes 1769476
  40.8 13.8 %collective-permute-start.2 = (bf16[384,256]{1,0:T(8,128)(2,1)}, bf16[384,256]{1,0:T(8,128)(2,1)S(1)}, u32[]{:S(2)}, u32[]{:S(2)}) collective-permute-start(bf16[384,256]{1,0:T(8,128)(2,1)} %get-tuple-element.36), channel_id=1, source_target_pairs={{0,1},{1,2},{2,3},{3,0},{4,5},{5,6},{6,7},{7,4},{8,9},{9,10},{10,1... | collective-permute-start | bytes 589832 | tf_op jit(solution)/shard_map/ppermute | solution.py:513
  42.4 24.0 %collective-permute-start.3 = (bf16[384,256]{1,0:T(8,128)(2,1)}, bf16[384,256]{1,0:T(8,128)(2,1)S(1)}, u32[]{:S(2)}, u32[]{:S(2)}) collective-permute-start(bf16[384,256]{1,0:T(8,128)(2,1)} %get-tuple-element.36), channel_id=1, source_target_pairs={{0,2},{1,3},{2,0},{3,1},{4,6},{5,7},{6,4},{7,5},{8,10},{9,11},{10,... | collective-permute-start | bytes 589832 | tf_op jit(solution)/shard_map/ppermute | solution.py:513
  45.0 21.4 %collective-permute-start.4 = (bf16[384,256]{1,0:T(8,128)(2,1)}, bf16[384,256]{1,0:T(8,128)(2,1)S(1)}, u32[]{:S(2)}, u32[]{:S(2)}) collective-permute-start(bf16[384,256]{1,0:T(8,128)(2,1)} %get-tuple-element.36), channel_id=1, source_target_pairs={{0,3},{1,0},{2,1},{3,2},{4,7},{5,4},{6,5},{7,6},{8,11},{9,8},{10,9... | collective-permute-start | bytes 589832 | tf_op jit(solution)/shard_map/ppermute | solution.py:513
  72.1 2.9 %collective-permute-start.6 = (bf16[128,4608]{1,0:T(8,128)(2,1)S(1)}, bf16[128,4608]{1,0:T(8,128)(2,1)S(1)}, u32[]{:S(2)}, u32[]{:S(2)}) collective-permute-start(bf16[128,4608]{1,0:T(8,128)(2,1)S(1)} %collective-permute-done.1.refs_0_), channel_id=1, source_target_pairs={{0,4},{4,0},{8,12},{12,8},{1,5},{5,1},{9,13},{13,9},{2,6},{6,2},{1... | collective-permute-start | bytes 3538952 | tf_op jit(solution)/shard_map/ppermute | solution.py:506
  72.2 15.7 %collective-permute-start.7 = (bf16[64,4608]{1,0:T(8,128)(2,1)S(1)}, bf16[64,4608]{1,0:T(8,128)(2,1)S(1)}, u32[]{:S(2)}, u32[]{:S(2)}) collective-permute-start(bf16[64,4608]{1,0:T(8,128)(2,1)S(1)} %copy-done.3), channel_id=1, source_target_pairs={{0,8},{4,12},{8,0},{12,4},{1,9},{5,13},{9,1},{13,5},{2,10},{6,14},... | collective-permute-start | bytes 1769480 | tf_op jit(solution)/shard_map/ppermute | solution.py:506
  79.3 16.2 %collective-permute-start.9 = (bf16[256,256]{1,0:T(8,128)(2,1)}, bf16[256,256]{1,0:T(8,128)(2,1)S(1)}, u32[]{:S(2)}, u32[]{:S(2)}) collective-permute-start(bf16[256,256]{1,0:T(8,128)(2,1)} %get-tuple-element.42), channel_id=1, source_target_pairs={{0,2},{1,3},{2,0},{3,1},{4,6},{5,7},{6,4},{7,5},{8,10},{9,11},{10,... | collective-permute-start | bytes 393224 | tf_op jit(solution)/shard_map/ppermute | solution.py:513
  81.6 13.9 %collective-permute-start.10 = (bf16[256,256]{1,0:T(8,128)(2,1)}, bf16[256,256]{1,0:T(8,128)(2,1)S(1)}, u32[]{:S(2)}, u32[]{:S(2)}) collective-permute-start(bf16[256,256]{1,0:T(8,128)(2,1)} %get-tuple-element.42), channel_id=1, source_target_pairs={{0,3},{1,0},{2,1},{3,2},{4,7},{5,4},{6,5},{7,6},{8,11},{9,8},{10,9... | collective-permute-start | bytes 393224 | tf_op jit(solution)/shard_map/ppermute | solution.py:513
  83.6 18.3 %collective-permute-start.8 = (bf16[256,256]{1,0:T(8,128)(2,1)}, bf16[256,256]{1,0:T(8,128)(2,1)S(1)}, u32[]{:S(2)}, u32[]{:S(2)}) collective-permute-start(bf16[256,256]{1,0:T(8,128)(2,1)} %get-tuple-element.42), channel_id=1, source_target_pairs={{0,1},{1,2},{2,3},{3,0},{4,5},{5,6},{6,7},{7,4},{8,9},{9,10},{10,1... | collective-permute-start | bytes 393224 | tf_op jit(solution)/shard_map/ppermute | solution.py:513
  101.9 2.0 %collective-permute-start.11 = (bf16[64,4608]{1,0:T(8,128)(2,1)S(1)}, bf16[64,4608]{1,0:T(8,128)(2,1)S(1)}, u32[]{:S(2)}, u32[]{:S(2)}) collective-permute-start(bf16[64,4608]{1,0:T(8,128)(2,1)S(1)} %collective-permute-done.7.refs_0_), channel_id=1, source_target_pairs={{0,4},{4,0},{8,12},{12,8},{1,5},{5,1},{9,13},{13,9},{2,6},{6,2},{1... | collective-permute-start | bytes 1769480 | tf_op jit(solution)/shard_map/ppermute | solution.py:506
  107.6 14.9 %collective-permute-start.12 = (bf16[128,256]{1,0:T(8,128)(2,1)}, bf16[128,256]{1,0:T(8,128)(2,1)S(1)}, u32[]{:S(2)}, u32[]{:S(2)}) collective-permute-start(bf16[128,256]{1,0:T(8,128)(2,1)} %get-tuple-element.47), channel_id=1, source_target_pairs={{0,1},{1,2},{2,3},{3,0},{4,5},{5,6},{6,7},{7,4},{8,9},{9,10},{10,1... | collective-permute-start | bytes 196616 | tf_op jit(solution)/shard_map/ppermute | solution.py:513
  111.8 10.7 %collective-permute-start.13 = (bf16[128,256]{1,0:T(8,128)(2,1)}, bf16[128,256]{1,0:T(8,128)(2,1)S(1)}, u32[]{:S(2)}, u32[]{:S(2)}) collective-permute-start(bf16[128,256]{1,0:T(8,128)(2,1)} %get-tuple-element.47), channel_id=1, source_target_pairs={{0,2},{1,3},{2,0},{3,1},{4,6},{5,7},{6,4},{7,5},{8,10},{9,11},{10,... | collective-permute-start | bytes 196616 | tf_op jit(solution)/shard_map/ppermute | solution.py:513
  111.8 10.7 %collective-permute-start.14 = (bf16[128,256]{1,0:T(8,128)(2,1)}, bf16[128,256]{1,0:T(8,128)(2,1)S(1)}, u32[]{:S(2)}, u32[]{:S(2)}) collective-permute-start(bf16[128,256]{1,0:T(8,128)(2,1)} %get-tuple-element.47), channel_id=1, source_target_pairs={{0,3},{1,0},{2,1},{3,2},{4,7},{5,4},{6,5},{7,6},{8,11},{9,8},{10,9... | collective-permute-start | bytes 196616 | tf_op jit(solution)/shard_map/ppermute | solution.py:513
  122.5 7.1 %copy-start.2 = (f32[4608]{0:T(1024)S(1)}, f32[4608]{0:T(1024)}, u32[]{:S(2)}) copy-start(f32[4608]{0:T(1024)} %param.10) | copy-start | bytes 55300
  127.5 8.5 %collective-permute-start.18 = (bf16[256,4608]{1,0:T(8,128)(2,1)}, bf16[256,4608]{1,0:T(8,128)(2,1)S(1)}, u32[]{:S(2)}, u32[]{:S(2)}) collective-permute-start(bf16[256,4608]{1,0:T(8,128)(2,1)} %all-gather.2.cloned.1.call-done.refs_2_), channel_id=1, source_target_pairs={{0,4},{4,0},{8,12},{12,8},{1,5},{5,1},{9,13},{13,9},{2,6},{6,2},{1... | collective-permute-start | bytes 7077896 | tf_op jit(solution)/shard_map/ppermute | solution.py:506
  127.6 4.9 %collective-permute-start.19 = (bf16[192,256]{1,0:T(8,128)(2,1)}, bf16[192,256]{1,0:T(8,128)(2,1)S(1)}, u32[]{:S(2)}, u32[]{:S(2)}) collective-permute-start(bf16[192,256]{1,0:T(8,128)(2,1)} %get-tuple-element.60), channel_id=1, source_target_pairs={{0,4},{4,0},{8,12},{12,8},{1,5},{5,1},{9,13},{13,9},{2,6},{6,2},{1... | collective-permute-start | bytes 294920 | tf_op jit(solution)/shard_map/ppermute | solution.py:506
  128.0 7.9 %collective-permute-start.15 = (bf16[192,256]{1,0:T(8,128)(2,1)}, bf16[192,256]{1,0:T(8,128)(2,1)S(1)}, u32[]{:S(2)}, u32[]{:S(2)}) collective-permute-start(bf16[192,256]{1,0:T(8,128)(2,1)} %get-tuple-element.54), channel_id=1, source_target_pairs={{0,8},{4,12},{8,0},{12,4},{1,9},{5,13},{9,1},{13,5},{2,10},{6,14},... | collective-permute-start | bytes 294920 | tf_op jit(solution)/shard_map/ppermute | solution.py:506
  129.6 6.4 %collective-permute-start.16 = (bf16[192,256]{1,0:T(8,128)(2,1)}, bf16[192,256]{1,0:T(8,128)(2,1)S(1)}, u32[]{:S(2)}, u32[]{:S(2)}) collective-permute-start(bf16[192,256]{1,0:T(8,128)(2,1)} %get-tuple-element.55), channel_id=1, source_target_pairs={{0,12},{4,8},{8,4},{12,0},{1,13},{5,9},{9,5},{13,1},{2,14},{6,10},... | collective-permute-start | bytes 294920 | tf_op jit(solution)/shard_map/ppermute | solution.py:506
  129.6 6.4 %copy-start = (bf16[256,4608]{1,0:T(8,128)(2,1)S(1)}, bf16[256,4608]{1,0:T(8,128)(2,1)}, u32[]{:S(2)}) copy-start(bf16[256,4608]{1,0:T(8,128)(2,1)} %all-gather.2.cloned.1.call-done.refs_2_) | copy-start | bytes 7077892
Sparse Core Ops, SparseCore 0:
  30.7 75.0 all-gather.1

commit v5 on v4

--- a/solution.py
+++ b/solution.py
@@ -26,7 +26,7 @@
         self.array, self.shape = array, array.shape
 
 
-def call(kernel, name, mib, in_specs, out_shape, scratch, *args, out=HBM):
+def call(kernel, name, mib, in_specs, outs, scratch, *args, aliases=None):
     in_specs, pinned = list(in_specs), []
     for at, arg in enumerate(args):
         if isinstance(arg, Came):
@@ -37,9 +37,10 @@
     return pl.pallas_call(
         kernel,
         in_specs=in_specs,
-        out_specs=[out] * len(out_shape),
-        out_shape=[out.memory_space(shape, dtype) for shape, dtype in out_shape],
+        out_specs=[spec for _, _, spec in outs],
+        out_shape=[spec.memory_space(shape, dtype) for shape, dtype, spec in outs],
         scratch_shapes=scratch,
+        input_output_aliases=aliases or {},
         compiler_params=pltpu.CompilerParams(vmem_limit_bytes=mib * MIB),
         cost_estimate=COST,
         name=name,
@@ -58,8 +59,8 @@
 
 
 def norm_kernel(cuts, pieces, table, hidden, gain, w_out, *refs):
-    whole, parts = refs[0], refs[1 : 1 + len(cuts)]
-    w_piece, rows, staged, semaphores = refs[1 + len(cuts) :]
+    parts = refs[: len(cuts)]
+    w_piece, rows, staged, bounced, semaphores = refs[len(cuts) :]
     copies = Copies(semaphores)
     count, width = hidden.shape
     step = count // pieces
@@ -67,7 +68,8 @@
     ins = [copies.start(hidden.at[span], rows.at[span]) for span in spans]
     size = w_piece.shape[0]
     first = pl.multiple_of(table[1] * size, size)
-    outs = [copies.start(w_out.at[pl.ds(first, size)], w_piece)]
+    piece = copies.start(w_out.at[pl.ds(first, size)], bounced)
+    outs = []
     scale = gain[...]
     for at, span in enumerate(spans):
         ins[at].wait()
@@ -78,13 +80,14 @@
             folded = folded + square[:, lane : lane + 128]
         mean = jnp.sum(folded, axis=1, keepdims=True) / width
         staged[span, :] = (x * lax.rsqrt(mean + EPS) * scale).astype(jnp.bfloat16)
-        outs.append(copies.start(staged.at[span], whole.at[span]))
         begin = 0
         for cut, part in zip(cuts, parts):
             if begin <= at * step < begin + cut:
                 inside = pl.ds(at * step - begin, step)
                 outs.append(copies.start(staged.at[span], part.at[inside]))
             begin += cut
+    piece.wait()
+    outs.append(copies.start(bounced, w_piece))
     for copy in outs:
         copy.wait()
 
@@ -92,17 +95,18 @@
 def norm(table, hidden, gain, w_out, cuts, share, pieces=3):
     rows, width = hidden.shape
     bf16 = jnp.bfloat16
-    out_shape = [((rows, width), bf16)] + [((cut, width), bf16) for cut in cuts]
+    outs = [((cut, width), bf16, HBM) for cut in cuts]
     return call(
         functools.partial(norm_kernel, cuts, pieces),
         "norm_rows",
         12,
         [SMEM, HBM, VMEM, HBM],
-        out_shape + [((share, width), bf16)],
+        outs + [((share, width), bf16, HBM)],
         [
             pltpu.VMEM((rows, width), bf16),
             pltpu.VMEM((rows, width), bf16),
-            pltpu.SemaphoreType.DMA((1 + 3 * pieces,)),
+            pltpu.VMEM((share, width), bf16),
+            pltpu.SemaphoreType.DMA((2 + 2 * pieces,)),
         ],
         table,
         hidden,
@@ -111,37 +115,45 @@
     )
 
 
-def qkv_kernel(runs, first, chunks, *refs):
+def hold_kernel(wq, wk, wv, out, semaphores):
+    copies, column, waits = Copies(semaphores), 0, []
+    for weight in (wq, wk, wv):
+        count = weight.shape[1]
+        waits.append(copies.start(weight, out.at[:, pl.ds(column, count)]))
+        column += count
+    for copy in waits:
+        copy.wait()
+
+
+def hold(wq, wk, wv):
+    shape = (wq.shape[0], wq.shape[1] + wk.shape[1] + wv.shape[1])
+    return call(
+        hold_kernel,
+        "hold_weights",
+        1,
+        [HBM] * 3,
+        [(shape, wq.dtype, VMEM)],
+        [pltpu.SemaphoreType.DMA((3,))],
+        wq,
+        wk,
+        wv,
+    )[0]
+
+
+def qkv_kernel(runs, first, weights, trig, *refs):
     parts = refs[: len(runs)]
-    wq, wk, wv, trig, q_out, kv_out = refs[len(runs) : len(runs) + 6]
-    rows, weights, angles, q, kv, semaphores = refs[len(runs) + 6 :]
-    copies = Copies(semaphores)
-    total, width = rows.shape
-    depth = width // chunks
-    queries = wq.shape[1]
-    waits = []
-    for chunk in range(chunks):
-        lanes = pl.ds(chunk * depth, depth)
-        here, put = [], 0
-        for part, (begin, count) in zip(parts, runs):
-            source = part.at[pl.ds(begin, count), lanes]
-            here.append(copies.start(source, rows.at[pl.ds(put, count), lanes]))
-            put += count
-        column = 0
-        for weight in (wq, wk, wv):
-            target = weights.at[lanes, pl.ds(column, weight.shape[1])]
-            here.append(copies.start(weight.at[lanes], target))
-            column += weight.shape[1]
-        waits.append(here)
-    waits[-1].append(copies.start(trig.at[pl.ds(first, total)], angles))
-    product = None
-    for chunk in range(chunks):
-        for copy in waits[chunk]:
-            copy.wait()
-        lanes = slice(chunk * depth, (chunk + 1) * depth)
-        term = jnp.dot(rows[:, lanes], weights[lanes, :], preferred_element_type=jnp.float32)
-        product = term if product is None else product + term
+    q, kv, rows, angles, semaphores = refs[len(runs) :]
+    copies, put, waits = Copies(semaphores), 0, []
+    for part, (begin, count) in zip(parts, runs):
+        target = rows.at[pl.ds(put, count)]
+        waits.append(copies.start(part.at[pl.ds(begin, count)], target))
+        put += count
+    waits.append(copies.start(trig.at[pl.ds(first, put)], angles))
+    for copy in waits:
+        copy.wait()
+    product = jnp.dot(rows[...], weights[...], preferred_element_type=jnp.float32)
     cos, sin = angles[:, :HD], angles[:, HD:]
+    queries = weights.shape[1] - 2 * HD
 
     def rotated(at):
         y = product[:, at : at + HD]
@@ -150,37 +162,29 @@
     factor = ATT_SCALAR ** (-0.5) * math.log2(math.e)
     kv[:, :HD] = rotated(queries).astype(jnp.bfloat16)
     kv[:, HD:] = product[:, queries + HD :].astype(jnp.bfloat16)
-    outs = [copies.start(kv, kv_out)]
     for head in range(queries // HD):
         q[head] = (rotated(head * HD) * factor).astype(jnp.bfloat16)
-    outs.append(copies.start(q, q_out))
-    for copy in outs:
-        copy.wait()
-
-
-def qkv(parts, weights, trig, first, chunks=4):
+
+
+def qkv(parts, weights, trig, first):
     total = sum(count for _, _, count in parts)
-    width, queries = weights[0].shape
-    bf16 = jnp.bfloat16
-    heads = queries // HD
+    width, columns = weights.shape
+    heads = columns // HD - 2
     runs = [(begin, count) for _, begin, count in parts]
     return call(
-        functools.partial(qkv_kernel, runs, first, chunks),
+        functools.partial(qkv_kernel, runs, first),
         "qkv",
-        24,
-        [HBM] * (len(parts) + 4),
-        [((heads, total, HD), bf16), ((total, 2 * HD), bf16)],
+        12,
+        [VMEM] + [HBM] * (len(parts) + 1),
+        [((heads, total, HD), jnp.bfloat16, VMEM), ((total, 2 * HD), jnp.bfloat16, VMEM)],
         [
-            pltpu.VMEM((total, width), bf16),
-            pltpu.VMEM((width, queries + 2 * HD), bf16),
+            pltpu.VMEM((total, width), jnp.bfloat16),
             pltpu.VMEM((total, 2 * HD), jnp.float32),
-            pltpu.VMEM((heads, total, HD), bf16),
-            pltpu.VMEM((total, 2 * HD), bf16),
-            pltpu.SemaphoreType.DMA((chunks * (len(parts) + 3) + 3,)),
+            pltpu.SemaphoreType.DMA((len(parts) + 1,)),
         ],
+        weights,
+        trig,
         *[array for array, _, _ in parts],
-        *weights,
-        trig,
     )
 
 
@@ -210,29 +214,25 @@
     refs = list(refs)
     take = lambda n: [refs.pop(0) for _ in range(n)]
     count = len(q_chunks)
-    q_refs = take(count)
+    qs = take(count)
     kv_parts = [take(n) for n in group_parts]
-    old = {q: take(2) for q in range(count) if q not in fresh}
-    outs = take(len(final) if final else 2 * count)
-    qs, kvs = take(count), take(len(group_parts))
-    if final:
-        states, staged = [take(2) for _ in range(count)], take(len(final))
-    else:
-        states = [outs[2 * q : 2 * q + 2] for q in range(count)]
+    take(2 * (count - len(fresh)))
+    outs = take(len(final))
+    states = [take(2) for _ in range(count)]
+    kvs, staged = take(len(group_parts)), take(len(final))
     (semaphores,) = refs
     copies = Copies(semaphores)
     core = table[0]
     waits = {}
-    for at, (source, target) in enumerate(zip(q_refs, qs)):
-        waits["q", at] = [copies.start(source, target)]
     for group, (parts, kv) in enumerate(zip(kv_parts, kvs)):
         each = kv.shape[0] // len(parts)
-        waits["kv", group] = [
+        waits[group] = [
             copies.start(part, kv.at[pl.ds(slot * each, each)])
             for slot, part in enumerate(parts)
         ]
-    def ready(*key):
-        for copy in waits.pop(key, []):
+
+    def ready(group):
+        for copy in waits.pop(group, []):
             copy.wait()
 
     def attend(q, keys_values, begin, visible=None, bias=None):
@@ -268,23 +268,20 @@
             peak[span, :] = top
 
     begun = set(range(count)) - set(fresh)
-    for q, held in old.items():
-        for source, target in zip(held, states[q]):
-            target[...] = source[...]
     for step in plan:
         q, group, kv = step.q, step.group, kvs[step.group]
         q_chunk, k_chunk = q_chunks[q], k_chunks[group]
-        ready("q", q)
-        ready("kv", group)
         if step.same is not None:
             keys_at = k_chunk.places(core, 1, 0, kv.shape[1])
             visible = lambda first, tile: keys_at <= q_chunk.places(core, 0, first, tile)
-            attend(q, kv[step.same], q not in begun, visible=visible)
+            own = kv_parts[group][0]
+            attend(q, own[step.same], q not in begun, visible=visible)
             begun.add(q)
         start = table[q_chunk.at]
         slots = step.slots
         if not slots:
             continue
+        ready(group)
         if step.merged:
             shown = [table[k_chunk.at + slot] < start for slot in slots]
 
@@ -309,73 +306,69 @@
 
             lax.fori_loop(slots[0], slots[-1] + 1, one, 0)
 
+    for group in list(waits):
+        ready(group)
     stores = []
-    if final:
-        for out, stage, spans in zip(outs, staged, final):
-            put = 0
-            for q, first, rows in spans:
-                acc = states[q][1]
-                heads, q_rows, _ = qs[q].shape
-                tile = min(q_rows, 128)
-                size = min(tile, rows)
-                for head in range(heads):
-                    for at in range(first, first + rows, size):
-                        begin = at // tile * tile * heads + head * tile + at % tile
-                        part = acc[begin : begin + size, :]
-                        to = put + at - first
-                        stage[to : to + size, head * HD : (head + 1) * HD] = (
-                            part[:, :HD] / part[:, HD:]
-                        ).astype(jnp.bfloat16)
-                put += rows
-            stores.append(copies.start(stage, out))
+    for out, stage, spans in zip(outs, staged, final):
+        put = 0
+        for q, first, rows in spans:
+            acc = states[q][1]
+            heads, q_rows, _ = qs[q].shape
+            tile = min(q_rows, 128)
+            size = min(tile, rows)
+            for head in range(heads):
+                for at in range(first, first + rows, size):
+                    begin = at // tile * tile * heads + head * tile + at % tile
+                    part = acc[begin : begin + size, :]
+                    to = put + at - first
+                    stage[to : to + size, head * HD : (head + 1) * HD] = (
+                        part[:, :HD] / part[:, HD:]
+                    ).astype(jnp.bfloat16)
+            put += rows
+        stores.append(copies.start(stage, out))
     for copy in stores:
         copy.wait()
 
 
-def attention(plan, table, qs, q_chunks, groups, k_chunks, state, final=None):
+def attention(plan, table, qs, q_chunks, groups, k_chunks, state, final=()):
     fresh = [at for at, held in enumerate(state) if held is None]
-    held = [array for pair in state if pair is not None for array in pair]
     shapes = []
     for q in qs:
         heads, rows, _ = q.shape
         shapes += [(heads * rows, HD), (heads * rows, 2 * HD)]
-    if final:
-        width = qs[0].shape[0] * HD
-        sums = [sum(rows for _, _, rows in spans) for spans in final]
-        out_shape = [((rows, width), jnp.bfloat16) for rows in sums]
-    else:
-        out_shape = [(shape, jnp.float32) for shape in shapes]
-    scratch = [pltpu.VMEM(q.shape, jnp.bfloat16) for q in qs]
+    width = qs[0].shape[0] * HD
+    sums = [sum(rows for _, _, rows in spans) for spans in final]
+    outs = [((rows, width), jnp.bfloat16, HBM) for rows in sums]
+    scratch = []
     for parts in groups:
         slots = sum(part.shape[0] for part in parts)
         scratch.append(pltpu.VMEM((slots,) + parts[0].shape[1:], jnp.bfloat16))
-    if final:
-        scratch += [pltpu.VMEM(shape, jnp.float32) for shape in shapes]
-        scratch += [pltpu.VMEM(shape, dtype) for shape, dtype in out_shape]
+    scratch += [pltpu.VMEM((rows, width), jnp.bfloat16) for rows in sums]
     parts = [part for parts in groups for part in parts]
-    inputs = [*qs, *parts]
     sizes = [len(parts) for parts in groups]
+    inputs, aliases = [table, *qs, *parts], {}
+    for at, pair in enumerate(state):
+        for half, array in enumerate(pair or ()):
+            aliases[len(inputs)] = len(outs) + 2 * at + half
+            inputs.append(array)
     results = call(
         functools.partial(attention_kernel, plan, q_chunks, k_chunks, sizes, fresh, final),
         "attention",
         20,
-        [SMEM] + [HBM] * len(inputs) + [VMEM] * len(held),
-        out_shape,
-        scratch + [pltpu.SemaphoreType.DMA((len(inputs) + len(out_shape),))],
-        table,
+        [SMEM] + [VMEM] * (len(inputs) - 1),
+        outs + [(shape, jnp.float32, VMEM) for shape in shapes],
+        scratch + [pltpu.SemaphoreType.DMA((len(parts) + len(outs),))],
         *inputs,
-        *held,
-        out=HBM if final else VMEM,
+        aliases=aliases,
     )
     if final:
-        return results
+        return results[: len(final)]
     return [tuple(results[2 * at : 2 * at + 2]) for at in range(len(qs))]
 
 
-def fetch(copies, lefts, left, pieces, weights, chunks):
+def fetch(copies, lefts, left, pieces, rows, weights, chunks):
     columns = lefts[0].shape[1]
-    depth, width = pieces[0].shape
-    step = width // chunks
+    step = weights.shape[1] // chunks
     first = [
         copies.start(part, left.at[:, pl.ds(at * columns, columns)])
         for at, part in enumerate(lefts)
@@ -385,8 +378,8 @@
         lanes = pl.ds(chunk * step, step)
         waits.append(
             [
-                copies.start(piece.at[:, lanes], weights.at[pl.ds(at * depth, depth), lanes])
-                for at, piece in enumerate(pieces)
+                copies.start(piece.at[:, lanes], weights.at[pl.ds(row, piece.shape[0]), lanes])
+                for row, piece in zip(rows, pieces)
             ]
         )
     waits[0] += first
@@ -397,7 +390,8 @@
     lefts, pieces = refs[:2], refs[2:4]
     out, left, weights, semaphores = refs[4:]
     copies = Copies(semaphores)
-    waits = fetch(copies, lefts, left, pieces, weights, chunks)
+    rows = [0, pieces[0].shape[0]]
+    waits = fetch(copies, lefts, left, pieces, rows, weights, chunks)
     step = out.shape[1] // chunks
     for chunk in range(chunks):
         for copy in waits[chunk]:
@@ -416,7 +410,7 @@
         "output_near",
         16,
         [HBM] * 4,
-        [((rows, width), bf16)],
+        [((rows, width), bf16, VMEM)],
         [
             pltpu.VMEM((rows, 2 * columns), bf16),
             pltpu.VMEM((2 * depth, width), bf16),
@@ -424,15 +418,21 @@
         ],
         *lefts,
         *pieces,
-        out=VMEM,
     )[0]
 
 
-def output_kernel(chunks, *refs):
-    lefts, pieces = refs[:2], refs[2:4]
-    hidden, near, gain, out, left, weights, held, projected, semaphores = refs[4:]
+def output_kernel(count, at, chunks, table, *refs):
+    lefts, pieces = refs[:2], refs[2 : 2 + count]
+    hidden, near, gain, out, left, weights, held, projected, semaphores = refs[2 + count :]
     copies = Copies(semaphores)
-    waits = fetch(copies, lefts, left, pieces, weights, chunks)
+    depth = left.shape[1] // 2
+    size = pieces[0].shape[0]
+    each = depth // size
+    rows = [
+        pl.multiple_of(index // each * depth + table[at + index % each] * size, size)
+        for index in range(count)
+    ]
+    waits = fetch(copies, lefts, left, pieces, rows, weights, chunks)
     width = hidden.shape[1]
     step = width // chunks
     late = copies.start(hidden, held)
@@ -461,23 +461,24 @@
         store.wait()
 
 
-def output(lefts, pieces, near, hidden, gain, chunks=6):
+def output(table, at, lefts, pieces, near, hidden, gain, chunks=6):
     rows, width = hidden.shape
-    columns, depth = lefts[0].shape[1], pieces[0].shape[0]
+    columns = lefts[0].shape[1]
     bf16 = jnp.bfloat16
     return call(
-        functools.partial(output_kernel, chunks),
+        functools.partial(output_kernel, len(pieces), at, chunks),
         "output_norm",
         24,
-        [HBM] * 5 + [VMEM] * 2,
-        [((rows, width), bf16)],
+        [SMEM] + [HBM] * (2 + len(pieces) + 1) + [VMEM] * 2,
+        [((rows, width), bf16, HBM)],
         [
             pltpu.VMEM((rows, 2 * columns), bf16),
-            pltpu.VMEM((2 * depth, width), bf16),
+            pltpu.VMEM((2 * columns, width), bf16),
             pltpu.VMEM((rows, width), bf16),
             pltpu.VMEM((rows, width), jnp.float32),
-            pltpu.SemaphoreType.DMA((3 + 3 * chunks,)),
+            pltpu.SemaphoreType.DMA((3 + (len(pieces) + 1) * chunks,)),
         ],
+        table,
         *lefts,
         *pieces,
         hidden,
@@ -515,6 +516,10 @@
     return parts
 
 
+def came(parts):
+    return [part.array for part in parts if isinstance(part, Came)]
+
+
 def after(array, *others):
     return lax.optimization_barrier((array, *others))[0]
 
@@ -530,24 +535,26 @@
     line = (seq - jnp.arange(lines, dtype=jnp.int32)) % lines
     near_starts = lookup(block_of, 2 * line + chip) * block_rows
     far_starts = lookup(block_of, 2 * line + 1 - chip) * block_rows
-    scalars = jnp.stack([core, group * lines + seq]).astype(jnp.int32)
+    mine, beside = seq % 2, 1 - seq % 2
+    quarters = [(group, mine), (1 - group, mine), (group, beside), (1 - group, beside)]
+    quarters = [2 * a + b for a, b in quarters]
+    scalars = jnp.stack([core, *quarters]).astype(jnp.int32)
     table = jnp.concatenate([scalars, near_starts, far_starts])
-    near_at, far_at = 2, 2 + lines
-
-    share = w_out.shape[0] // (groups * lines)
-    own, own_head, own_tail, w_piece = norm(table, hidden, pre_gain, w_out, cuts, share)
-    partner = flipped(own, "tp", 1)
-    w_piece = flipped(w_piece, "tp", 2)
-    head, tail = flipped(own_head, "tp", 2), flipped(own_tail, "tp", 2)
+    quarter_at, near_at, far_at = 1, 5, 5 + lines
+
+    share = w_out.shape[0] // 4
+    own_head, own_tail, w_quarter = norm(table, hidden, pre_gain, w_out, cuts, share)
+    w_quarter = flipped(w_quarter, "tp", 2)
+    head, tail = flipped(after(own_head, w_quarter), "tp", 2), flipped(own_tail, "tp", 2)
+    partner_head, partner_tail = flipped(own_head, "tp", 1), flipped(own_tail, "tp", 1)
     w_partner = flipped(w_out, "tp", 1)
-    w_far = lax.all_gather(after(w_piece, partner), ("groups", "seq"), axis=0, tiled=True)
+    weights = hold(wq, wk, wv)
 
     run = [jnp.arange(size, dtype=jnp.int32) for size in cuts]
     place = [core * rows + run[0], (1 - core) * rows + run[0]]
     place += [core * rows + cuts[0] + run[1], (1 - core) * rows + cuts[0] + run[1]]
     place = jnp.concatenate(place)
     trig = rotary_table(jnp.concatenate([near_starts[0] + place, far_starts[0] + place]))
-    weights = [wq, wk, wv]
     head_runs = [(0, 0, cuts[0]), (1, 0, cuts[0])]
     tail_runs = [(0, cuts[0], cuts[1]), (1, cuts[0], cuts[1])]
     near_chunk = Chunk(near_at, head_runs + tail_runs, rows)
@@ -556,28 +563,44 @@
 
     q_near, kv_near = qkv(
         [
-            (own, 0, cuts[0]),
-            (Came(partner), 0, cuts[0]),
-            (own, cuts[0], cuts[1]),
-            (Came(partner), cuts[0], cuts[1]),
+            (own_head, 0, cuts[0]),
+            (Came(partner_head), 0, cuts[0]),
+            (own_tail, 0, cuts[1]),
+            (Came(after(partner_tail, w_partner)), 0, cuts[1]),
         ],
         weights,
         trig,
         0,
     )
     near = along_line(kv_near)
+    swap = lambda array: flipped(array, "groups", 1)
+    w_other = swap(w_quarter)
+    w_beside = lax.ppermute(
+        after(w_quarter, *came(near)), "seq", [(i, i ^ 1) for i in range(lines)]
+    )
+    w_last = swap(w_beside)
+    cross_early = [flipped(piece, "tp", 1) for piece in (w_quarter, w_other)]
+    cross_beside = flipped(w_beside, "tp", 1)
+    q_near = after(q_near, w_other)
     (near_state,) = attention(
         [Step(0, 0, others, same=0)], table, [q_near], [near_chunk], [near], [near_chunk], [None]
     )
 
-    head = after(head, *near_state, w_partner)
+    sizes = [cuts[0] * 3 // 8, cuts[0] * 3 // 8, cuts[0] // 4]
+    pieces = list(zip((0, sizes[0], sizes[0] + sizes[1]), sizes))
+    head = after(head, *near_state)
     q_head, kv_head = qkv(
-        [(Came(head), 0, cuts[0]), (Came(flipped(head, "tp", 1)), 0, cuts[0])],
+        [(Came(head), 0, cuts[0])]
+        + [
+            (Came(flipped(head[at : at + size], "tp", 1)), 0, size)
+            for at, size in pieces
+        ],
         weights,
         trig,
         block_rows,
     )
     far_head = along_line(kv_head)
+    q_head = after(q_head, w_beside)
     (head_state,) = attention(
         [Step(0, 1, [], same=0), Step(0, 0, everyone)],
         table,
@@ -588,7 +611,7 @@
         [None],
     )
 
-    tail = after(tail, *head_state, *[part.array for part in far_head[1:]])
+    tail = after(tail, *head_state, *came(far_head))
     q_tail, kv_tail = qkv(
         [(Came(tail), 0, cuts[1]), (Came(flipped(tail, "tp", 1)), 0, cuts[1])],
         weights,
@@ -596,6 +619,7 @@
         block_rows + 2 * cuts[0],
     )
     far_tail = along_line(kv_tail)
+    q_tail = after(q_tail, cross_beside, *cross_early)
     qs, q_chunks = [q_near, q_head, q_tail], [near_chunk, head_chunk, tail_chunk]
     state = attention(
         [
@@ -631,10 +655,14 @@
     )
     cross, same = flipped(cross, "tp", 3), flipped(same, "tp", 2)
     near_sum = output_near([mine, Came(flipped(partners, "tp", 1))], [w_out, Came(w_partner)])
-    w_cross = flipped(after(w_far, mine), "tp", 1)
+    w_last = after(w_last, mine)
+    quarters = [w_quarter, w_other, w_beside, w_last]
+    quarters += [*cross_early, cross_beside, flipped(w_last, "tp", 1)]
     return output(
+        table,
+        quarter_at,
         [Came(same), Came(cross)],
-        [Came(w_far), Came(w_cross)],
+        [Came(piece) for piece in quarters],
         near_sum,
         hidden,
         post_gain.reshape(1, -1),
@@ -649,14 +677,15 @@
     block_rows = rows * lax.axis_size("tp") // 2
     starts = lookup(block_of, block) * block_rows
     table = jnp.concatenate([jnp.zeros(2, jnp.int32), starts])
-    normed = norm(table, hidden, pre_gain, w_out, [], 16, 1)[0]
+    normed = norm(table, hidden, pre_gain, w_out, [rows], 16, 1)[0]
     normed = lax.all_gather(normed, "tp", axis=0, tiled=True)
     place = jnp.arange(block_rows, dtype=jnp.int32)
     trig = rotary_table((starts[:2, None] + place).reshape(-1))
+    weights = hold(wq, wk, wv)
     qs, keys_values = [], []
     for at in range(2):
         first = at * block_rows
-        q, kv = qkv([(normed, first, block_rows)], [wq, wk, wv], trig, first)
+        q, kv = qkv([(normed, first, block_rows)], weights, trig, first)
         qs.append(q)
         keys_values.append(kv)
     kv = lax.all_gather(jnp.stack(keys_values), "seq")[line].reshape(-1, block_rows, 2 * HD)

time: 146 us -> 122 us (0.84); the launches traced: 147 us -> 120 us
  between operations: 13.7 us -> 0.45 us
  waiting for transfers between devices: 50.3 us -> 37.7 us
  Pallas kernels: 53.2 us -> 43.9 us
  starting transfers between devices: 24.6 us -> 33.3 us
    ppermute x9, waiting for transfers between devices: 34.1 us -> 11.4 us  [along_line(): lax.ppermute(array, 'seq', [(i, (i + by) % size) for i in range(size)])]
    pallas_call x10 -> x11, Pallas kernels: 53.2 us -> 43.9 us  [call(): pl.pallas_call(kernel, in_specs=in_specs, out_specs=[spec for _, _, spec...]
    ppermute x0 -> x1, waiting for transfers between devices: none -> 8.14 us  [two_chips(): lax.ppermute(after(w_quarter, *came(near)), 'seq', [(i, i ^ 1) for i in r...]
    ppermute x0 -> x1, starting transfers between devices: none -> 6.73 us  [two_chips(): lax.ppermute(after(w_quarter, *came(near)), 'seq', [(i, i ^ 1) for i in r...]
    ppermute x11 -> x19, starting transfers between devices: 7.34 us -> 11.4 us  [flipped(): return lax.ppermute(array, axis, [(i, i ^ bit) for i in range(size)])]
    ppermute x9, starting transfers between devices: 17.3 us -> 15.2 us  [along_line(): lax.ppermute(array, 'seq', [(i, (i + by) % size) for i in range(size)])]
    ppermute x11 -> x19, waiting for transfers between devices: 16.2 us -> 18.1 us  [flipped(): return lax.ppermute(array, axis, [(i, i ^ bit) for i in range(size)])]
  transfers between devices with their start and end apart: 21 -> 29, of which waited for: 9 -> 9; matrix products, arithmetic and copies ran while one was open for 2% -> 4% of each run, Pallas kernels for 26% -> 32%
where the time goes in v5:
time: 122 us; the launch traced here: 120 us
  Pallas kernels  43.9 us (36%)
  waiting for transfers between devices  37.7 us (31%)
  starting transfers between devices  33.3 us (27%)
  other arithmetic  3.75 us (3%)
    pallas_call x11, Pallas kernels, call(): pl.pallas_call(kernel, in_specs=in_specs, out_specs=[spec for _, _, spec...  43.9 us
    ppermute x19, waiting for transfers between devices, flipped(): return lax.ppermute(array, axis, [(i, i ^ bit) for i in range(size)])  18.1 us
    ppermute x9, starting transfers between devices, along_line(): lax.ppermute(array, 'seq', [(i, (i + by) % size) for i in range(size)])  15.2 us
    ppermute x9, waiting for transfers between devices, along_line(): lax.ppermute(array, 'seq', [(i, (i + by) % size) for i in range(size)])  11.4 us
    ppermute x19, starting transfers between devices, flipped(): return lax.ppermute(array, axis, [(i, i ^ bit) for i in range(size)])  11.4 us
    ppermute x1, waiting for transfers between devices, two_chips(): lax.ppermute(after(w_quarter, *came(near)), 'seq', [(i, i ^ 1) for i in r...  8.14 us
    ppermute x1, starting transfers between devices, two_chips(): lax.ppermute(after(w_quarter, *came(near)), 'seq', [(i, i ^ 1) for i in r...  6.73 us
  transfers between devices with their start and end apart: 29, of which 9 were waited for; matrix products, arithmetic and copies ran while one was open for 4% of the time, Pallas kernels for 32%

profile of v5, /device:TPU:0, one launch (start us, length us, event | category | flops | bytes accessed | tf_op | source)
XLA Modules:
  0.0 120.1 jit_solution(14065945310119617625)
XLA Ops:
  0.5 0.7 reshape.68.gain
  1.2 0.9 select_reduce_fusion
  2.2 3.7 %norm_rows.1 = (bf16[128,4608]{1,0:T(8,128)(2,1)}, bf16[64,4608]{1,0:T(8,128)(2,1)}, bf16[64,4608]{1,0:T(8,128)(2,1)}) custom-call(s32[13]{0:T(128)S(1)} %concatenate.20.table, bf16[192,4608]{1,0:T(8,128)(2,1)} %refs_10_.1, f32[1,4608]{1,0:T(1,128)S(1)} %reshape.68.gain, bf16[256,4608]{1,0:T(8,128)(2,1)} %refs_2_.1), custom_call_target="tpu_custom_call" | custom-call | flops 1 | bytes 1 | tf_op jit(solution)/shard_map/norm_rows/pallas_call | solution.py:37
  5.9 2.6 %collective-permute-start.3 = (bf16[64,4608]{1,0:T(8,128)(2,1)}, bf16[64,4608]{1,0:T(8,128)(2,1)}, u32[]{:S(2)}, u32[]{:S(2)}) collective-permute-start(bf16[64,4608]{1,0:T(8,128)(2,1)} %get-tuple-element.41), channel_id=1, source_target_pairs={{0,8},{4,12},{8,0},{12,4},{1,9},{5,13},{9,1},{13,5},{2,10},{6,14},... | collective-permute-start | bytes 1769480 | tf_op jit(solution)/shard_map/ppermute | solution.py:507
  8.7 14.1 %collective-permute-done.3.refs_2_ = bf16[64,4608]{1,0:T(8,128)(2,1)} collective-permute-done((bf16[64,4608]{1,0:T(8,128)(2,1)}, bf16[64,4608]{1,0:T(8,128)(2,1)}, u32[]{:S(2)}, u32[]{:S(2)}) %collective-permute-start.3) | collective-permute-done | bytes 589856 | tf_op jit(solution)/shard_map/ppermute | solution.py:507
  22.8 1.7 %collective-permute-start.5 = (bf16[128,4608]{1,0:T(8,128)(2,1)}, bf16[128,4608]{1,0:T(8,128)(2,1)S(1)}, u32[]{:S(2)}, u32[]{:S(2)}) collective-permute-start(bf16[128,4608]{1,0:T(8,128)(2,1)} %get-tuple-element.43.refs_0_), channel_id=1, source_target_pairs={{0,8},{4,12},{8,0},{12,4},{1,9},{5,13},{9,1},{13,5},{2,10},{6,14},... | collective-permute-start | bytes 3538952 | tf_op jit(solution)/shard_map/ppermute | solution.py:507
  24.7 1.5 %collective-permute-start.4 = (bf16[64,4608]{1,0:T(8,128)(2,1)}, bf16[64,4608]{1,0:T(8,128)(2,1)S(1)}, u32[]{:S(2)}, u32[]{:S(2)}) collective-permute-start(bf16[64,4608]{1,0:T(8,128)(2,1)} %collective-permute-done.3.refs_2_), channel_id=1, source_target_pairs={{0,16},{16,0},{1,17},{17,1},{2,18},{18,2},{3,19},{19,3},{4,20},{20... | collective-permute-start | bytes 1769480 | tf_op jit(solution)/shard_map/ppermute | solution.py:507
  26.2 2.4 %hold_weights.1.weights = bf16[4608,512]{1,0:T(8,128)(2,1)S(1)} custom-call(bf16[4608,256]{1,0:T(8,128)(2,1)} %wq.1, bf16[4608,128]{1,0:T(8,128)(2,1)} %wk.1, bf16[4608,128]{1,0:T(8,128)(2,1)} %wv.1), custom_call_target="tpu_custom_call" | custom-call | flops 1 | bytes 1 | tf_op jit(solution)/shard_map/hold_weights/pallas_call | solution.py:37
  28.6 1.4 %multiply_cosine_fusion = (f32[768,64]{1,0:T(8,128)S(1)}, f32[768,64]{1,0:T(8,128)S(1)}, f32[768,64]{1,0:T(8,128)S(1)}) fusion(f32[768]{0:T(1024)S(1)} %add_convert_fusion, f32[64]{0:T(128)S(1)} %multiply_power_fusion), kind=kLoop, calls=%fused_computation.2 | loop fusion | flops 98304 | bytes 593152 | tf_op jit(solution)/shard_map/cos | solution.py:496
  30.0 1.3 %pad_maximum_fusion.trig = f32[768,256]{1,0:T(8,128)} fusion(f32[768,64]{1,0:T(8,128)S(1)} %get-tuple-element.75, f32[768,64]{1,0:T(8,128)S(1)} %get-tuple-element.74, f32[768,64]{1,0:T(8,128)S(1)} %get-tuple-element.73), kind=kLoop, calls=%fused_computation | loop fusion | flops 589824 | bytes 1376256 | tf_op jit(solution)/shard_map/concatenate | solution.py:497
  31.3 4.3 %qkv.3 = (bf16[2,384,128]{2,1,0:T(8,128)(2,1)S(1)}, bf16[384,256]{1,0:T(8,128)(2,1)S(1)}) custom-call(bf16[4608,512]{1,0:T(8,128)(2,1)S(1)} %hold_weights.1.weights, f32[768,256]{1,0:T(8,128)} %pad_maximum_fusion.trig, bf16[128,4608]{1,0:T(8,128)(2,1)} %get-tuple-element.43.refs_0_, bf16[128,4608]{1,0:T(8,128)(2,1)} %collective-permute-done.refs_1_, ...), custom_call_target="tpu_custom_call" | custom-call | flops 1 | bytes 1 | tf_op jit(solution)/shard_map/qkv/pallas_call | solution.py:37
  35.6 1.6 %collective-permute-start.6 = (bf16[384,256]{1,0:T(8,128)(2,1)S(1)}, bf16[384,256]{1,0:T(8,128)(2,1)S(1)}, u32[]{:S(2)}, u32[]{:S(2)}) collective-permute-start(bf16[384,256]{1,0:T(8,128)(2,1)S(1)} %get-tuple-element.44), channel_id=1, source_target_pairs={{0,1},{1,2},{2,3},{3,0},{4,5},{5,6},{6,7},{7,4},{8,9},{9,10},{10,1... | collective-permute-start | bytes 589832 | tf_op jit(solution)/shard_map/ppermute | solution.py:514
  37.2 2.6 %collective-permute-start.7 = (bf16[384,256]{1,0:T(8,128)(2,1)S(1)}, bf16[384,256]{1,0:T(8,128)(2,1)S(1)}, u32[]{:S(2)}, u32[]{:S(2)}) collective-permute-start(bf16[384,256]{1,0:T(8,128)(2,1)S(1)} %get-tuple-element.44), channel_id=1, source_target_pairs={{0,2},{1,3},{2,0},{3,1},{4,6},{5,7},{6,4},{7,5},{8,10},{9,11},{10,... | collective-permute-start | bytes 589832 | tf_op jit(solution)/shard_map/ppermute | solution.py:514
  39.8 1.3 %collective-permute-start.8 = (bf16[384,256]{1,0:T(8,128)(2,1)S(1)}, bf16[384,256]{1,0:T(8,128)(2,1)S(1)}, u32[]{:S(2)}, u32[]{:S(2)}) collective-permute-start(bf16[384,256]{1,0:T(8,128)(2,1)S(1)} %get-tuple-element.44), channel_id=1, source_target_pairs={{0,3},{1,0},{2,1},{3,2},{4,7},{5,4},{6,5},{7,6},{8,11},{9,8},{10,9... | collective-permute-start | bytes 589832 | tf_op jit(solution)/shard_map/ppermute | solution.py:514
  41.7 3.6 %collective-permute-done.6 = bf16[384,256]{1,0:T(8,128)(2,1)S(1)} collective-permute-done((bf16[384,256]{1,0:T(8,128)(2,1)S(1)}, bf16[384,256]{1,0:T(8,128)(2,1)S(1)}, u32[]{:S(2)}, u32[]{:S(2)}) %collective-permute-start.6) | collective-permute-done | bytes 196640 | tf_op jit(solution)/shard_map/ppermute | solution.py:514
  45.3 7.8 %collective-permute-done.7 = bf16[384,256]{1,0:T(8,128)(2,1)S(1)} collective-permute-done((bf16[384,256]{1,0:T(8,128)(2,1)S(1)}, bf16[384,256]{1,0:T(8,128)(2,1)S(1)}, u32[]{:S(2)}, u32[]{:S(2)}) %collective-permute-start.7) | collective-permute-done | bytes 196640 | tf_op jit(solution)/shard_map/ppermute | solution.py:514
  53.1 2.6 %attention.4 = (f32[768,128]{1,0:T(8,128)S(1)}, f32[768,256]{1,0:T(8,128)S(1)}) custom-call(s32[13]{0:T(128)S(1)} %concatenate.20.table, bf16[2,384,128]{2,1,0:T(8,128)(2,1)S(1)} %get-tuple-element.42.refs_0_, bf16[1,384,256]{2,1,0:T(8,128)(2,1)S(1)} %bitcast.21, bf16[1,384,256]{2,1,0:T(8,128)(2,1)S(1)} %bitcast.24, bf16[1,384,256]{2,1,0:T(8,128)(2,1)S(1)} %bitcast.27, ...), custom_call_target="tpu_custom_call" | custom-call | flops 1 | bytes 1 | tf_op jit(solution)/shard_map/attention/pallas_call | solution.py:37
  55.7 6.7 %collective-permute-start.12 = (bf16[64,4608]{1,0:T(8,128)(2,1)}, bf16[64,4608]{1,0:T(8,128)(2,1)S(1)}, u32[]{:S(2)}, u32[]{:S(2)}) collective-permute-start(bf16[64,4608]{1,0:T(8,128)(2,1)} %collective-permute-done.3.refs_2_), channel_id=1, source_target_pairs={{0,1},{1,0},{2,3},{3,2},{4,5},{5,4},{6,7},{7,6},{8,9},{9,8},{10,11... | collective-permute-start | bytes 1769480 | tf_op jit(solution)/shard_map/ppermute | solution.py:578
  63.3 2.2 %collective-permute-done.11.refs_3_ = bf16[32,4608]{1,0:T(8,128)(2,1)S(1)} collective-permute-done((bf16[32,4608]{1,0:T(8,128)(2,1)S(1)}, bf16[32,4608]{1,0:T(8,128)(2,1)S(1)}, u32[]{:S(2)}, u32[]{:S(2)}) %collective-permute-start.11) | collective-permute-done | bytes 294944 | tf_op jit(solution)/shard_map/ppermute | solution.py:507
  65.4 3.3 %qkv.4 = (bf16[2,256,128]{2,1,0:T(8,128)(2,1)S(1)}, bf16[256,256]{1,0:T(8,128)(2,1)S(1)}) custom-call(bf16[4608,512]{1,0:T(8,128)(2,1)S(1)} %hold_weights.1.weights, f32[768,256]{1,0:T(8,128)} %pad_maximum_fusion.trig, bf16[128,4608]{1,0:T(8,128)(2,1)S(1)} %collective-permute-done.5.refs_0_, bf16[48,4608]{1,0:T(8,128)(2,1)S(1)} %collective-permute-done.9.refs_1_, ...), custom_call_target="tpu_custom_call" | custom-call | flops 1 | bytes 1 | tf_op jit(solution)/shard_map/qkv/pallas_call | solution.py:37
  68.8 2.6 %collective-permute-start.15 = (bf16[256,256]{1,0:T(8,128)(2,1)S(1)}, bf16[256,256]{1,0:T(8,128)(2,1)S(1)}, u32[]{:S(2)}, u32[]{:S(2)}) collective-permute-start(bf16[256,256]{1,0:T(8,128)(2,1)S(1)} %get-tuple-element.51), channel_id=1, source_target_pairs={{0,2},{1,3},{2,0},{3,1},{4,6},{5,7},{6,4},{7,5},{8,10},{9,11},{10,... | collective-permute-start | bytes 393224 | tf_op jit(solution)/shard_map/ppermute | solution.py:514
  71.4 2.8 %collective-permute-start.16 = (bf16[256,256]{1,0:T(8,128)(2,1)S(1)}, bf16[256,256]{1,0:T(8,128)(2,1)S(1)}, u32[]{:S(2)}, u32[]{:S(2)}) collective-permute-start(bf16[256,256]{1,0:T(8,128)(2,1)S(1)} %get-tuple-element.51), channel_id=1, source_target_pairs={{0,3},{1,0},{2,1},{3,2},{4,7},{5,4},{6,5},{7,6},{8,11},{9,8},{10,9... | collective-permute-start | bytes 393224 | tf_op jit(solution)/shard_map/ppermute | solution.py:514
  74.3 8.1 %collective-permute-done.12.refs_4_ = bf16[64,4608]{1,0:T(8,128)(2,1)S(1)} collective-permute-done((bf16[64,4608]{1,0:T(8,128)(2,1)}, bf16[64,4608]{1,0:T(8,128)(2,1)S(1)}, u32[]{:S(2)}, u32[]{:S(2)}) %collective-permute-start.12) | collective-permute-done | bytes 589856 | tf_op jit(solution)/shard_map/ppermute | solution.py:578
  82.4 4.9 %attention.5 = (f32[512,128]{1,0:T(8,128)S(1)}, f32[512,256]{1,0:T(8,128)S(1)}) custom-call(s32[13]{0:T(128)S(1)} %concatenate.20.table, bf16[2,256,128]{2,1,0:T(8,128)(2,1)S(1)} %get-tuple-element.50.refs_0_.refs_1_, bf16[1,384,256]{2,1,0:T(8,128)(2,1)S(1)} %bitcast.22, bf16[1,384,256]{2,1,0:T(8,128)(2,1)S(1)} %bitcast.25, ...), custom_call_target="tpu_custom_call" | custom-call | flops 1 | bytes 1 | tf_op jit(solution)/shard_map/attention/pallas_call | solution.py:37
  89.5 2.0 %qkv.5 = (bf16[2,128,128]{2,1,0:T(8,128)(2,1)S(1)}, bf16[128,256]{1,0:T(8,128)(2,1)S(1)}) custom-call(bf16[4608,512]{1,0:T(8,128)(2,1)S(1)} %hold_weights.1.weights, f32[768,256]{1,0:T(8,128)} %pad_maximum_fusion.trig, bf16[64,4608]{1,0:T(8,128)(2,1)S(1)} %collective-permute-done.13.refs_0_, bf16[64,4608]{1,0:T(8,128)(2,1)S(1)} %collective-permute-done.17.refs_1_), custom_call_target="tpu_custom_call" | custom-call | flops 1 | bytes 1 | tf_op jit(solution)/shard_map/qkv/pallas_call | solution.py:37
  91.6 2.0 %collective-permute-start.22 = (bf16[128,256]{1,0:T(8,128)(2,1)S(1)}, bf16[128,256]{1,0:T(8,128)(2,1)S(1)}, u32[]{:S(2)}, u32[]{:S(2)}) collective-permute-start(bf16[128,256]{1,0:T(8,128)(2,1)S(1)} %get-tuple-element.57), channel_id=1, source_target_pairs={{0,2},{1,3},{2,0},{3,1},{4,6},{5,7},{6,4},{7,5},{8,10},{9,11},{10,... | collective-permute-start | bytes 196616 | tf_op jit(solution)/shard_map/ppermute | solution.py:514
  93.6 2.0 %collective-permute-start.23 = (bf16[128,256]{1,0:T(8,128)(2,1)S(1)}, bf16[128,256]{1,0:T(8,128)(2,1)S(1)}, u32[]{:S(2)}, u32[]{:S(2)}) collective-permute-start(bf16[128,256]{1,0:T(8,128)(2,1)S(1)} %get-tuple-element.57), channel_id=1, source_target_pairs={{0,3},{1,0},{2,1},{3,2},{4,7},{5,4},{6,5},{7,6},{8,11},{9,8},{10,9... | collective-permute-start | bytes 196616 | tf_op jit(solution)/shard_map/ppermute | solution.py:514
  95.7 8.3 %attention.6 = (f32[768,128]{1,0:T(8,128)S(1)}, f32[768,256]{1,0:T(8,128)S(1)}, f32[512,128]{1,0:T(8,128)S(1)}, f32[512,256]{1,0:T(8,128)S(1)}, f32[256,128]{1,0:T(8,128)S(1)}, /*index=5*/f32[256,256]{1,0:T(8,128)S(1)}) custom-call(s32[13]{0:T(128)S(1)} %concatenate.20.table, ...), custom_call_target="tpu_custom_call", output_to_operand_aliasing={{0}: (13, {}), {1}: (14, {}), {2}: (15, {}), {3}: (16, {})} | custom-call | flops 1 | bytes 1 | tf_op jit(solution)/shard_map/attention/pallas_call | solution.py:37
  104.0 3.4 %attention.7 = (bf16[192,256]{1,0:T(8,128)(2,1)}, bf16[192,256]{1,0:T(8,128)(2,1)}, bf16[192,256]{1,0:T(8,128)(2,1)}, bf16[192,256]{1,0:T(8,128)(2,1)}, f32[768,...) custom-call(s32[13]{0:T(128)S(1)} %concatenate.20.table, ...), custom_call_target="tpu_custom_call", output_to_operand_aliasing={{4}: (8, {}), {5}: (9, {}), {6}: (10, {}), {7}: (11, {}), {... | custom-call | flops 1 | bytes 1 | tf_op jit(solution)/shard_map/attention/pallas_call | solution.py:37
  108.0 1.4 %collective-permute-start.25 = (bf16[192,256]{1,0:T(8,128)(2,1)}, bf16[192,256]{1,0:T(8,128)(2,1)S(1)}, u32[]{:S(2)}, u32[]{:S(2)}) collective-permute-start(bf16[192,256]{1,0:T(8,128)(2,1)} %get-tuple-element.65), channel_id=1, source_target_pairs={{0,12},{4,8},{8,4},{12,0},{1,13},{5,9},{9,5},{13,1},{2,14},{6,10},... | collective-permute-start | bytes 294920 | tf_op jit(solution)/shard_map/ppermute | solution.py:507
  109.9 3.4 %output_near.1.refs_11_ = bf16[192,4608]{1,0:T(8,128)(2,1)S(1)} custom-call(bf16[192,256]{1,0:T(8,128)(2,1)} %get-tuple-element.66.refs_0_, bf16[192,256]{1,0:T(8,128)(2,1)S(1)} %collective-permute-done.28.refs_1_, bf16[256,4608]{1,0:T(8,128)(2,1)} %refs_2_.1, bf16[256,4608]{1,0:T(8,128)(2,1)S(1)} %collective-permute-done.2.refs_3_), custom_call_target="tpu_custom_call" | custom-call | flops 1 | bytes 1 | tf_op jit(solution)/shard_map/output_near/pallas_call | solution.py:37
  114.2 5.7 %output_norm.1 = bf16[192,4608]{1,0:T(8,128)(2,1)} custom-call(s32[13]{0:T(128)S(1)} %concatenate.20.table, bf16[192,256]{1,0:T(8,128)(2,1)S(1)} %collective-permute-done.24.refs_0_, bf16[192,256]{1,0:T(8,128)(2,1)S(1)} %collective-permute-done.25.refs_1_, bf16[64,4608]{1,0:T(8,128)(2,1)} %collective-permute-done.3.refs_2_, ...), custom_call_target="tpu_custom_call" | custom-call | flops 1 | bytes 1 | tf_op jit(solution)/shard_map/output_norm/pallas_call | solution.py:37
  (57 shorter events, 6.5 us)
Async XLA Ops:
  0.0 31.3 %collective-permute-start.2 = (bf16[256,4608]{1,0:T(8,128)(2,1)}, bf16[256,4608]{1,0:T(8,128)(2,1)S(1)}, u32[]{:S(2)}, u32[]{:S(2)}) collective-permute-start(bf16[256,4608]{1,0:T(8,128)(2,1)} %refs_2_.1), channel_id=1, source_target_pairs={{0,4},{4,0},{8,12},{12,8},{1,5},{5,1},{9,13},{13,9},{2,6},{6,2},{1... | collective-permute-start | bytes 7077896 | tf_op jit(solution)/shard_map/ppermute | solution.py:507
  5.9 16.9 %collective-permute-start.3 = (bf16[64,4608]{1,0:T(8,128)(2,1)}, bf16[64,4608]{1,0:T(8,128)(2,1)}, u32[]{:S(2)}, u32[]{:S(2)}) collective-permute-start(bf16[64,4608]{1,0:T(8,128)(2,1)} %get-tuple-element.41), channel_id=1, source_target_pairs={{0,8},{4,12},{8,0},{12,4},{1,9},{5,13},{9,1},{13,5},{2,10},{6,14},... | collective-permute-start | bytes 1769480 | tf_op jit(solution)/shard_map/ppermute | solution.py:507
  8.5 22.9 %collective-permute-start = (bf16[128,4608]{1,0:T(8,128)(2,1)}, bf16[128,4608]{1,0:T(8,128)(2,1)}, u32[]{:S(2)}, u32[]{:S(2)}) collective-permute-start(bf16[128,4608]{1,0:T(8,128)(2,1)} %get-tuple-element.43.refs_0_), channel_id=1, source_target_pairs={{0,4},{4,0},{8,12},{12,8},{1,5},{5,1},{9,13},{13,9},{2,6},{6,2},{1... | collective-permute-start | bytes 3538952 | tf_op jit(solution)/shard_map/ppermute | solution.py:507
  22.8 32.9 %collective-permute-start.5 = (bf16[128,4608]{1,0:T(8,128)(2,1)}, bf16[128,4608]{1,0:T(8,128)(2,1)S(1)}, u32[]{:S(2)}, u32[]{:S(2)}) collective-permute-start(bf16[128,4608]{1,0:T(8,128)(2,1)} %get-tuple-element.43.refs_0_), channel_id=1, source_target_pairs={{0,8},{4,12},{8,0},{12,4},{1,9},{5,13},{9,1},{13,5},{2,10},{6,14},... | collective-permute-start | bytes 3538952 | tf_op jit(solution)/shard_map/ppermute | solution.py:507
  24.5 6.8 %collective-permute-start.1 = (bf16[64,4608]{1,0:T(8,128)(2,1)}, bf16[64,4608]{1,0:T(8,128)(2,1)}, u32[]{:S(2)}, u32[]{:S(2)}) collective-permute-start(bf16[64,4608]{1,0:T(8,128)(2,1)} %get-tuple-element.38.refs_2_), channel_id=1, source_target_pairs={{0,4},{4,0},{8,12},{12,8},{1,5},{5,1},{9,13},{13,9},{2,6},{6,2},{1... | collective-permute-start | bytes 1769480 | tf_op jit(solution)/shard_map/ppermute | solution.py:507
  24.7 16.5 %collective-permute-start.4 = (bf16[64,4608]{1,0:T(8,128)(2,1)}, bf16[64,4608]{1,0:T(8,128)(2,1)S(1)}, u32[]{:S(2)}, u32[]{:S(2)}) collective-permute-start(bf16[64,4608]{1,0:T(8,128)(2,1)} %collective-permute-done.3.refs_2_), channel_id=1, source_target_pairs={{0,16},{16,0},{1,17},{17,1},{2,18},{18,2},{3,19},{19,3},{4,20},{20... | collective-permute-start | bytes 1769480 | tf_op jit(solution)/shard_map/ppermute | solution.py:507
  31.3 9.9 %copy-start = (bf16[64,4608]{1,0:T(8,128)(2,1)S(1)}, bf16[64,4608]{1,0:T(8,128)(2,1)}, u32[]{:S(2)}) copy-start(bf16[64,4608]{1,0:T(8,128)(2,1)} %get-tuple-element.38.refs_2_) | copy-start | bytes 1769476
  35.6 9.7 %collective-permute-start.6 = (bf16[384,256]{1,0:T(8,128)(2,1)S(1)}, bf16[384,256]{1,0:T(8,128)(2,1)S(1)}, u32[]{:S(2)}, u32[]{:S(2)}) collective-permute-start(bf16[384,256]{1,0:T(8,128)(2,1)S(1)} %get-tuple-element.44), channel_id=1, source_target_pairs={{0,1},{1,2},{2,3},{3,0},{4,5},{5,6},{6,7},{7,4},{8,9},{9,10},{10,1... | collective-permute-start | bytes 589832 | tf_op jit(solution)/shard_map/ppermute | solution.py:514
  37.2 15.9 %collective-permute-start.7 = (bf16[384,256]{1,0:T(8,128)(2,1)S(1)}, bf16[384,256]{1,0:T(8,128)(2,1)S(1)}, u32[]{:S(2)}, u32[]{:S(2)}) collective-permute-start(bf16[384,256]{1,0:T(8,128)(2,1)S(1)} %get-tuple-element.44), channel_id=1, source_target_pairs={{0,2},{1,3},{2,0},{3,1},{4,6},{5,7},{6,4},{7,5},{8,10},{9,11},{10,... | collective-permute-start | bytes 589832 | tf_op jit(solution)/shard_map/ppermute | solution.py:514
  39.8 13.3 %collective-permute-start.8 = (bf16[384,256]{1,0:T(8,128)(2,1)S(1)}, bf16[384,256]{1,0:T(8,128)(2,1)S(1)}, u32[]{:S(2)}, u32[]{:S(2)}) collective-permute-start(bf16[384,256]{1,0:T(8,128)(2,1)S(1)} %get-tuple-element.44), channel_id=1, source_target_pairs={{0,3},{1,0},{2,1},{3,2},{4,7},{5,4},{6,5},{7,6},{8,11},{9,8},{10,9... | collective-permute-start | bytes 589832 | tf_op jit(solution)/shard_map/ppermute | solution.py:514
  41.2 46.1 %collective-permute-start.13 = (bf16[64,4608]{1,0:T(8,128)(2,1)S(1)}, bf16[64,4608]{1,0:T(8,128)(2,1)S(1)}, u32[]{:S(2)}, u32[]{:S(2)}) collective-permute-start(bf16[64,4608]{1,0:T(8,128)(2,1)S(1)} %copy-done), channel_id=1, source_target_pairs={{0,8},{4,12},{8,0},{12,4},{1,9},{5,13},{9,1},{13,5},{2,10},{6,14},... | collective-permute-start | bytes 1769480 | tf_op jit(solution)/shard_map/ppermute | solution.py:507
  55.7 26.7 %collective-permute-start.12 = (bf16[64,4608]{1,0:T(8,128)(2,1)}, bf16[64,4608]{1,0:T(8,128)(2,1)S(1)}, u32[]{:S(2)}, u32[]{:S(2)}) collective-permute-start(bf16[64,4608]{1,0:T(8,128)(2,1)} %collective-permute-done.3.refs_2_), channel_id=1, source_target_pairs={{0,1},{1,0},{2,3},{3,2},{4,5},{5,4},{6,7},{7,6},{8,9},{9,8},{10,11... | collective-permute-start | bytes 1769480 | tf_op jit(solution)/shard_map/ppermute | solution.py:578
  62.5 2.9 %collective-permute-start.9 = (bf16[48,4608]{1,0:T(8,128)(2,1)S(1)}, bf16[48,4608]{1,0:T(8,128)(2,1)S(1)}, u32[]{:S(2)}, u32[]{:S(2)}) collective-permute-start(bf16[48,4608]{1,0:T(8,128)(2,1)S(1)} %get-tuple-element.72), channel_id=1, source_target_pairs={{0,4},{4,0},{8,12},{12,8},{1,5},{5,1},{9,13},{13,9},{2,6},{6,2},{1... | collective-permute-start | bytes 1327112 | tf_op jit(solution)/shard_map/ppermute | solution.py:507
  62.6 2.8 %collective-permute-start.10 = (bf16[48,4608]{1,0:T(8,128)(2,1)S(1)}, bf16[48,4608]{1,0:T(8,128)(2,1)S(1)}, u32[]{:S(2)}, u32[]{:S(2)}) collective-permute-start(bf16[48,4608]{1,0:T(8,128)(2,1)S(1)} %get-tuple-element.71), channel_id=1, source_target_pairs={{0,4},{4,0},{8,12},{12,8},{1,5},{5,1},{9,13},{13,9},{2,6},{6,2},{1... | collective-permute-start | bytes 1327112 | tf_op jit(solution)/shard_map/ppermute | solution.py:507
  63.1 2.3 %collective-permute-start.11 = (bf16[32,4608]{1,0:T(8,128)(2,1)S(1)}, bf16[32,4608]{1,0:T(8,128)(2,1)S(1)}, u32[]{:S(2)}, u32[]{:S(2)}) collective-permute-start(bf16[32,4608]{1,0:T(8,128)(2,1)S(1)} %slice.19), channel_id=1, source_target_pairs={{0,4},{4,0},{8,12},{12,8},{1,5},{5,1},{9,13},{13,9},{2,6},{6,2},{1... | collective-permute-start | bytes 884744 | tf_op jit(solution)/shard_map/ppermute | solution.py:507
  68.7 18.6 %collective-permute-start.14 = (bf16[256,256]{1,0:T(8,128)(2,1)S(1)}, bf16[256,256]{1,0:T(8,128)(2,1)S(1)}, u32[]{:S(2)}, u32[]{:S(2)}) collective-permute-start(bf16[256,256]{1,0:T(8,128)(2,1)S(1)} %get-tuple-element.51), channel_id=1, source_target_pairs={{0,1},{1,2},{2,3},{3,0},{4,5},{5,6},{6,7},{7,4},{8,9},{9,10},{10,1... | collective-permute-start | bytes 393224 | tf_op jit(solution)/shard_map/ppermute | solution.py:514
  68.8 18.5 %collective-permute-start.15 = (bf16[256,256]{1,0:T(8,128)(2,1)S(1)}, bf16[256,256]{1,0:T(8,128)(2,1)S(1)}, u32[]{:S(2)}, u32[]{:S(2)}) collective-permute-start(bf16[256,256]{1,0:T(8,128)(2,1)S(1)} %get-tuple-element.51), channel_id=1, source_target_pairs={{0,2},{1,3},{2,0},{3,1},{4,6},{5,7},{6,4},{7,5},{8,10},{9,11},{10,... | collective-permute-start | bytes 393224 | tf_op jit(solution)/shard_map/ppermute | solution.py:514
  71.4 15.9 %collective-permute-start.16 = (bf16[256,256]{1,0:T(8,128)(2,1)S(1)}, bf16[256,256]{1,0:T(8,128)(2,1)S(1)}, u32[]{:S(2)}, u32[]{:S(2)}) collective-permute-start(bf16[256,256]{1,0:T(8,128)(2,1)S(1)} %get-tuple-element.51), channel_id=1, source_target_pairs={{0,3},{1,0},{2,1},{3,2},{4,7},{5,4},{6,5},{7,6},{8,11},{9,8},{10,9... | collective-permute-start | bytes 393224 | tf_op jit(solution)/shard_map/ppermute | solution.py:514
  87.4 2.1 %collective-permute-start.17 = (bf16[64,4608]{1,0:T(8,128)(2,1)S(1)}, bf16[64,4608]{1,0:T(8,128)(2,1)S(1)}, u32[]{:S(2)}, u32[]{:S(2)}) collective-permute-start(bf16[64,4608]{1,0:T(8,128)(2,1)S(1)} %collective-permute-done.13.refs_0_), channel_id=1, source_target_pairs={{0,4},{4,0},{8,12},{12,8},{1,5},{5,1},{9,13},{13,9},{2,6},{6,2},{1... | collective-permute-start | bytes 1769480 | tf_op jit(solution)/shard_map/ppermute | solution.py:507
  87.4 4.2 %collective-permute-start.19 = (bf16[64,4608]{1,0:T(8,128)(2,1)}, bf16[64,4608]{1,0:T(8,128)(2,1)S(1)}, u32[]{:S(2)}, u32[]{:S(2)}) collective-permute-start(bf16[64,4608]{1,0:T(8,128)(2,1)} %collective-permute-done.3.refs_2_), channel_id=1, source_target_pairs={{0,4},{4,0},{8,12},{12,8},{1,5},{5,1},{9,13},{13,9},{2,6},{6,2},{1... | collective-permute-start | bytes 1769480 | tf_op jit(solution)/shard_map/ppermute | solution.py:507
  87.9 5.7 %collective-permute-start.20 = (bf16[64,4608]{1,0:T(8,128)(2,1)S(1)}, bf16[64,4608]{1,0:T(8,128)(2,1)S(1)}, u32[]{:S(2)}, u32[]{:S(2)}) collective-permute-start(bf16[64,4608]{1,0:T(8,128)(2,1)S(1)} %collective-permute-done.4.refs_3_), channel_id=1, source_target_pairs={{0,4},{4,0},{8,12},{12,8},{1,5},{5,1},{9,13},{13,9},{2,6},{6,2},{1... | collective-permute-start | bytes 1769480 | tf_op jit(solution)/shard_map/ppermute | solution.py:507
  88.0 7.6 %collective-permute-start.18 = (bf16[64,4608]{1,0:T(8,128)(2,1)S(1)}, bf16[64,4608]{1,0:T(8,128)(2,1)S(1)}, u32[]{:S(2)}, u32[]{:S(2)}) collective-permute-start(bf16[64,4608]{1,0:T(8,128)(2,1)S(1)} %collective-permute-done.12.refs_4_), channel_id=1, source_target_pairs={{0,4},{4,0},{8,12},{12,8},{1,5},{5,1},{9,13},{13,9},{2,6},{6,2},{1... | collective-permute-start | bytes 1769480 | tf_op jit(solution)/shard_map/ppermute | solution.py:507
  88.4 19.0 %collective-permute-start.26 = (bf16[64,4608]{1,0:T(8,128)(2,1)S(1)}, bf16[64,4608]{1,0:T(8,128)(2,1)S(1)}, u32[]{:S(2)}, u32[]{:S(2)}) collective-permute-start(bf16[64,4608]{1,0:T(8,128)(2,1)S(1)} %collective-permute-done.12.refs_4_), channel_id=1, source_target_pairs={{0,16},{16,0},{1,17},{17,1},{2,18},{18,2},{3,19},{19,3},{4,20},{20... | collective-permute-start | bytes 1769480 | tf_op jit(solution)/shard_map/ppermute | solution.py:507
  91.5 12.4 %collective-permute-start.21 = (bf16[128,256]{1,0:T(8,128)(2,1)S(1)}, bf16[128,256]{1,0:T(8,128)(2,1)S(1)}, u32[]{:S(2)}, u32[]{:S(2)}) collective-permute-start(bf16[128,256]{1,0:T(8,128)(2,1)S(1)} %get-tuple-element.57), channel_id=1, source_target_pairs={{0,1},{1,2},{2,3},{3,0},{4,5},{5,6},{6,7},{7,4},{8,9},{9,10},{10,1... | collective-permute-start | bytes 196616 | tf_op jit(solution)/shard_map/ppermute | solution.py:514
  91.6 12.4 %collective-permute-start.22 = (bf16[128,256]{1,0:T(8,128)(2,1)S(1)}, bf16[128,256]{1,0:T(8,128)(2,1)S(1)}, u32[]{:S(2)}, u32[]{:S(2)}) collective-permute-start(bf16[128,256]{1,0:T(8,128)(2,1)S(1)} %get-tuple-element.57), channel_id=1, source_target_pairs={{0,2},{1,3},{2,0},{3,1},{4,6},{5,7},{6,4},{7,5},{8,10},{9,11},{10,... | collective-permute-start | bytes 196616 | tf_op jit(solution)/shard_map/ppermute | solution.py:514
  93.6 10.4 %collective-permute-start.23 = (bf16[128,256]{1,0:T(8,128)(2,1)S(1)}, bf16[128,256]{1,0:T(8,128)(2,1)S(1)}, u32[]{:S(2)}, u32[]{:S(2)}) collective-permute-start(bf16[128,256]{1,0:T(8,128)(2,1)S(1)} %get-tuple-element.57), channel_id=1, source_target_pairs={{0,3},{1,0},{2,1},{3,2},{4,7},{5,4},{6,5},{7,6},{8,11},{9,8},{10,9... | collective-permute-start | bytes 196616 | tf_op jit(solution)/shard_map/ppermute | solution.py:514
  104.0 5.5 %copy-start.1 = (f32[4608]{0:T(1024)S(1)}, f32[4608]{0:T(1024)}, u32[]{:S(2)}) copy-start(f32[4608]{0:T(1024)} %param.10) | copy-start | bytes 55300
  107.4 6.8 %collective-permute-start.27 = (bf16[64,4608]{1,0:T(8,128)(2,1)S(1)}, bf16[64,4608]{1,0:T(8,128)(2,1)S(1)}, u32[]{:S(2)}, u32[]{:S(2)}) collective-permute-start(bf16[64,4608]{1,0:T(8,128)(2,1)S(1)} %collective-permute-done.26.refs_5_), channel_id=1, source_target_pairs={{0,4},{4,0},{8,12},{12,8},{1,5},{5,1},{9,13},{13,9},{2,6},{6,2},{1... | collective-permute-start | bytes 1769480 | tf_op jit(solution)/shard_map/ppermute | solution.py:507
  107.5 2.3 %collective-permute-start.28 = (bf16[192,256]{1,0:T(8,128)(2,1)}, bf16[192,256]{1,0:T(8,128)(2,1)S(1)}, u32[]{:S(2)}, u32[]{:S(2)}) collective-permute-start(bf16[192,256]{1,0:T(8,128)(2,1)} %get-tuple-element.68), channel_id=1, source_target_pairs={{0,4},{4,0},{8,12},{12,8},{1,5},{5,1},{9,13},{13,9},{2,6},{6,2},{1... | collective-permute-start | bytes 294920 | tf_op jit(solution)/shard_map/ppermute | solution.py:507
  108.0 5.9 %collective-permute-start.24 = (bf16[192,256]{1,0:T(8,128)(2,1)}, bf16[192,256]{1,0:T(8,128)(2,1)S(1)}, u32[]{:S(2)}, u32[]{:S(2)}) collective-permute-start(bf16[192,256]{1,0:T(8,128)(2,1)} %get-tuple-element.64), channel_id=1, source_target_pairs={{0,8},{4,12},{8,0},{12,4},{1,9},{5,13},{9,1},{13,5},{2,10},{6,14},... | collective-permute-start | bytes 294920 | tf_op jit(solution)/shard_map/ppermute | solution.py:507
  108.0 6.2 %collective-permute-start.25 = (bf16[192,256]{1,0:T(8,128)(2,1)}, bf16[192,256]{1,0:T(8,128)(2,1)S(1)}, u32[]{:S(2)}, u32[]{:S(2)}) collective-permute-start(bf16[192,256]{1,0:T(8,128)(2,1)} %get-tuple-element.65), channel_id=1, source_target_pairs={{0,12},{4,8},{8,4},{12,0},{1,13},{5,9},{9,5},{13,1},{2,14},{6,10},... | collective-permute-start | bytes 294920 | tf_op jit(solution)/shard_map/ppermute | solution.py:507

commit v6 on v5

--- a/solution.py
+++ b/solution.py
@@ -58,19 +58,15 @@
         return copy
 
 
-def norm_kernel(cuts, pieces, table, hidden, gain, w_out, *refs):
-    parts = refs[: len(cuts)]
-    w_piece, rows, staged, bounced, semaphores = refs[len(cuts) :]
+def norm_kernel(cuts, pieces, hidden, gain, *refs):
+    parts, (rows, staged, semaphores) = refs[: len(cuts)], refs[len(cuts) :]
     copies = Copies(semaphores)
     count, width = hidden.shape
     step = count // pieces
     spans = [pl.ds(at * step, step) for at in range(pieces)]
     ins = [copies.start(hidden.at[span], rows.at[span]) for span in spans]
-    size = w_piece.shape[0]
-    first = pl.multiple_of(table[1] * size, size)
-    piece = copies.start(w_out.at[pl.ds(first, size)], bounced)
+    scale = gain[...].reshape(1, width)
     outs = []
-    scale = gain[...]
     for at, span in enumerate(spans):
         ins[at].wait()
         x = rows[span, :].astype(jnp.float32)
@@ -86,32 +82,26 @@
                 inside = pl.ds(at * step - begin, step)
                 outs.append(copies.start(staged.at[span], part.at[inside]))
             begin += cut
-    piece.wait()
-    outs.append(copies.start(bounced, w_piece))
     for copy in outs:
         copy.wait()
 
 
-def norm(table, hidden, gain, w_out, cuts, share, pieces=3):
+def norm(hidden, gain, cuts, pieces=3):
     rows, width = hidden.shape
     bf16 = jnp.bfloat16
-    outs = [((cut, width), bf16, HBM) for cut in cuts]
     return call(
         functools.partial(norm_kernel, cuts, pieces),
         "norm_rows",
         12,
-        [SMEM, HBM, VMEM, HBM],
-        outs + [((share, width), bf16, HBM)],
+        [HBM, VMEM],
+        [((cut, width), bf16, HBM) for cut in cuts],
         [
             pltpu.VMEM((rows, width), bf16),
             pltpu.VMEM((rows, width), bf16),
-            pltpu.VMEM((share, width), bf16),
-            pltpu.SemaphoreType.DMA((2 + 2 * pieces,)),
-        ],
-        table,
+            pltpu.SemaphoreType.DMA((2 * pieces,)),
+        ],
         hidden,
-        gain.reshape(1, -1),
-        w_out,
+        gain,
     )
 
 
@@ -366,123 +356,198 @@
     return [tuple(results[2 * at : 2 * at + 2]) for at in range(len(qs))]
 
 
-def fetch(copies, lefts, left, pieces, rows, weights, chunks):
-    columns = lefts[0].shape[1]
-    step = weights.shape[1] // chunks
-    first = [
-        copies.start(part, left.at[:, pl.ds(at * columns, columns)])
-        for at, part in enumerate(lefts)
+def cut_kernel(pieces, at, table, weights, *refs):
+    outs, (held, semaphores) = refs[:pieces], refs[pieces:]
+    copies = Copies(semaphores)
+    size = outs[0].shape[0]
+    half = size * pieces
+    first = pl.multiple_of(table[at] * half, half)
+    ins = [
+        copies.start(
+            weights.at[pl.ds(first + piece * size, size)], held.at[pl.ds(piece * size, size)]
+        )
+        for piece in range(pieces)
     ]
-    waits = []
-    for chunk in range(chunks):
-        lanes = pl.ds(chunk * step, step)
-        waits.append(
-            [
-                copies.start(piece.at[:, lanes], weights.at[pl.ds(row, piece.shape[0]), lanes])
-                for row, piece in zip(rows, pieces)
-            ]
-        )
-    waits[0] += first
-    return waits
-
-
-def near_kernel(chunks, *refs):
-    lefts, pieces = refs[:2], refs[2:4]
-    out, left, weights, semaphores = refs[4:]
+    stores = []
+    for piece in range(pieces):
+        ins[piece].wait()
+        stores.append(copies.start(held.at[pl.ds(piece * size, size)], outs[piece]))
+    for copy in stores:
+        copy.wait()
+
+
+def cut(table, at, weights, pieces):
+    depth, width = weights.shape
+    size = depth // 2 // pieces
+    return call(
+        functools.partial(cut_kernel, pieces, at),
+        "cut_weights",
+        4,
+        [SMEM, HBM],
+        [((size, width), weights.dtype, HBM)] * pieces,
+        [
+            pltpu.VMEM((depth // 2, width), weights.dtype),
+            pltpu.SemaphoreType.DMA((2 * pieces,)),
+        ],
+        table,
+        weights,
+    )
+
+
+def near_kernel(chunks, left_hbm, weights_hbm, out, left, weights, semaphores):
     copies = Copies(semaphores)
-    rows = [0, pieces[0].shape[0]]
-    waits = fetch(copies, lefts, left, pieces, rows, weights, chunks)
     step = out.shape[1] // chunks
-    for chunk in range(chunks):
-        for copy in waits[chunk]:
-            copy.wait()
-        lanes = pl.ds(chunk * step, step)
-        out[:, lanes] = jnp.dot(
-            left[...], weights[:, lanes], preferred_element_type=jnp.float32
-        ).astype(jnp.bfloat16)
-
-
-def output_near(lefts, pieces, chunks=6):
-    (rows, columns), (depth, width) = lefts[0].shape, pieces[0].shape
-    bf16 = jnp.bfloat16
+    first = copies.start(left_hbm, left)
+    lanes = [pl.ds(chunk * step, step) for chunk in range(chunks)]
+    waits = [copies.start(weights_hbm.at[:, at], weights.at[:, at]) for at in lanes]
+    first.wait()
+    for at, copy in zip(lanes, waits):
+        copy.wait()
+        out[:, at] = jnp.dot(left[...], weights[:, at], preferred_element_type=jnp.float32)
+
+
+def output_near(left, weights, chunks=6):
+    (rows, columns), width = left.shape, weights.shape[1]
     return call(
         functools.partial(near_kernel, chunks),
         "output_near",
+        12,
+        [HBM] * 2,
+        [((rows, width), jnp.float32, VMEM)],
+        [
+            pltpu.VMEM(left.shape, left.dtype),
+            pltpu.VMEM(weights.shape, weights.dtype),
+            pltpu.SemaphoreType.DMA((1 + chunks,)),
+        ],
+        left,
+        weights,
+    )[0]
+
+
+def send_kernel(at, chunks, table, left_hbm, near, *refs):
+    count = len(refs) - 5
+    pieces, (out, weights, left, staged, semaphores) = refs[:count], refs[count:]
+    copies = Copies(semaphores)
+    depth, width = weights.shape
+    size = pieces[0].shape[0]
+    step = width // chunks
+    first = copies.start(left_hbm, left)
+    lanes = [pl.ds(chunk * step, step) for chunk in range(chunks)]
+    waits = []
+    for span in lanes:
+        here = []
+        for index, piece in enumerate(pieces):
+            half = table[at] if index < count // 2 else 1 - table[at]
+            row = half * (depth // 2) + index % (count // 2) * size
+            target = weights.at[pl.ds(pl.multiple_of(row, size), size), span]
+            here.append(copies.start(piece.at[:, span], target))
+        waits.append(here)
+    first.wait()
+    half = left.shape[0] // 2
+    stores = []
+    for span, here in zip(lanes, waits):
+        for copy in here:
+            copy.wait()
+        staged[:, span] = (
+            near[half:, span]
+            + jnp.dot(left[half:, :], weights[:, span], preferred_element_type=jnp.float32)
+        ).astype(jnp.bfloat16)
+        stores.append(copies.start(staged.at[:, span], out.at[:, span]))
+    for copy in stores:
+        copy.wait()
+
+
+def output_send(table, at, left, near, pieces, chunks=6):
+    (rows, width), columns = near.shape, left.shape[1]
+    half, bf16 = (rows // 2, width), jnp.bfloat16
+    return call(
+        functools.partial(send_kernel, at, chunks),
+        "output_send",
         16,
-        [HBM] * 4,
-        [((rows, width), bf16, VMEM)],
-        [
-            pltpu.VMEM((rows, 2 * columns), bf16),
-            pltpu.VMEM((2 * depth, width), bf16),
-            pltpu.SemaphoreType.DMA((2 + 2 * chunks,)),
-        ],
-        *lefts,
+        [SMEM, HBM, VMEM] + [HBM] * len(pieces),
+        [(half, bf16, HBM), ((columns, width), bf16, VMEM)],
+        [
+            pltpu.VMEM(left.shape, bf16),
+            pltpu.VMEM(half, bf16),
+            pltpu.SemaphoreType.DMA((1 + (len(pieces) + 1) * chunks,)),
+        ],
+        table,
+        left,
+        near,
         *pieces,
+    )
+
+
+def keep_kernel(chunks, left_hbm, near, weights, out, left, semaphores):
+    Copies(semaphores).start(left_hbm, left).wait()
+    half, step = left.shape[0] // 2, out.shape[1] // chunks
+    for chunk in range(chunks):
+        span = pl.ds(chunk * step, step)
+        out[:, span] = near[:half, span] + jnp.dot(
+            left[:half, :], weights[:, span], preferred_element_type=jnp.float32
+        )
+
+
+def output_keep(left, near, weights, chunks=6):
+    rows, width = near.shape
+    return call(
+        functools.partial(keep_kernel, chunks),
+        "output_keep",
+        4,
+        [HBM, VMEM, VMEM],
+        [((rows // 2, width), jnp.float32, VMEM)],
+        [pltpu.VMEM(left.shape, jnp.bfloat16), pltpu.SemaphoreType.DMA((1,))],
+        left,
+        near,
+        weights,
     )[0]
 
 
-def output_kernel(count, at, chunks, table, *refs):
-    lefts, pieces = refs[:2], refs[2 : 2 + count]
-    hidden, near, gain, out, left, weights, held, projected, semaphores = refs[2 + count :]
+def final_kernel(chunks, received, hidden, kept, gain, out, other, held, semaphores):
     copies = Copies(semaphores)
-    depth = left.shape[1] // 2
-    size = pieces[0].shape[0]
-    each = depth // size
-    rows = [
-        pl.multiple_of(index // each * depth + table[at + index % each] * size, size)
-        for index in range(count)
-    ]
-    waits = fetch(copies, lefts, left, pieces, rows, weights, chunks)
     width = hidden.shape[1]
     step = width // chunks
+    lanes = [pl.ds(chunk * step, step) for chunk in range(chunks)]
+    waits = [copies.start(received.at[:, span], other.at[:, span]) for span in lanes]
     late = copies.start(hidden, held)
     square = jnp.zeros((hidden.shape[0], 128), jnp.float32)
-    for chunk in range(chunks):
-        for copy in waits[chunk]:
-            copy.wait()
-        lanes = pl.ds(chunk * step, step)
-        total = near[:, lanes].astype(jnp.float32) + jnp.dot(
-            left[...], weights[:, lanes], preferred_element_type=jnp.float32
-        )
-        projected[:, lanes] = total
+    for span, copy in zip(lanes, waits):
+        copy.wait()
+        total = kept[:, span] + other[:, span].astype(jnp.float32)
         for lane in range(0, step, 128):
             part = total[:, lane : lane + 128]
             square = square + part * part
     mean = jnp.sum(square, axis=1, keepdims=True) / width
     scale = lax.rsqrt(mean + EPS)
     late.wait()
+    gains = gain[...].reshape(1, width)
     stores = []
-    for chunk in range(chunks):
-        lanes = pl.ds(chunk * step, step)
-        normed = projected[:, lanes] * scale * gain[:, lanes]
-        held[:, lanes] = (held[:, lanes].astype(jnp.float32) + normed).astype(jnp.bfloat16)
-        stores.append(copies.start(held.at[:, lanes], out.at[:, lanes]))
+    for chunk, span in enumerate(lanes):
+        total = kept[:, span] + other[:, span].astype(jnp.float32)
+        normed = total * scale * gains[:, chunk * step : (chunk + 1) * step]
+        held[:, span] = (held[:, span].astype(jnp.float32) + normed).astype(jnp.bfloat16)
+        stores.append(copies.start(held.at[:, span], out.at[:, span]))
     for store in stores:
         store.wait()
 
 
-def output(table, at, lefts, pieces, near, hidden, gain, chunks=6):
+def output(received, kept, hidden, gain, chunks=6):
     rows, width = hidden.shape
-    columns = lefts[0].shape[1]
     bf16 = jnp.bfloat16
     return call(
-        functools.partial(output_kernel, len(pieces), at, chunks),
+        functools.partial(final_kernel, chunks),
         "output_norm",
-        24,
-        [SMEM] + [HBM] * (2 + len(pieces) + 1) + [VMEM] * 2,
+        12,
+        [HBM, HBM, VMEM, VMEM],
         [((rows, width), bf16, HBM)],
         [
-            pltpu.VMEM((rows, 2 * columns), bf16),
-            pltpu.VMEM((2 * columns, width), bf16),
             pltpu.VMEM((rows, width), bf16),
-            pltpu.VMEM((rows, width), jnp.float32),
-            pltpu.SemaphoreType.DMA((3 + (len(pieces) + 1) * chunks,)),
-        ],
-        table,
-        *lefts,
-        *pieces,
+            pltpu.VMEM((rows, width), bf16),
+            pltpu.SemaphoreType.DMA((1 + 2 * chunks,)),
+        ],
+        received,
         hidden,
-        near,
+        kept,
         gain,
     )[0]
 
@@ -535,19 +600,12 @@
     line = (seq - jnp.arange(lines, dtype=jnp.int32)) % lines
     near_starts = lookup(block_of, 2 * line + chip) * block_rows
     far_starts = lookup(block_of, 2 * line + 1 - chip) * block_rows
-    mine, beside = seq % 2, 1 - seq % 2
-    quarters = [(group, mine), (1 - group, mine), (group, beside), (1 - group, beside)]
-    quarters = [2 * a + b for a, b in quarters]
-    scalars = jnp.stack([core, *quarters]).astype(jnp.int32)
-    table = jnp.concatenate([scalars, near_starts, far_starts])
-    quarter_at, near_at, far_at = 1, 5, 5 + lines
-
-    share = w_out.shape[0] // 4
-    own_head, own_tail, w_quarter = norm(table, hidden, pre_gain, w_out, cuts, share)
-    w_quarter = flipped(w_quarter, "tp", 2)
-    head, tail = flipped(after(own_head, w_quarter), "tp", 2), flipped(own_tail, "tp", 2)
+    table = jnp.concatenate([jnp.stack([core, group]).astype(jnp.int32), near_starts, far_starts])
+    group_at, near_at, far_at = 1, 2, 2 + lines
+
+    own_head, own_tail = norm(hidden, pre_gain, cuts)
+    head, tail = flipped(own_head, "tp", 2), flipped(own_tail, "tp", 2)
     partner_head, partner_tail = flipped(own_head, "tp", 1), flipped(own_tail, "tp", 1)
-    w_partner = flipped(w_out, "tp", 1)
     weights = hold(wq, wk, wv)
 
     run = [jnp.arange(size, dtype=jnp.int32) for size in cuts]
@@ -566,22 +624,15 @@
             (own_head, 0, cuts[0]),
             (Came(partner_head), 0, cuts[0]),
             (own_tail, 0, cuts[1]),
-            (Came(after(partner_tail, w_partner)), 0, cuts[1]),
+            (Came(partner_tail), 0, cuts[1]),
         ],
         weights,
         trig,
         0,
     )
     near = along_line(kv_near)
-    swap = lambda array: flipped(array, "groups", 1)
-    w_other = swap(w_quarter)
-    w_beside = lax.ppermute(
-        after(w_quarter, *came(near)), "seq", [(i, i ^ 1) for i in range(lines)]
-    )
-    w_last = swap(w_beside)
-    cross_early = [flipped(piece, "tp", 1) for piece in (w_quarter, w_other)]
-    cross_beside = flipped(w_beside, "tp", 1)
-    q_near = after(q_near, w_other)
+    w_cut = cut(table, group_at, after(w_out, kv_near), 4)
+    q_near = after(q_near, *w_cut)
     (near_state,) = attention(
         [Step(0, 0, others, same=0)], table, [q_near], [near_chunk], [near], [near_chunk], [None]
     )
@@ -600,7 +651,6 @@
         block_rows,
     )
     far_head = along_line(kv_head)
-    q_head = after(q_head, w_beside)
     (head_state,) = attention(
         [Step(0, 1, [], same=0), Step(0, 0, everyone)],
         table,
@@ -619,7 +669,12 @@
         block_rows + 2 * cuts[0],
     )
     far_tail = along_line(kv_tail)
-    q_tail = after(q_tail, cross_beside, *cross_early)
+
+    w_far = [flipped(after(w_cut[0], head), "tp", 2), flipped(after(w_cut[1], tail), "tp", 2)]
+    swap = lambda array: flipped(array, "groups", 1)
+    w_far[0] = after(w_far[0], kv_tail)
+    w_far.append(flipped(after(w_cut[2], w_far[0]), "tp", 2))
+    w_other = [swap(w_far[0])]
     qs, q_chunks = [q_near, q_head, q_tail], [near_chunk, head_chunk, tail_chunk]
     state = attention(
         [
@@ -636,10 +691,14 @@
         [near_chunk, head_chunk, tail_chunk],
         [near_state, head_state, None],
     )
+    w_far[1] = after(w_far[1], *state[0], *came(far_tail))
+    w_far.append(flipped(after(w_cut[3], w_far[1]), "tp", 2))
+    w_other.append(swap(w_far[1]))
+    state[0] = tuple(after(array, w_other[0]) for array in state[0])
     first = 2 * cuts[0]
     to = lambda half: [(0, half * cuts[0], cuts[0]), (0, first + half * cuts[1], cuts[1])]
     over = lambda half: [(1, half * cuts[0], cuts[0]), (2, half * cuts[1], cuts[1])]
-    mine, partners, same, cross = attention(
+    attended, away = attention(
         [
             Step(1, 0, others, same=0, merged=True),
             Step(2, 0, others, merged=True),
@@ -651,22 +710,16 @@
         [far_tail],
         [tail_chunk],
         state,
-        final=[to(0), to(1), over(0), over(1)],
-    )
-    cross, same = flipped(cross, "tp", 3), flipped(same, "tp", 2)
-    near_sum = output_near([mine, Came(flipped(partners, "tp", 1))], [w_out, Came(w_partner)])
-    w_last = after(w_last, mine)
-    quarters = [w_quarter, w_other, w_beside, w_last]
-    quarters += [*cross_early, cross_beside, flipped(w_last, "tp", 1)]
-    return output(
-        table,
-        quarter_at,
-        [Came(same), Came(cross)],
-        [Came(piece) for piece in quarters],
-        near_sum,
-        hidden,
-        post_gain.reshape(1, -1),
-    )
+        final=[to(0) + to(1), over(0) + over(1)],
+    )
+    away = flipped(away, "tp", 2)
+    near_sum = output_near(after(attended, w_other[1]), w_out)
+    w_other += [swap(after(w_far[2], attended)), swap(after(w_far[3], near_sum))]
+    pieces = [Came(piece) for piece in w_far + w_other]
+    sent, w_laid = output_send(table, group_at, Came(away), near_sum, pieces)
+    received = flipped(sent, "tp", 1)
+    kept = output_keep(Came(away), near_sum, w_laid)
+    return output(Came(received), kept, hidden, post_gain)
 
 
 def any_count(hidden, pre_gain, post_gain, wq, wk, wv, w_out, block_of):
@@ -677,7 +730,7 @@
     block_rows = rows * lax.axis_size("tp") // 2
     starts = lookup(block_of, block) * block_rows
     table = jnp.concatenate([jnp.zeros(2, jnp.int32), starts])
-    normed = norm(table, hidden, pre_gain, w_out, [rows], 16, 1)[0]
+    normed = norm(hidden, pre_gain, [rows], 1)[0]
     normed = lax.all_gather(normed, "tp", axis=0, tiled=True)
     place = jnp.arange(block_rows, dtype=jnp.int32)
     trig = rotary_table((starts[:2, None] + place).reshape(-1))

time: 122 us -> 116 us (0.951); the launches traced: 120 us -> 117 us
  Pallas kernels: 43.9 us -> 53.6 us
  waiting for transfers between devices: 37.7 us -> 29.6 us
  starting transfers between devices: 33.3 us -> 29 us
    pallas_call x11 -> x14, Pallas kernels: 43.9 us -> 53.6 us  [call(): pl.pallas_call(kernel, in_specs=in_specs, out_specs=[spec for _, _, spec...]
    ppermute x1 -> x0, waiting for transfers between devices: 8.14 us -> none  [two_chips(): lax.ppermute(after(w_quarter, *came(near)), 'seq', [(i, i ^ 1) for i in r...]
    ppermute x1 -> x0, starting transfers between devices: 6.73 us -> none  [two_chips(): lax.ppermute(after(w_quarter, *came(near)), 'seq', [(i, i ^ 1) for i in r...]
    ppermute x9, waiting for transfers between devices: 11.4 us -> 13.3 us  [along_line(): lax.ppermute(array, 'seq', [(i, (i + by) % size) for i in range(size)])]
    ppermute x19 -> x18, waiting for transfers between devices: 18.1 us -> 16.3 us  [flipped(): return lax.ppermute(array, axis, [(i, i ^ bit) for i in range(size)])]
    ppermute x9, starting transfers between devices: 15.2 us -> 16.7 us  [along_line(): lax.ppermute(array, 'seq', [(i, (i + by) % size) for i in range(size)])]
    ppermute x19 -> x18, starting transfers between devices: 11.4 us -> 12.3 us  [flipped(): return lax.ppermute(array, axis, [(i, i ^ bit) for i in range(size)])]
  transfers between devices with their start and end apart: 29 -> 27, of which waited for: 9 -> 9; matrix products, arithmetic and copies ran while one was open for 4% -> 3% of each run, Pallas kernels for 32% -> 37%
where the time goes in v6:
time: 116 us; the launch traced here: 117 us
  Pallas kernels  53.6 us (46%)
  waiting for transfers between devices  29.6 us (26%)
  starting transfers between devices  29 us (25%)
  other arithmetic  3.22 us (3%)
    pallas_call x14, Pallas kernels, call(): pl.pallas_call(kernel, in_specs=in_specs, out_specs=[spec for _, _, spec...  53.6 us
    ppermute x9, starting transfers between devices, along_line(): lax.ppermute(array, 'seq', [(i, (i + by) % size) for i in range(size)])  16.7 us
    ppermute x18, waiting for transfers between devices, flipped(): return lax.ppermute(array, axis, [(i, i ^ bit) for i in range(size)])  16.3 us
    ppermute x9, waiting for transfers between devices, along_line(): lax.ppermute(array, 'seq', [(i, (i + by) % size) for i in range(size)])  13.3 us
    ppermute x18, starting transfers between devices, flipped(): return lax.ppermute(array, axis, [(i, i ^ bit) for i in range(size)])  12.3 us
  transfers between devices with their start and end apart: 27, of which 9 were waited for; matrix products, arithmetic and copies ran while one was open for 3% of the time, Pallas kernels for 37%

profile of v6, /device:TPU:0, one launch (start us, length us, event | category | flops | bytes accessed | tf_op | source)
XLA Modules:
  0.0 116.7 jit_solution(17277182944240029742)
XLA Ops:
  0.7 2.9 %norm_rows.1 = (bf16[128,4608]{1,0:T(8,128)(2,1)}, bf16[64,4608]{1,0:T(8,128)(2,1)}) custom-call(bf16[192,4608]{1,0:T(8,128)(2,1)} %hidden.3, f32[4608]{0:T(1024)S(1)} %copy-done.2), custom_call_target="tpu_custom_call" | custom-call | flops 1 | bytes 1 | tf_op jit(solution)/shard_map/norm_rows/pallas_call | solution.py:37
  4.2 2.6 %collective-permute-start.2 = (bf16[128,4608]{1,0:T(8,128)(2,1)}, bf16[128,4608]{1,0:T(8,128)(2,1)S(1)}, u32[]{:S(2)}, u32[]{:S(2)}) collective-permute-start(bf16[128,4608]{1,0:T(8,128)(2,1)} %get-tuple-element.46.refs_0_), channel_id=1, source_target_pairs={{0,8},{4,12},{8,0},{12,4},{1,9},{5,13},{9,1},{13,5},{2,10},{6,14},... | collective-permute-start | bytes 3538952 | tf_op jit(solution)/shard_map/ppermute | solution.py:572
  7.2 2.4 %hold_weights.1.weights = bf16[4608,512]{1,0:T(8,128)(2,1)S(1)} custom-call(bf16[4608,256]{1,0:T(8,128)(2,1)} %wq.1, bf16[4608,128]{1,0:T(8,128)(2,1)} %wk.1, bf16[4608,128]{1,0:T(8,128)(2,1)} %wv.1), custom_call_target="tpu_custom_call" | custom-call | flops 1 | bytes 1 | tf_op jit(solution)/shard_map/hold_weights/pallas_call | solution.py:37
  9.7 1.5 %multiply_cosine_fusion = (f32[768,64]{1,0:T(8,128)S(1)}, f32[768,64]{1,0:T(8,128)S(1)}, f32[768,64]{1,0:T(8,128)S(1)}) fusion(f32[768]{0:T(1024)S(1)} %add_convert_fusion, f32[64]{0:T(128)S(1)} %multiply_power_fusion), kind=kLoop, calls=%fused_computation.2 | loop fusion | flops 98304 | bytes 593152 | tf_op jit(solution)/shard_map/cos | solution.py:561
  12.5 3.8 %qkv.3 = (bf16[2,384,128]{2,1,0:T(8,128)(2,1)S(1)}, bf16[384,256]{1,0:T(8,128)(2,1)S(1)}) custom-call(bf16[4608,512]{1,0:T(8,128)(2,1)S(1)} %hold_weights.1.weights, f32[768,256]{1,0:T(8,128)} %pad_maximum_fusion.trig, bf16[128,4608]{1,0:T(8,128)(2,1)} %get-tuple-element.46.refs_0_, bf16[128,4608]{1,0:T(8,128)(2,1)S(1)} %collective-permute-done.refs_1_, ...), custom_call_target="tpu_custom_call" | custom-call | flops 1 | bytes 1 | tf_op jit(solution)/shard_map/qkv/pallas_call | solution.py:37
  16.3 1.6 %collective-permute-start.3 = (bf16[384,256]{1,0:T(8,128)(2,1)S(1)}, bf16[384,256]{1,0:T(8,128)(2,1)S(1)}, u32[]{:S(2)}, u32[]{:S(2)}) collective-permute-start(bf16[384,256]{1,0:T(8,128)(2,1)S(1)} %get-tuple-element.49), channel_id=1, source_target_pairs={{0,1},{1,2},{2,3},{3,0},{4,5},{5,6},{6,7},{7,4},{8,9},{9,10},{10,1... | collective-permute-start | bytes 589832 | tf_op jit(solution)/shard_map/ppermute | solution.py:579
  17.9 2.6 %collective-permute-start.4 = (bf16[384,256]{1,0:T(8,128)(2,1)S(1)}, bf16[384,256]{1,0:T(8,128)(2,1)S(1)}, u32[]{:S(2)}, u32[]{:S(2)}) collective-permute-start(bf16[384,256]{1,0:T(8,128)(2,1)S(1)} %get-tuple-element.49), channel_id=1, source_target_pairs={{0,2},{1,3},{2,0},{3,1},{4,6},{5,7},{6,4},{7,5},{8,10},{9,11},{10,... | collective-permute-start | bytes 589832 | tf_op jit(solution)/shard_map/ppermute | solution.py:579
  20.5 1.3 %collective-permute-start.5 = (bf16[384,256]{1,0:T(8,128)(2,1)S(1)}, bf16[384,256]{1,0:T(8,128)(2,1)S(1)}, u32[]{:S(2)}, u32[]{:S(2)}) collective-permute-start(bf16[384,256]{1,0:T(8,128)(2,1)S(1)} %get-tuple-element.49), channel_id=1, source_target_pairs={{0,3},{1,0},{2,1},{3,2},{4,7},{5,4},{6,5},{7,6},{8,11},{9,8},{10,9... | collective-permute-start | bytes 589832 | tf_op jit(solution)/shard_map/ppermute | solution.py:579
  22.5 2.9 %cut_weights.1 = (bf16[32,4608]{1,0:T(8,128)(2,1)}, bf16[32,4608]{1,0:T(8,128)(2,1)}, bf16[32,4608]{1,0:T(8,128)(2,1)}, bf16[32,4608]{1,0:T(8,128)(2,1)}) custom-call(s32[10]{0:T(128)S(1)} %pad_add_fusion.1.table, bf16[256,4608]{1,0:T(8,128)(2,1)} %weights_hbm.1), custom_call_target="tpu_custom_call" | custom-call | flops 1 | bytes 1 | tf_op jit(solution)/shard_map/cut_weights/pallas_call | solution.py:37
  26.0 7.9 %collective-permute-done.4 = bf16[384,256]{1,0:T(8,128)(2,1)S(1)} collective-permute-done((bf16[384,256]{1,0:T(8,128)(2,1)S(1)}, bf16[384,256]{1,0:T(8,128)(2,1)S(1)}, u32[]{:S(2)}, u32[]{:S(2)}) %collective-permute-start.4) | collective-permute-done | bytes 196640 | tf_op jit(solution)/shard_map/ppermute | solution.py:579
  33.9 5.5 %attention.4 = (f32[768,128]{1,0:T(8,128)S(1)}, f32[768,256]{1,0:T(8,128)S(1)}) custom-call(s32[10]{0:T(128)S(1)} %pad_add_fusion.1.table, bf16[2,384,128]{2,1,0:T(8,128)(2,1)S(1)} %get-tuple-element.55.refs_0_, bf16[1,384,256]{2,1,0:T(8,128)(2,1)S(1)} %bitcast.18, bf16[1,384,256]{2,1,0:T(8,128)(2,1)S(1)} %bitcast.21, bf16[1,384,256]{2,1,0:T(8,128)(2,1)S(1)} %bitcast.24, ...), custom_call_target="tpu_custom_call" | custom-call | flops 1 | bytes 1 | tf_op jit(solution)/shard_map/attention/pallas_call | solution.py:37
  40.3 2.1 %collective-permute-done.8.refs_3_ = bf16[32,4608]{1,0:T(8,128)(2,1)S(1)} collective-permute-done((bf16[32,4608]{1,0:T(8,128)(2,1)S(1)}, bf16[32,4608]{1,0:T(8,128)(2,1)S(1)}, u32[]{:S(2)}, u32[]{:S(2)}) %collective-permute-start.8) | collective-permute-done | bytes 294944 | tf_op jit(solution)/shard_map/ppermute | solution.py:572
  42.5 3.3 %qkv.4 = (bf16[2,256,128]{2,1,0:T(8,128)(2,1)S(1)}, bf16[256,256]{1,0:T(8,128)(2,1)S(1)}) custom-call(bf16[4608,512]{1,0:T(8,128)(2,1)S(1)} %copy-done.1, f32[768,256]{1,0:T(8,128)} %pad_maximum_fusion.trig, bf16[128,4608]{1,0:T(8,128)(2,1)S(1)} %collective-permute-done.2.refs_0_, bf16[48,4608]{1,0:T(8,128)(2,1)S(1)} %collective-permute-done.6.refs_1_, ...), custom_call_target="tpu_custom_call" | custom-call | flops 1 | bytes 1 | tf_op jit(solution)/shard_map/qkv/pallas_call | solution.py:37
  45.8 1.8 %collective-permute-start.10 = (bf16[256,256]{1,0:T(8,128)(2,1)S(1)}, bf16[256,256]{1,0:T(8,128)(2,1)S(1)}, u32[]{:S(2)}, u32[]{:S(2)}) collective-permute-start(bf16[256,256]{1,0:T(8,128)(2,1)S(1)} %get-tuple-element.60), channel_id=1, source_target_pairs={{0,1},{1,2},{2,3},{3,0},{4,5},{5,6},{6,7},{7,4},{8,9},{9,10},{10,1... | collective-permute-start | bytes 393224 | tf_op jit(solution)/shard_map/ppermute | solution.py:579
  47.5 3.6 %collective-permute-start.11 = (bf16[256,256]{1,0:T(8,128)(2,1)S(1)}, bf16[256,256]{1,0:T(8,128)(2,1)S(1)}, u32[]{:S(2)}, u32[]{:S(2)}) collective-permute-start(bf16[256,256]{1,0:T(8,128)(2,1)S(1)} %get-tuple-element.60), channel_id=1, source_target_pairs={{0,2},{1,3},{2,0},{3,1},{4,6},{5,7},{6,4},{7,5},{8,10},{9,11},{10,... | collective-permute-start | bytes 393224 | tf_op jit(solution)/shard_map/ppermute | solution.py:579
  51.1 4.2 %attention.5 = (f32[512,128]{1,0:T(8,128)S(1)}, f32[512,256]{1,0:T(8,128)S(1)}) custom-call(s32[10]{0:T(128)S(1)} %pad_add_fusion.1.table, bf16[2,256,128]{2,1,0:T(8,128)(2,1)S(1)} %get-tuple-element.59.refs_0_.refs_1_, bf16[1,384,256]{2,1,0:T(8,128)(2,1)S(1)} %bitcast.19, bf16[1,384,256]{2,1,0:T(8,128)(2,1)S(1)} %bitcast.22, ...), custom_call_target="tpu_custom_call" | custom-call | flops 1 | bytes 1 | tf_op jit(solution)/shard_map/attention/pallas_call | solution.py:37
  55.4 4.7 %collective-permute-done.11 = bf16[256,256]{1,0:T(8,128)(2,1)S(1)} collective-permute-done((bf16[256,256]{1,0:T(8,128)(2,1)S(1)}, bf16[256,256]{1,0:T(8,128)(2,1)S(1)}, u32[]{:S(2)}, u32[]{:S(2)}) %collective-permute-start.11) | collective-permute-done | bytes 131104 | tf_op jit(solution)/shard_map/ppermute | solution.py:579
  60.1 2.0 %collective-permute-start.20 = (bf16[32,4608]{1,0:T(8,128)(2,1)S(1)}, bf16[32,4608]{1,0:T(8,128)(2,1)S(1)}, u32[]{:S(2)}, u32[]{:S(2)}) collective-permute-start(bf16[32,4608]{1,0:T(8,128)(2,1)S(1)} %copy-done.7), channel_id=1, source_target_pairs={{0,8},{4,12},{8,0},{12,4},{1,9},{5,13},{9,1},{13,5},{2,10},{6,14},... | collective-permute-start | bytes 884744 | tf_op jit(solution)/shard_map/ppermute | solution.py:572
  62.2 2.0 %qkv.5 = (bf16[2,128,128]{2,1,0:T(8,128)(2,1)S(1)}, bf16[128,256]{1,0:T(8,128)(2,1)S(1)}) custom-call(bf16[4608,512]{1,0:T(8,128)(2,1)S(1)} %copy-done.1, f32[768,256]{1,0:T(8,128)} %pad_maximum_fusion.trig, bf16[64,4608]{1,0:T(8,128)(2,1)S(1)} %collective-permute-done.9.refs_0_, bf16[64,4608]{1,0:T(8,128)(2,1)S(1)} %collective-permute-done.13.refs_1_), custom_call_target="tpu_custom_call" | custom-call | flops 1 | bytes 1 | tf_op jit(solution)/shard_map/qkv/pallas_call | solution.py:37
  64.2 3.3 %collective-permute-start.14 = (bf16[128,256]{1,0:T(8,128)(2,1)S(1)}, bf16[128,256]{1,0:T(8,128)(2,1)S(1)}, u32[]{:S(2)}, u32[]{:S(2)}) collective-permute-start(bf16[128,256]{1,0:T(8,128)(2,1)S(1)} %get-tuple-element.65), channel_id=1, source_target_pairs={{0,1},{1,2},{2,3},{3,0},{4,5},{5,6},{6,7},{7,4},{8,9},{9,10},{10,1... | collective-permute-start | bytes 196616 | tf_op jit(solution)/shard_map/ppermute | solution.py:579
  67.5 2.4 %collective-permute-start.16 = (bf16[128,256]{1,0:T(8,128)(2,1)S(1)}, bf16[128,256]{1,0:T(8,128)(2,1)S(1)}, u32[]{:S(2)}, u32[]{:S(2)}) collective-permute-start(bf16[128,256]{1,0:T(8,128)(2,1)S(1)} %get-tuple-element.65), channel_id=1, source_target_pairs={{0,3},{1,0},{2,1},{3,2},{4,7},{5,4},{6,5},{7,6},{8,11},{9,8},{10,9... | collective-permute-start | bytes 196616 | tf_op jit(solution)/shard_map/ppermute | solution.py:579
  70.0 1.5 %collective-permute-start.18 = (bf16[32,4608]{1,0:T(8,128)(2,1)S(1)}, bf16[32,4608]{1,0:T(8,128)(2,1)S(1)}, u32[]{:S(2)}, u32[]{:S(2)}) collective-permute-start(bf16[32,4608]{1,0:T(8,128)(2,1)S(1)} %collective-permute-done.17.refs_0_), channel_id=1, source_target_pairs={{0,16},{16,0},{1,17},{17,1},{2,18},{18,2},{3,19},{19,3},{4,20},{20... | collective-permute-start | bytes 884744 | tf_op jit(solution)/shard_map/ppermute | solution.py:572
  71.4 10.1 %attention.6 = (f32[768,128]{1,0:T(8,128)S(1)}, f32[768,256]{1,0:T(8,128)S(1)}, f32[512,128]{1,0:T(8,128)S(1)}, f32[512,256]{1,0:T(8,128)S(1)}, f32[256,128]{1,0:T(8,128)S(1)}, /*index=5*/f32[256,256]{1,0:T(8,128)S(1)}) custom-call(s32[10]{0:T(128)S(1)} %pad_add_fusion.1.table, ...), custom_call_target="tpu_custom_call", output_to_operand_aliasing={{0}: (13, {}), {1}: (14, {}), {2}: (15, {}), {3}: (16, {})} | custom-call | flops 1 | bytes 1 | tf_op jit(solution)/shard_map/attention/pallas_call | solution.py:37
  82.3 2.0 %collective-permute-start.23 = (bf16[32,4608]{1,0:T(8,128)(2,1)S(1)}, bf16[32,4608]{1,0:T(8,128)(2,1)S(1)}, u32[]{:S(2)}, u32[]{:S(2)}) collective-permute-start(bf16[32,4608]{1,0:T(8,128)(2,1)S(1)} %copy-done.5), channel_id=1, source_target_pairs={{0,8},{4,12},{8,0},{12,4},{1,9},{5,13},{9,1},{13,5},{2,10},{6,14},... | collective-permute-start | bytes 884744 | tf_op jit(solution)/shard_map/ppermute | solution.py:572
  84.3 4.3 %attention.7 = (bf16[384,256]{1,0:T(8,128)(2,1)}, bf16[384,256]{1,0:T(8,128)(2,1)}, f32[768,128]{1,0:T(8,128)S(1)}, f32[768,256]{1,0:T(8,128)S(1)}, f32[512,128]...) custom-call(s32[10]{0:T(128)S(1)} %pad_add_fusion.1.table, ...), custom_call_target="tpu_custom_call", output_to_operand_aliasing={{2}: (8, {}), {3}: (9, {}), {4}: (10, {}), {5}: (11, {}), {... | custom-call | flops 1 | bytes 1 | tf_op jit(solution)/shard_map/attention/pallas_call | solution.py:37
  88.5 3.0 %collective-permute-done.22.refs_2_ = bf16[32,4608]{1,0:T(8,128)(2,1)S(1)} collective-permute-done((bf16[32,4608]{1,0:T(8,128)(2,1)S(1)}, bf16[32,4608]{1,0:T(8,128)(2,1)S(1)}, u32[]{:S(2)}, u32[]{:S(2)}) %collective-permute-start.22) | collective-permute-done | bytes 294944 | tf_op jit(solution)/shard_map/ppermute | solution.py:572
  92.1 3.4 %output_near.1.near = f32[384,4608]{1,0:T(8,128)S(1)} custom-call(bf16[384,256]{1,0:T(8,128)(2,1)} %get-tuple-element.80.left_hbm, bf16[256,4608]{1,0:T(8,128)(2,1)} %weights_hbm.1), custom_call_target="tpu_custom_call" | custom-call | flops 1 | bytes 1 | tf_op jit(solution)/shard_map/output_near/pallas_call | solution.py:37
  97.0 5.7 %collective-permute-done.19.left_hbm = bf16[384,256]{1,0:T(8,128)(2,1)S(1)} collective-permute-done((bf16[384,256]{1,0:T(8,128)(2,1)S(1)}, bf16[384,256]{1,0:T(8,128)(2,1)S(1)}, u32[]{:S(2)}, u32[]{:S(2)}) %collective-permute-start.19) | collective-permute-done | bytes 196640 | tf_op jit(solution)/shard_map/ppermute | solution.py:572
  102.7 1.9 %collective-permute-done.25.refs_7_ = bf16[32,4608]{1,0:T(8,128)(2,1)S(1)} collective-permute-done((bf16[32,4608]{1,0:T(8,128)(2,1)S(1)}, bf16[32,4608]{1,0:T(8,128)(2,1)S(1)}, u32[]{:S(2)}, u32[]{:S(2)}) %collective-permute-start.25) | collective-permute-done | bytes 294944 | tf_op jit(solution)/shard_map/ppermute | solution.py:572
  104.6 4.7 %output_send.1 = (bf16[192,4608]{1,0:T(8,128)(2,1)}, bf16[256,4608]{1,0:T(8,128)(2,1)S(1)}) custom-call(s32[10]{0:T(128)S(1)} %pad_add_fusion.1.table, bf16[384,256]{1,0:T(8,128)(2,1)S(1)} %collective-permute-done.19.left_hbm, f32[384,4608]{1,0:T(8,128)S(1)} %output_near.1.near, bf16[32,4608]{1,0:T(8,128)(2,1)S(1)} %collective-permute-done.17.refs_0_, ...), custom_call_target="tpu_custom_call" | custom-call | flops 1 | bytes 1 | tf_op jit(solution)/shard_map/output_send/pallas_call | solution.py:37
  110.3 2.9 %collective-permute-done.26.received = bf16[192,4608]{1,0:T(8,128)(2,1)S(1)} collective-permute-done((bf16[192,4608]{1,0:T(8,128)(2,1)}, bf16[192,4608]{1,0:T(8,128)(2,1)S(1)}, u32[]{:S(2)}, u32[]{:S(2)}) %collective-permute-start.26) | collective-permute-done | bytes 1769504 | tf_op jit(solution)/shard_map/ppermute | solution.py:572
  113.3 3.3 %output_norm.1 = bf16[192,4608]{1,0:T(8,128)(2,1)} custom-call(bf16[192,4608]{1,0:T(8,128)(2,1)S(1)} %collective-permute-done.26.received, bf16[192,4608]{1,0:T(8,128)(2,1)} %hidden.3, f32[192,4608]{1,0:T(8,128)S(1)} %output_keep.1.kept, f32[4608]{0:T(1024)S(1)} %copy-done.3), custom_call_target="tpu_custom_call" | custom-call | flops 1 | bytes 1 | tf_op jit(solution)/shard_map/output_norm/pallas_call | solution.py:37
  (70 shorter events, 9.1 us)
Async XLA Ops:
  3.7 8.9 %collective-permute-start = (bf16[128,4608]{1,0:T(8,128)(2,1)}, bf16[128,4608]{1,0:T(8,128)(2,1)S(1)}, u32[]{:S(2)}, u32[]{:S(2)}) collective-permute-start(bf16[128,4608]{1,0:T(8,128)(2,1)} %get-tuple-element.46.refs_0_), channel_id=1, source_target_pairs={{0,4},{4,0},{8,12},{12,8},{1,5},{5,1},{9,13},{13,9},{2,6},{6,2},{1... | collective-permute-start | bytes 3538952 | tf_op jit(solution)/shard_map/ppermute | solution.py:572
  4.2 35.3 %collective-permute-start.2 = (bf16[128,4608]{1,0:T(8,128)(2,1)}, bf16[128,4608]{1,0:T(8,128)(2,1)S(1)}, u32[]{:S(2)}, u32[]{:S(2)}) collective-permute-start(bf16[128,4608]{1,0:T(8,128)(2,1)} %get-tuple-element.46.refs_0_), channel_id=1, source_target_pairs={{0,8},{4,12},{8,0},{12,4},{1,9},{5,13},{9,1},{13,5},{2,10},{6,14},... | collective-permute-start | bytes 3538952 | tf_op jit(solution)/shard_map/ppermute | solution.py:572
  6.8 5.8 %collective-permute-start.1 = (bf16[64,4608]{1,0:T(8,128)(2,1)}, bf16[64,4608]{1,0:T(8,128)(2,1)S(1)}, u32[]{:S(2)}, u32[]{:S(2)}) collective-permute-start(bf16[64,4608]{1,0:T(8,128)(2,1)} %get-tuple-element.47.refs_2_), channel_id=1, source_target_pairs={{0,4},{4,0},{8,12},{12,8},{1,5},{5,1},{9,13},{13,9},{2,6},{6,2},{1... | collective-permute-start | bytes 1769480 | tf_op jit(solution)/shard_map/ppermute | solution.py:572
  16.3 9.7 %collective-permute-start.3 = (bf16[384,256]{1,0:T(8,128)(2,1)S(1)}, bf16[384,256]{1,0:T(8,128)(2,1)S(1)}, u32[]{:S(2)}, u32[]{:S(2)}) collective-permute-start(bf16[384,256]{1,0:T(8,128)(2,1)S(1)} %get-tuple-element.49), channel_id=1, source_target_pairs={{0,1},{1,2},{2,3},{3,0},{4,5},{5,6},{6,7},{7,4},{8,9},{9,10},{10,1... | collective-permute-start | bytes 589832 | tf_op jit(solution)/shard_map/ppermute | solution.py:579
  17.9 16.0 %collective-permute-start.4 = (bf16[384,256]{1,0:T(8,128)(2,1)S(1)}, bf16[384,256]{1,0:T(8,128)(2,1)S(1)}, u32[]{:S(2)}, u32[]{:S(2)}) collective-permute-start(bf16[384,256]{1,0:T(8,128)(2,1)S(1)} %get-tuple-element.49), channel_id=1, source_target_pairs={{0,2},{1,3},{2,0},{3,1},{4,6},{5,7},{6,4},{7,5},{8,10},{9,11},{10,... | collective-permute-start | bytes 589832 | tf_op jit(solution)/shard_map/ppermute | solution.py:579
  20.5 13.4 %collective-permute-start.5 = (bf16[384,256]{1,0:T(8,128)(2,1)S(1)}, bf16[384,256]{1,0:T(8,128)(2,1)S(1)}, u32[]{:S(2)}, u32[]{:S(2)}) collective-permute-start(bf16[384,256]{1,0:T(8,128)(2,1)S(1)} %get-tuple-element.49), channel_id=1, source_target_pairs={{0,3},{1,0},{2,1},{3,2},{4,7},{5,4},{6,5},{7,6},{8,11},{9,8},{10,9... | collective-permute-start | bytes 589832 | tf_op jit(solution)/shard_map/ppermute | solution.py:579
  21.9 33.5 %collective-permute-start.9 = (bf16[64,4608]{1,0:T(8,128)(2,1)}, bf16[64,4608]{1,0:T(8,128)(2,1)S(1)}, u32[]{:S(2)}, u32[]{:S(2)}) collective-permute-start(bf16[64,4608]{1,0:T(8,128)(2,1)} %get-tuple-element.47.refs_2_), channel_id=1, source_target_pairs={{0,8},{4,12},{8,0},{12,4},{1,9},{5,13},{9,1},{13,5},{2,10},{6,14},... | collective-permute-start | bytes 1769480 | tf_op jit(solution)/shard_map/ppermute | solution.py:572
  22.5 20.0 %copy-start.1 = (bf16[4608,512]{1,0:T(8,128)(2,1)S(1)}, bf16[4608,512]{1,0:T(8,128)(2,1)}, u32[]{:S(2)}) copy-start(bf16[4608,512]{1,0:T(8,128)(2,1)} %copy-done) | copy-start | bytes 14155780
  39.6 2.9 %collective-permute-start.6 = (bf16[48,4608]{1,0:T(8,128)(2,1)S(1)}, bf16[48,4608]{1,0:T(8,128)(2,1)S(1)}, u32[]{:S(2)}, u32[]{:S(2)}) collective-permute-start(bf16[48,4608]{1,0:T(8,128)(2,1)S(1)} %get-tuple-element.90), channel_id=1, source_target_pairs={{0,4},{4,0},{8,12},{12,8},{1,5},{5,1},{9,13},{13,9},{2,6},{6,2},{1... | collective-permute-start | bytes 1327112 | tf_op jit(solution)/shard_map/ppermute | solution.py:572
  39.6 2.8 %collective-permute-start.7 = (bf16[48,4608]{1,0:T(8,128)(2,1)S(1)}, bf16[48,4608]{1,0:T(8,128)(2,1)S(1)}, u32[]{:S(2)}, u32[]{:S(2)}) collective-permute-start(bf16[48,4608]{1,0:T(8,128)(2,1)S(1)} %get-tuple-element.89), channel_id=1, source_target_pairs={{0,4},{4,0},{8,12},{12,8},{1,5},{5,1},{9,13},{13,9},{2,6},{6,2},{1... | collective-permute-start | bytes 1327112 | tf_op jit(solution)/shard_map/ppermute | solution.py:572
  40.2 19.9 %copy-start.8 = (bf16[32,4608]{1,0:T(8,128)(2,1)S(1)}, bf16[32,4608]{1,0:T(8,128)(2,1)}, u32[]{:S(2)}) copy-start(bf16[32,4608]{1,0:T(8,128)(2,1)} %get-tuple-element.67) | copy-start | bytes 884740
  40.2 20.0 %copy-start.7 = (bf16[32,4608]{1,0:T(8,128)(2,1)S(1)}, bf16[32,4608]{1,0:T(8,128)(2,1)}, u32[]{:S(2)}) copy-start(bf16[32,4608]{1,0:T(8,128)(2,1)} %get-tuple-element.78) | copy-start | bytes 884740
  40.2 2.3 %collective-permute-start.8 = (bf16[32,4608]{1,0:T(8,128)(2,1)S(1)}, bf16[32,4608]{1,0:T(8,128)(2,1)S(1)}, u32[]{:S(2)}, u32[]{:S(2)}) collective-permute-start(bf16[32,4608]{1,0:T(8,128)(2,1)S(1)} %slice.19), channel_id=1, source_target_pairs={{0,4},{4,0},{8,12},{12,8},{1,5},{5,1},{9,13},{13,9},{2,6},{6,2},{1... | collective-permute-start | bytes 884744 | tf_op jit(solution)/shard_map/ppermute | solution.py:572
  45.8 9.6 %collective-permute-start.10 = (bf16[256,256]{1,0:T(8,128)(2,1)S(1)}, bf16[256,256]{1,0:T(8,128)(2,1)S(1)}, u32[]{:S(2)}, u32[]{:S(2)}) collective-permute-start(bf16[256,256]{1,0:T(8,128)(2,1)S(1)} %get-tuple-element.60), channel_id=1, source_target_pairs={{0,1},{1,2},{2,3},{3,0},{4,5},{5,6},{6,7},{7,4},{8,9},{9,10},{10,1... | collective-permute-start | bytes 393224 | tf_op jit(solution)/shard_map/ppermute | solution.py:579
  47.5 12.5 %collective-permute-start.11 = (bf16[256,256]{1,0:T(8,128)(2,1)S(1)}, bf16[256,256]{1,0:T(8,128)(2,1)S(1)}, u32[]{:S(2)}, u32[]{:S(2)}) collective-permute-start(bf16[256,256]{1,0:T(8,128)(2,1)S(1)} %get-tuple-element.60), channel_id=1, source_target_pairs={{0,2},{1,3},{2,0},{3,1},{4,6},{5,7},{6,4},{7,5},{8,10},{9,11},{10,... | collective-permute-start | bytes 393224 | tf_op jit(solution)/shard_map/ppermute | solution.py:579
  51.1 8.9 %collective-permute-start.12 = (bf16[256,256]{1,0:T(8,128)(2,1)S(1)}, bf16[256,256]{1,0:T(8,128)(2,1)S(1)}, u32[]{:S(2)}, u32[]{:S(2)}) collective-permute-start(bf16[256,256]{1,0:T(8,128)(2,1)S(1)} %get-tuple-element.60), channel_id=1, source_target_pairs={{0,3},{1,0},{2,1},{3,2},{4,7},{5,4},{6,5},{7,6},{8,11},{9,8},{10,9... | collective-permute-start | bytes 393224 | tf_op jit(solution)/shard_map/ppermute | solution.py:579
  60.0 2.1 %collective-permute-start.13 = (bf16[64,4608]{1,0:T(8,128)(2,1)S(1)}, bf16[64,4608]{1,0:T(8,128)(2,1)S(1)}, u32[]{:S(2)}, u32[]{:S(2)}) collective-permute-start(bf16[64,4608]{1,0:T(8,128)(2,1)S(1)} %collective-permute-done.9.refs_0_), channel_id=1, source_target_pairs={{0,4},{4,0},{8,12},{12,8},{1,5},{5,1},{9,13},{13,9},{2,6},{6,2},{1... | collective-permute-start | bytes 1769480 | tf_op jit(solution)/shard_map/ppermute | solution.py:572
  60.1 9.9 %collective-permute-start.17 = (bf16[32,4608]{1,0:T(8,128)(2,1)S(1)}, bf16[32,4608]{1,0:T(8,128)(2,1)S(1)}, u32[]{:S(2)}, u32[]{:S(2)}) collective-permute-start(bf16[32,4608]{1,0:T(8,128)(2,1)S(1)} %copy-done.8), channel_id=1, source_target_pairs={{0,8},{4,12},{8,0},{12,4},{1,9},{5,13},{9,1},{13,5},{2,10},{6,14},... | collective-permute-start | bytes 884744 | tf_op jit(solution)/shard_map/ppermute | solution.py:572
  60.1 21.4 %collective-permute-start.20 = (bf16[32,4608]{1,0:T(8,128)(2,1)S(1)}, bf16[32,4608]{1,0:T(8,128)(2,1)S(1)}, u32[]{:S(2)}, u32[]{:S(2)}) collective-permute-start(bf16[32,4608]{1,0:T(8,128)(2,1)S(1)} %copy-done.7), channel_id=1, source_target_pairs={{0,8},{4,12},{8,0},{12,4},{1,9},{5,13},{9,1},{13,5},{2,10},{6,14},... | collective-permute-start | bytes 884744 | tf_op jit(solution)/shard_map/ppermute | solution.py:572
  64.2 17.4 %collective-permute-start.14 = (bf16[128,256]{1,0:T(8,128)(2,1)S(1)}, bf16[128,256]{1,0:T(8,128)(2,1)S(1)}, u32[]{:S(2)}, u32[]{:S(2)}) collective-permute-start(bf16[128,256]{1,0:T(8,128)(2,1)S(1)} %get-tuple-element.65), channel_id=1, source_target_pairs={{0,1},{1,2},{2,3},{3,0},{4,5},{5,6},{6,7},{7,4},{8,9},{9,10},{10,1... | collective-permute-start | bytes 196616 | tf_op jit(solution)/shard_map/ppermute | solution.py:579
  67.5 14.1 %collective-permute-start.15 = (bf16[128,256]{1,0:T(8,128)(2,1)S(1)}, bf16[128,256]{1,0:T(8,128)(2,1)S(1)}, u32[]{:S(2)}, u32[]{:S(2)}) collective-permute-start(bf16[128,256]{1,0:T(8,128)(2,1)S(1)} %get-tuple-element.65), channel_id=1, source_target_pairs={{0,2},{1,3},{2,0},{3,1},{4,6},{5,7},{6,4},{7,5},{8,10},{9,11},{10,... | collective-permute-start | bytes 196616 | tf_op jit(solution)/shard_map/ppermute | solution.py:579
  67.5 14.1 %collective-permute-start.16 = (bf16[128,256]{1,0:T(8,128)(2,1)S(1)}, bf16[128,256]{1,0:T(8,128)(2,1)S(1)}, u32[]{:S(2)}, u32[]{:S(2)}) collective-permute-start(bf16[128,256]{1,0:T(8,128)(2,1)S(1)} %get-tuple-element.65), channel_id=1, source_target_pairs={{0,3},{1,0},{2,1},{3,2},{4,7},{5,4},{6,5},{7,6},{8,11},{9,8},{10,9... | collective-permute-start | bytes 196616 | tf_op jit(solution)/shard_map/ppermute | solution.py:579
  70.0 14.3 %collective-permute-start.18 = (bf16[32,4608]{1,0:T(8,128)(2,1)S(1)}, bf16[32,4608]{1,0:T(8,128)(2,1)S(1)}, u32[]{:S(2)}, u32[]{:S(2)}) collective-permute-start(bf16[32,4608]{1,0:T(8,128)(2,1)S(1)} %collective-permute-done.17.refs_0_), channel_id=1, source_target_pairs={{0,16},{16,0},{1,17},{17,1},{2,18},{18,2},{3,19},{19,3},{4,20},{20... | collective-permute-start | bytes 884744 | tf_op jit(solution)/shard_map/ppermute | solution.py:572
  71.4 10.1 %copy-start.6 = (bf16[32,4608]{1,0:T(8,128)(2,1)S(1)}, bf16[32,4608]{1,0:T(8,128)(2,1)}, u32[]{:S(2)}) copy-start(bf16[32,4608]{1,0:T(8,128)(2,1)} %get-tuple-element.81) | copy-start | bytes 884740
  71.4 10.8 %copy-start.5 = (bf16[32,4608]{1,0:T(8,128)(2,1)S(1)}, bf16[32,4608]{1,0:T(8,128)(2,1)}, u32[]{:S(2)}) copy-start(bf16[32,4608]{1,0:T(8,128)(2,1)} %get-tuple-element.82) | copy-start | bytes 884740
  81.5 10.0 %collective-permute-start.22 = (bf16[32,4608]{1,0:T(8,128)(2,1)S(1)}, bf16[32,4608]{1,0:T(8,128)(2,1)S(1)}, u32[]{:S(2)}, u32[]{:S(2)}) collective-permute-start(bf16[32,4608]{1,0:T(8,128)(2,1)S(1)} %copy-done.6), channel_id=1, source_target_pairs={{0,8},{4,12},{8,0},{12,4},{1,9},{5,13},{9,1},{13,5},{2,10},{6,14},... | collective-permute-start | bytes 884744 | tf_op jit(solution)/shard_map/ppermute | solution.py:572
  81.7 10.4 %collective-permute-start.21 = (bf16[32,4608]{1,0:T(8,128)(2,1)S(1)}, bf16[32,4608]{1,0:T(8,128)(2,1)S(1)}, u32[]{:S(2)}, u32[]{:S(2)}) collective-permute-start(bf16[32,4608]{1,0:T(8,128)(2,1)S(1)} %collective-permute-done.20.refs_1_), channel_id=1, source_target_pairs={{0,16},{16,0},{1,17},{17,1},{2,18},{18,2},{3,19},{19,3},{4,20},{20... | collective-permute-start | bytes 884744 | tf_op jit(solution)/shard_map/ppermute | solution.py:572
  82.3 13.8 %collective-permute-start.23 = (bf16[32,4608]{1,0:T(8,128)(2,1)S(1)}, bf16[32,4608]{1,0:T(8,128)(2,1)S(1)}, u32[]{:S(2)}, u32[]{:S(2)}) collective-permute-start(bf16[32,4608]{1,0:T(8,128)(2,1)S(1)} %copy-done.5), channel_id=1, source_target_pairs={{0,8},{4,12},{8,0},{12,4},{1,9},{5,13},{9,1},{13,5},{2,10},{6,14},... | collective-permute-start | bytes 884744 | tf_op jit(solution)/shard_map/ppermute | solution.py:572
  91.6 11.1 %collective-permute-start.24 = (bf16[32,4608]{1,0:T(8,128)(2,1)S(1)}, bf16[32,4608]{1,0:T(8,128)(2,1)S(1)}, u32[]{:S(2)}, u32[]{:S(2)}) collective-permute-start(bf16[32,4608]{1,0:T(8,128)(2,1)S(1)} %collective-permute-done.22.refs_2_), channel_id=1, source_target_pairs={{0,16},{16,0},{1,17},{17,1},{2,18},{18,2},{3,19},{19,3},{4,20},{20... | collective-permute-start | bytes 884744 | tf_op jit(solution)/shard_map/ppermute | solution.py:572
  96.1 8.5 %collective-permute-start.25 = (bf16[32,4608]{1,0:T(8,128)(2,1)S(1)}, bf16[32,4608]{1,0:T(8,128)(2,1)S(1)}, u32[]{:S(2)}, u32[]{:S(2)}) collective-permute-start(bf16[32,4608]{1,0:T(8,128)(2,1)S(1)} %collective-permute-done.23.refs_3_), channel_id=1, source_target_pairs={{0,16},{16,0},{1,17},{17,1},{2,18},{18,2},{3,19},{19,3},{4,20},{20... | collective-permute-start | bytes 884744 | tf_op jit(solution)/shard_map/ppermute | solution.py:572
  97.0 5.7 %collective-permute-start.19 = (bf16[384,256]{1,0:T(8,128)(2,1)S(1)}, bf16[384,256]{1,0:T(8,128)(2,1)S(1)}, u32[]{:S(2)}, u32[]{:S(2)}) collective-permute-start(bf16[384,256]{1,0:T(8,128)(2,1)S(1)} %copy-done.9), channel_id=1, source_target_pairs={{0,8},{4,12},{8,0},{12,4},{1,9},{5,13},{9,1},{13,5},{2,10},{6,14},... | collective-permute-start | bytes 589832 | tf_op jit(solution)/shard_map/ppermute | solution.py:572
  109.3 4.0 %collective-permute-start.26 = (bf16[192,4608]{1,0:T(8,128)(2,1)}, bf16[192,4608]{1,0:T(8,128)(2,1)S(1)}, u32[]{:S(2)}, u32[]{:S(2)}) collective-permute-start(bf16[192,4608]{1,0:T(8,128)(2,1)} %get-tuple-element.85), channel_id=1, source_target_pairs={{0,4},{4,0},{8,12},{12,8},{1,5},{5,1},{9,13},{13,9},{2,6},{6,2},{1... | collective-permute-start | bytes 5308424 | tf_op jit(solution)/shard_map/ppermute | solution.py:572
  (5 other events, 23.0 us)
